TPU v7x, 32 devices: a whole 2x2x4 slice. The times are simulated.
32 devices in a mesh: groups: 2 (over y), row: 4 (over x, core), col: 4 (over z).
Axes of the slice: x: 2, y: 2, z: 4, core: 2. Of those that a mesh axis runs over, the one named last changes fastest.
Arguments:
- upper: bfloat16 [128, 8, 128, 128], P(('groups', 'row', 'col')), parts along dimension 0, as said below
- present: int32 [128, 8], P(('groups', 'row', 'col')), parts along dimension 0, may hold values from 0 to 1, as said below
Outputs:
- purified: bfloat16 [128, 8, 128, 128], P(('groups', 'row', 'col')), parts along dimension 0
There are 2 independent parts, one for each index of `groups`. A program takes and returns all parts, laid end to end along the dimension named above; each array names one. Nothing has to cross between parts.
Inputs may be any that keep to these rules, and one draw needn't show every extreme that they name: upper[i, 0] is a symmetric block for every i. present[i, 0] is 1 for every i.
All inputs are finite; a program needn't handle non-finite values.
Results may differ from a plain program's by a relative error of at most 0.024.
Values may be sent and summed in bfloat16 or wider, within the bound.
No kernel may reach another device: no remote copies, remote signals or barrier semaphores. Data moves between devices by JAX's collectives and lax.ppermute only.
A program may use at most 512 MiB of HBM per device.

v0:
```python
import jax
import jax.numpy as jnp
from jax import lax
from jax.sharding import PartitionSpec as P


def from_behind(block, axis, distance):
    devices = range(lax.axis_size(axis))
    route = [((i - distance) % len(devices), i) for i in devices]
    return lax.ppermute(block, axis, route)


def take_band(extended, first, count, offset):
    if offset >= 0:
        return (extended[first : first + count, offset], False)
    return (extended[first + offset : first + offset + count, -offset], True)


def band_product(left, left_first, right, right_first, count, width):
    results = []
    for offset in range(width + 1):
        left_pieces = []
        right_pieces = []
        for middle in range(offset - width, width + 1):
            first_blocks, first_flip = take_band(left, left_first, count, middle)
            second_blocks, second_flip = take_band(
                right, right_first + middle, count, offset - middle
            )
            if first_flip:
                first_blocks = jnp.swapaxes(first_blocks, 1, 2)
            if second_flip:
                second_blocks = jnp.swapaxes(second_blocks, 1, 2)
            left_pieces.append(first_blocks)
            right_pieces.append(second_blocks)
        left_wide = jnp.concatenate(left_pieces, axis=2)
        right_tall = jnp.concatenate(right_pieces, axis=1)
        results.append(
            jnp.einsum("nab,nbc->nac", left_wide, right_tall, preferred_element_type=jnp.float32)
        )
    return jnp.stack(results, axis=1)


def shift_plan(rows, depth):
    reach = -(-depth // rows)
    below_plan = []
    above_plan = []
    for step in range(reach, 0, -1):
        needed = min(rows, depth - (step - 1) * rows)
        below_plan.append((step, rows - needed, rows))
    for step in range(1, reach + 1):
        needed = min(rows, depth - (step - 1) * rows)
        above_plan.append((-step, 0, needed))
    return (reach, below_plan + above_plan)


def assemble(pieces, local, reach):
    return jnp.concatenate(pieces[:reach] + [local] + pieces[reach:], axis=0)


def per_device(upper, present):
    width = upper.shape[1] - 1
    rows = upper.shape[0]
    masked = upper * present.astype(jnp.bfloat16)[:, :, None, None]
    weights = present.astype(jnp.float32)[:, :, None, None]
    reach, plan = shift_plan(rows, width)
    received = [from_behind(masked[low:high], ("row", "col"), by) for by, low, high in plan]
    band = assemble(received, masked, reach)
    square_local = (band_product(band, width, band, width, rows, width) * weights).astype(
        jnp.bfloat16
    )
    neighbours = [from_behind(square_local[low:high], ("row", "col"), by) for by, low, high in plan]
    squares = assemble(neighbours, square_local, reach)
    cube = band_product(band, width, squares, width, rows, width) * weights
    square_mine = squares[width : width + rows].astype(jnp.float32)
    return (3.0 * square_mine - 2.0 * cube).astype(jnp.bfloat16)


def solution(mesh):
    return jax.shard_map(
        per_device,
        mesh=mesh,
        in_specs=(P(("groups", "row", "col"), None, None, None), P(("groups", "row", "col"), None)),
        out_specs=P(("groups", "row", "col"), None, None, None),
        check_vma=False,
    )
```

profile of v0, /device:TPU:25, one launch (start us, length us, event | category | flops | bytes accessed | tf_op | source)
XLA Modules:
  0.0 493.9 jit_solution(10566005627031994526)
XLA Ops:
  4.9 1.7 collective-permute-start
  7.3 91.7 %collective-permute-done = bf16[3,8,128,128]{2,3,0,1:T(8,128)(2,1)} collective-permute-done((bf16[3,8,128,128]{2,3,0,1:T(8,128)(2,1)}, bf16[3,8,128,128]{2,3,0,1:T(8,128)(2,1)}, u32[]{:S(2)}, u32[]{:S(2)}) %collective-permute-start) | collective-permute-done | bytes 786464 | tf_op jit(solution)/shard_map/ppermute | solution.py:10
  103.9 1.7 copy.5
  109.4 1.7 copy.16
  111.1 1.7 constant_dynamic-update-slice_fusion.45
  112.8 1.8 constant_dynamic-update-slice_fusion.72
  122.8 1.7 copy.29
  124.5 1.7 copy.30
  127.2 1.7 copy.31
  128.8 1.7 copy.32
  130.5 1.7 copy.33
  138.1 1.7 copy.44
  141.4 1.7 copy.45
  143.0 1.7 copy.46
  146.4 1.7 copy.9
  148.0 1.7 copy.50
  152.9 1.7 copy.52
  154.6 1.7 copy.10
  156.2 1.7 copy.11
  157.9 1.7 copy.64
  159.6 1.7 copy.12
  162.9 1.7 copy.137
  164.5 1.7 copy.54
  166.2 1.7 copy.55
  167.8 1.7 copy.48
  171.2 1.7 copy.141
  172.9 1.7 constant_dynamic-update-slice_fusion.30
  174.5 1.7 constant_dynamic-update-slice_fusion.29
  227.1 1.7 copy.143
  231.8 2.1 constant_dynamic-update-slice_fusion.174
  237.7 1.7 constant_dynamic-update-slice_fusion.180
  246.7 3.3 fusion.15
  250.8 2.2 fusion.14
  253.0 2.2 fusion.13
  257.8 2.0 fusion.5
  264.8 2.8 collective-permute-start.4
  267.5 1.7 collective-permute-start.6
  271.7 85.5 %collective-permute-done.4 = bf16[3,8,128,128]{2,3,0,1:T(8,128)(2,1)} collective-permute-done((bf16[3,8,128,128]{2,3,0,1:T(8,128)(2,1)}, bf16[3,8,128,128]{2,3,0,1:T(8,128)(2,1)}, u32[]{:S(2)}, u32[]{:S(2)}) %collective-permute-start.4) | collective-permute-done | bytes 786464 | tf_op jit(solution)/shard_map/ppermute | solution.py:10
  368.2 1.7 copy.151
  369.9 1.7 constant_dynamic-update-slice_fusion.230
  371.7 1.9 constant_dynamic-update-slice_fusion.275
  374.4 1.7 constant_dynamic-update-slice_fusion.252
  387.9 2.3 fusion.103
  391.8 1.7 copy.109
  393.5 1.7 copy.97
  396.7 1.7 copy.98
  398.4 1.7 copy.99
  400.1 1.7 copy.100
  406.6 1.7 copy.86
  408.3 1.7 copy.87
  409.9 1.7 copy.88
  411.6 1.7 copy.89
  430.0 1.7 copy.148
  436.4 1.7 copy.153
  438.1 1.7 copy.154
  439.7 1.7 copy.96
  445.2 2.3 fusion.11
  452.6 1.7 copy.156
  460.4 1.7 copy.114
  468.5 1.7 copy.115
  470.1 1.7 constant_dynamic-update-slice_fusion.276
  479.0 2.7 fusion.10
  481.7 2.7 fusion.9
  485.1 2.2 fusion.3
  (392 shorter events, 203.6 us)
Async XLA Ops:
  1.9 98.3 %collective-permute-start.1 = (bf16[4,8,128,128]{2,3,0,1:T(8,128)(2,1)S(1)}, bf16[4,8,128,128]{2,3,0,1:T(8,128)(2,1)S(1)}, u32[]{:S(2)}, u32[]{:S(2)}) collective-permute-start(bf16[4,8,128,128]{2,3,0,1:T(8,128)(2,1)S(1)} %broadcast_multiply_fusion), channel_id=1, source_target_pairs={{15,0},{0,1},{1,2},{2,3},{3,4},{4,5},{5,6},{6,7},{7,8},{8,9},{9,10... | collective-permute-start | bytes 3145736 | tf_op jit(solution)/shard_map/ppermute | solution.py:10
  4.9 94.2 %collective-permute-start = (bf16[3,8,128,128]{2,3,0,1:T(8,128)(2,1)}, bf16[3,8,128,128]{2,3,0,1:T(8,128)(2,1)}, u32[]{:S(2)}, u32[]{:S(2)}) collective-permute-start(bf16[3,8,128,128]{2,3,0,1:T(8,128)(2,1)} %get-tuple-element.154), channel_id=1, source_target_pairs={{14,0},{15,1},{0,2},{1,3},{2,4},{3,5},{4,6},{5,7},{6,8},{7,9},{8,1... | collective-permute-start | bytes 2359304 | tf_op jit(solution)/shard_map/ppermute | solution.py:10
  6.5 96.0 %collective-permute-start.2 = (bf16[4,8,128,128]{2,3,0,1:T(8,128)(2,1)S(1)}, bf16[4,8,128,128]{2,3,0,1:T(8,128)(2,1)S(1)}, u32[]{:S(2)}, u32[]{:S(2)}) collective-permute-start(bf16[4,8,128,128]{2,3,0,1:T(8,128)(2,1)S(1)} %broadcast_multiply_fusion), channel_id=1, source_target_pairs={{1,0},{2,1},{3,2},{4,3},{5,4},{6,5},{7,6},{8,7},{9,8},{10,9},{11,1... | collective-permute-start | bytes 3145736 | tf_op jit(solution)/shard_map/ppermute | solution.py:10
  6.7 215.1 %collective-permute-start.3 = (bf16[3,8,128,128]{2,3,0,1:T(8,128)(2,1)}, bf16[3,8,128,128]{2,3,0,1:T(8,128)(2,1)}, u32[]{:S(2)}, u32[]{:S(2)}) collective-permute-start(bf16[3,8,128,128]{2,3,0,1:T(8,128)(2,1)} %get-tuple-element.153), channel_id=1, source_target_pairs={{2,0},{3,1},{4,2},{5,3},{6,4},{7,5},{8,6},{9,7},{10,8},{11,9},{12,... | collective-permute-start | bytes 2359304 | tf_op jit(solution)/shard_map/ppermute | solution.py:10
  172.8 11.3 %copy-start.60 = (bf16[4,128,128]{2,1,0:T(8,128)(2,1)S(1)}, bf16[4,128,128]{2,1,0:T(8,128)(2,1)}, u32[]{:S(2)}) copy-start(bf16[4,128,128]{2,1,0:T(8,128)(2,1)} %copy.30) | copy-start | bytes 393220
  172.8 12.0 %copy-start.63 = (bf16[4,128,128]{2,1,0:T(8,128)(2,1)S(1)}, bf16[4,128,128]{2,1,0:T(8,128)(2,1)}, u32[]{:S(2)}) copy-start(bf16[4,128,128]{2,1,0:T(8,128)(2,1)} %copy.31) | copy-start | bytes 393220
  172.8 12.7 %copy-start.62 = (bf16[4,128,128]{2,1,0:T(8,128)(2,1)S(1)}, bf16[4,128,128]{2,1,0:T(8,128)(2,1)}, u32[]{:S(2)}) copy-start(bf16[4,128,128]{2,1,0:T(8,128)(2,1)} %copy.32) | copy-start | bytes 393220
  172.8 13.4 %copy-start.61 = (bf16[4,128,128]{2,1,0:T(8,128)(2,1)S(1)}, bf16[4,128,128]{2,1,0:T(8,128)(2,1)}, u32[]{:S(2)}) copy-start(bf16[4,128,128]{2,1,0:T(8,128)(2,1)} %copy.33) | copy-start | bytes 393220
  172.8 14.0 %copy-start.66 = (bf16[4,128,128]{2,1,0:T(8,128)(2,1)S(1)}, bf16[4,128,128]{2,1,0:T(8,128)(2,1)}, u32[]{:S(2)}) copy-start(bf16[4,128,128]{2,1,0:T(8,128)(2,1)} %copy.45) | copy-start | bytes 393220
  172.9 14.7 %copy-start.67 = (bf16[4,128,128]{2,1,0:T(8,128)(2,1)S(1)}, bf16[4,128,128]{2,1,0:T(8,128)(2,1)}, u32[]{:S(2)}) copy-start(bf16[4,128,128]{2,1,0:T(8,128)(2,1)} %copy.46) | copy-start | bytes 393220
  172.9 15.4 %copy-start.65 = (bf16[4,128,128]{2,1,0:T(8,128)(2,1)S(1)}, bf16[4,128,128]{2,1,0:T(8,128)(2,1)}, u32[]{:S(2)}) copy-start(bf16[4,128,128]{2,1,0:T(8,128)(2,1)} %copy.47) | copy-start | bytes 393220
  174.5 14.4 %copy-start.23 = (bf16[4,1408,128]{2,1,0:T(8,128)(2,1)S(1)}, bf16[4,1408,128]{2,1,0:T(8,128)(2,1)}, u32[]{:S(2)}) copy-start(bf16[4,1408,128]{2,1,0:T(8,128)(2,1)} %constant_dynamic-update-slice_fusion.131) | copy-start | bytes 4325380
  174.5 14.4 %copy-start.68 = (bf16[4,128,128]{2,1,0:T(8,128)(2,1)S(1)}, bf16[4,128,128]{2,1,0:T(8,128)(2,1)}, u32[]{:S(2)}) copy-start(bf16[4,128,128]{2,1,0:T(8,128)(2,1)} %copy.51) | copy-start | bytes 393220
  176.2 12.7 %copy-start.69 = (bf16[4,128,128]{2,1,0:T(8,128)(2,1)S(1)}, bf16[4,128,128]{2,1,0:T(8,128)(2,1)}, u32[]{:S(2)}) copy-start(bf16[4,128,128]{2,1,0:T(8,128)(2,1)} %copy.52) | copy-start | bytes 393220
  187.6 4.6 copy-start.45
  189.0 4.5 copy-start.48
  191.0 3.9 copy-start.77
  191.0 3.9 copy-start.78
  193.5 2.7 copy-start.47
  194.9 2.7 copy-start.46
  194.9 4.0 copy-start.55
  196.2 2.8 copy-start.33
  196.2 2.8 copy-start.54
  196.2 2.8 copy-start.53
  196.2 2.9 copy-start.52
  196.2 3.7 copy-start.34
  197.6 3.0 copy-start.51
  198.9 3.2 copy-start.13
  219.0 2.8 copy-start.31
  221.8 6.9 %copy-start.44 = (bf16[4,128,128]{1,2,0:T(8,128)(2,1)S(1)}, bf16[4,128,128]{1,2,0:T(8,128)(2,1)}, u32[]{:S(2)}) copy-start(bf16[4,128,128]{1,2,0:T(8,128)(2,1)} %get-tuple-element.62) | copy-start | bytes 393220
  223.1 2.3 copy-start.17
  223.1 8.7 %copy-start.2 = (bf16[4,128,1920]{2,1,0:T(8,128)(2,1)S(1)}, bf16[4,128,1920]{2,1,0:T(8,128)(2,1)}, u32[]{:S(2)}) copy-start(bf16[4,128,1920]{2,1,0:T(8,128)(2,1)} %get-tuple-element.212) | copy-start | bytes 5898244
  223.9 10.0 %copy-start.43 = (bf16[4,1,128,128]{3,2,0,1:T(8,128)(2,1)S(1)}, bf16[4,1,128,128]{3,2,0,1:T(8,128)(2,1)}, u32[]{:S(2)}) copy-start(bf16[4,1,128,128]{3,2,0,1:T(8,128)(2,1)} %copy.11) | copy-start | bytes 393220
  229.5 5.7 %copy-start.71 = (bf16[4,128,128]{2,1,0:T(8,128)(2,1)S(1)}, bf16[4,128,128]{2,1,0:T(8,128)(2,1)}, u32[]{:S(2)}) copy-start(bf16[4,128,128]{2,1,0:T(8,128)(2,1)} %copy.65) | copy-start | bytes 393220
  231.1 5.4 %copy-start.42 = (bf16[4,128,128]{1,2,0:T(8,128)(2,1)S(1)}, bf16[4,128,128]{1,2,0:T(8,128)(2,1)}, u32[]{:S(2)}) copy-start(bf16[4,128,128]{1,2,0:T(8,128)(2,1)} %get-tuple-element.58) | copy-start | bytes 393220
  235.1 10.3 %copy-start.14 = (bf16[4,128,1024]{2,1,0:T(8,128)(2,1)S(1)}, bf16[4,128,1024]{2,1,0:T(8,128)(2,1)}, u32[]{:S(2)}) copy-start(bf16[4,128,1024]{2,1,0:T(8,128)(2,1)} %get-tuple-element.187) | copy-start | bytes 3145732
  235.1 10.3 %copy-start.41 = (bf16[4,128,128]{2,1,0:T(8,128)(2,1)S(1)}, bf16[4,128,128]{2,1,0:T(8,128)(2,1)}, u32[]{:S(2)}) copy-start(bf16[4,128,128]{2,1,0:T(8,128)(2,1)} %copy.12) | copy-start | bytes 393220
  245.4 4.6 copy-start.22
  246.6 3.4 copy-start.3
  246.6 13.6 %copy-start.15 = (bf16[4,128,1024]{2,1,0:T(8,128)(2,1)}, bf16[4,128,1024]{2,1,0:T(8,128)(2,1)S(1)}, u32[]{:S(2)}) copy-start(bf16[4,128,1024]{2,1,0:T(8,128)(2,1)S(1)} %get-tuple-element.179) | copy-start | bytes 3145732
  246.6 3.4 copy-start.21
  246.6 3.4 copy-start.56
  246.6 3.4 copy-start.49
  246.7 3.5 copy-start.57
  246.7 4.1 copy-start.20
  253.0 2.2 copy-start.5
  263.8 94.6 %collective-permute-start.5 = (bf16[4,8,128,128]{2,3,0,1:T(8,128)(2,1)S(1)}, bf16[4,8,128,128]{2,3,0,1:T(8,128)(2,1)}, u32[]{:S(2)}, u32[]{:S(2)}) collective-permute-start(bf16[4,8,128,128]{2,3,0,1:T(8,128)(2,1)S(1)} %copy.73), channel_id=1, source_target_pairs={{15,0},{0,1},{1,2},{2,3},{3,4},{4,5},{5,6},{6,7},{7,8},{8,9},{9,10... | collective-permute-start | bytes 3145736 | tf_op jit(solution)/shard_map/ppermute | solution.py:10
  264.8 92.5 %collective-permute-start.4 = (bf16[3,8,128,128]{2,3,0,1:T(8,128)(2,1)}, bf16[3,8,128,128]{2,3,0,1:T(8,128)(2,1)}, u32[]{:S(2)}, u32[]{:S(2)}) collective-permute-start(bf16[3,8,128,128]{2,3,0,1:T(8,128)(2,1)} %slice.962), channel_id=1, source_target_pairs={{14,0},{15,1},{0,2},{1,3},{2,4},{3,5},{4,6},{5,7},{6,8},{7,9},{8,1... | collective-permute-start | bytes 2359304 | tf_op jit(solution)/shard_map/ppermute | solution.py:10
  267.5 95.1 %collective-permute-start.6 = (bf16[4,8,128,128]{3,2,0,1:T(8,128)(2,1)S(1)}, bf16[4,8,128,128]{3,2,0,1:T(8,128)(2,1)S(1)}, u32[]{:S(2)}, u32[]{:S(2)}) collective-permute-start(bf16[4,8,128,128]{3,2,0,1:T(8,128)(2,1)S(1)} %multiply_convert_fusion), channel_id=1, source_target_pairs={{1,0},{2,1},{3,2},{4,3},{5,4},{6,5},{7,6},{8,7},{9,8},{10,9},{11,1... | collective-permute-start | bytes 3145736 | tf_op jit(solution)/shard_map/ppermute | solution.py:10
  271.0 176.4 %collective-permute-start.7 = (bf16[3,8,128,128]{3,2,0,1:T(8,128)(2,1)}, bf16[3,8,128,128]{3,2,0,1:T(8,128)(2,1)}, u32[]{:S(2)}, u32[]{:S(2)}) collective-permute-start(bf16[3,8,128,128]{3,2,0,1:T(8,128)(2,1)} %slice.1053), channel_id=1, source_target_pairs={{2,0},{3,1},{4,2},{5,3},{6,4},{7,5},{8,6},{9,7},{10,8},{11,9},{12,... | collective-permute-start | bytes 2359304 | tf_op jit(solution)/shard_map/ppermute | solution.py:10
  366.4 12.1 %copy-start.35 = (bf16[4,1,128,128]{2,3,0,1:T(8,128)(2,1)}, bf16[4,1,128,128]{2,3,0,1:T(8,128)(2,1)S(1)}, u32[]{:S(2)}) copy-start(bf16[4,1,128,128]{2,3,0,1:T(8,128)(2,1)S(1)} %copy.152) | copy-start | bytes 393220
  368.2 11.1 %copy-start.37 = (bf16[4,1,128,128]{2,3,0,1:T(8,128)(2,1)}, bf16[4,1,128,128]{2,3,0,1:T(8,128)(2,1)S(1)}, u32[]{:S(2)}) copy-start(bf16[4,1,128,128]{2,3,0,1:T(8,128)(2,1)S(1)} %copy.145) | copy-start | bytes 393220
  376.1 2.3 copy-start.74
  376.1 2.4 copy-start.72
  376.1 2.5 copy-start.73
  376.1 2.6 copy-start.59
  376.1 3.9 copy-start.70
  413.2 10.4 %copy-start.75 = (bf16[4,128,128]{2,1,0:T(8,128)(2,1)S(1)}, bf16[4,128,128]{2,1,0:T(8,128)(2,1)}, u32[]{:S(2)}) copy-start(bf16[4,128,128]{2,1,0:T(8,128)(2,1)} %copy.88) | copy-start | bytes 393220
  413.2 11.1 %copy-start.76 = (bf16[4,128,128]{2,1,0:T(8,128)(2,1)S(1)}, bf16[4,128,128]{2,1,0:T(8,128)(2,1)}, u32[]{:S(2)}) copy-start(bf16[4,128,128]{2,1,0:T(8,128)(2,1)} %copy.89) | copy-start | bytes 393220
  447.4 10.0 %copy-start.39 = (bf16[4,1,128,128]{2,3,0,1:T(8,128)(2,1)S(1)}, bf16[4,1,128,128]{2,3,0,1:T(8,128)(2,1)}, u32[]{:S(2)}) copy-start(bf16[4,1,128,128]{2,3,0,1:T(8,128)(2,1)} %copy.149) | copy-start | bytes 393220
  460.4 11.4 %copy-start.40 = (bf16[4,1,128,128]{2,3,0,1:T(8,128)(2,1)S(1)}, bf16[4,1,128,128]{2,3,0,1:T(8,128)(2,1)}, u32[]{:S(2)}) copy-start(bf16[4,1,128,128]{2,3,0,1:T(8,128)(2,1)} %copy.155) | copy-start | bytes 393220
  481.6 2.8 copy-start.58
  481.6 3.4 copy-start.6
  485.1 2.3 copy-start.27
  (24 other events, 36.8 us)
where the time goes:
time: 502 us; the launch traced here: 494 us
  local copies, waits for them, and re-layouts  248 us (49%)
  waiting for transfers between devices  177 us (35%)
  other arithmetic  35.1 us (7%)
  matrix products  23.7 us (5%)
  starting transfers between devices  8.46 us (2%)
    ppermute x8, waiting for transfers between devices, from_behind(): return lax.ppermute(block, axis, route)  177 us
    unnamed x297, local copies, waits for them, and re-layouts  144 us
    squeeze x32, local copies, waits for them, and re-layouts, take_band(): return (extended[first:first + count, offset], False)  47.9 us
    unnamed x29, other arithmetic  25.3 us
    dot_general x16, matrix products, band_product(): jnp.einsum('nab,nbc->nac', left_wide, right_tall, preferred_element_type=...  23.7 us
    squeeze x21, local copies, waits for them, and re-layouts, take_band(): return (extended[first + offset:first + offset + count, -offset], True)  22.2 us
    slice x9, local copies, waits for them, and re-layouts, take_band(): return (extended[first:first + count, offset], False)  13.1 us
    concatenate x12, local copies, waits for them, and re-layouts, band_product(): right_tall = jnp.concatenate(right_pieces, axis=1)  11 us
  transfers between devices with their start and end apart: 8, of which 2 were waited for; matrix products, arithmetic and copies ran while one was open for 44% of the time, Pallas kernels for 0%

commit v1 on v0

v1 whole, which is shorter than its diff:
```python
import functools

import jax
import jax.numpy as jnp
from jax import lax
from jax.experimental import pallas as pl
from jax.experimental.pallas import tpu as pltpu
from jax.sharding import PartitionSpec as P

B = 128
NT = (((1,), (1,)), ((), ()))
NN = (((1,), (0,)), ((), ()))


def blk(a, n=1):
    return pl.ds(a * B, n * B)


def kernel(z_count, place, present, own, fw1, bw1, fw2, bw2, ends, cross, out, x_ref, y_ref):
    zero = jnp.zeros((B, B), jnp.bfloat16)
    for c in range(1, 9):
        x_ref[blk(0), blk(c)] = zero
    for c in range(11, 27):
        x_ref[blk(19), blk(c)] = zero
    for a in range(1, 19):
        if a % 2 == 0:
            x_ref[blk(a), blk(a + 8)] = zero
        elif a >= 9:
            x_ref[blk(a), blk(a - 8)] = zero

    def put(ref, first, a, count):
        for r in range(count):
            for k in range(8):
                u = ref[first + r, k]
                x_ref[blk(a + r), blk(a + r + k)] = u
                if 0 < k <= 18 - a - r:
                    x_ref[blk(a + r + k), blk(a + r)] = u.T

    z = place[0]
    put(own, 0, 8, 4)
    for at_end, ref, end_ref, first, end_first, a, count in (
        (z == 0, fw1, ends, 0, 0, 4, 4),
        (z == z_count - 1, bw1, ends, 0, 0, 12, 4),
        (z <= 1, fw2, cross, 1, 0, 1, 3),
        (z >= z_count - 2, bw2, cross, 0, 0, 16, 3),
    ):
        pl.when(at_end)(functools.partial(put, end_ref, end_first, a, count))
        pl.when(jnp.logical_not(at_end))(functools.partial(put, ref, first, a, count))

    for L in range(4, 10):
        for J in range(L - 4, L + 1):
            k0 = 2 * L - 7
            n = 2 * J + 9 - k0
            s = lax.dot_general(
                x_ref[blk(2 * J, 2), blk(k0, n)],
                x_ref[blk(2 * L, 2), blk(k0, n)],
                NT,
                preferred_element_type=jnp.float32,
            )
            for dj in range(2):
                for dl in range(2):
                    j, l = 2 * J + dj, 2 * L + dl
                    off = abs(l - j)
                    if off > 7 or j in (0, 19) or l in (0, 19):
                        y_ref[blk(j), blk(l - 8)] = zero
                    else:
                        w = present[min(j, l) * 8 + off].astype(jnp.float32)
                        y_ref[blk(j), blk(l - 8)] = (
                            s[dj * B : (dj + 1) * B, dl * B : (dl + 1) * B] * w
                        ).astype(jnp.bfloat16)
    for I in (4, 5):
        for L in range(I, I + 5):
            k0 = 2 * L - 7
            n = min(2 * L, 2 * I + 8) - k0 + 1
            c = lax.dot_general(
                x_ref[blk(2 * I, 2), blk(k0, n)],
                y_ref[blk(k0, n), blk(2 * L - 8, 2)],
                NN,
                preferred_element_type=jnp.float32,
            )
            n = 2 * I + 8 - 2 * L
            if n > 0:
                c += lax.dot_general(
                    x_ref[blk(2 * I, 2), blk(2 * L + 1, n)],
                    y_ref[blk(2 * L, 2), blk(2 * L - 7, n)],
                    NT,
                    preferred_element_type=jnp.float32,
                )
            for di in range(2):
                for dl in range(2):
                    i, l = 2 * I + di, 2 * L + dl
                    off = l - i
                    if 0 <= off <= 7:
                        w = present[i * 8 + off].astype(jnp.float32)
                        sq = y_ref[blk(i), blk(l - 8)].astype(jnp.float32)
                        cube = w * c[di * B : (di + 1) * B, dl * B : (dl + 1) * B]
                        out[i - 8, off] = (3.0 * sq - 2.0 * cube).astype(jnp.bfloat16)


def compute(z_count, place, present, *rows):
    smem = pl.BlockSpec(memory_space=pltpu.SMEM)
    vmem = pl.BlockSpec(memory_space=pltpu.VMEM)
    return pl.pallas_call(
        functools.partial(kernel, z_count),
        out_shape=jax.ShapeDtypeStruct(rows[0].shape, jnp.bfloat16),
        in_specs=[smem, smem] + [vmem] * len(rows),
        out_specs=vmem,
        scratch_shapes=[
            pltpu.VMEM((20 * B, 28 * B), jnp.bfloat16),
            pltpu.VMEM((20 * B, 12 * B), jnp.bfloat16),
        ],
        compiler_params=pltpu.CompilerParams(vmem_limit_bytes=56 * 1024 * 1024),
    )(place, present, *rows)


def per_device(upper, present):
    s_count, z_count = lax.axis_size("row"), lax.axis_size("col")
    s, z = lax.axis_index("row"), lax.axis_index("col")
    rows, wide = present.shape
    total = rows * s_count * z_count
    masked = upper * present.astype(jnp.bfloat16)[:, :, None, None]

    def step(block, d, pairs=None):
        pairs = pairs or [(i, i + d) for i in range(z_count) if 0 <= i + d < z_count]
        return lax.ppermute(block, "col", pairs)

    def hop(block, route):
        pairs = [
            (i * z_count + a, (i + d) % s_count * z_count + b)
            for i in range(s_count)
            for a, d, b in route
        ]
        return lax.ppermute(block, ("row", "col"), pairs)

    fw1, bw1 = step(masked, 1), step(masked, -1)
    last = z_count - 1
    ends = hop(masked, [(last, 1, 0), (0, -1, last)])
    fw2, bw2 = step(fw1, 1), step(bw1, -1)
    if z_count == 4:
        route = [(0, 1, 0), (1, 1, 1), (2, -1, 2), (3, -1, 3)]
        cross = hop(jnp.where(z < 2, bw2[1:], fw2[:3]), route)
    else:
        route = [(last - 1, 1, 0), (last, 1, 1), (0, -1, last - 1), (1, -1, last)]
        cross = hop(jnp.where(z < 2, masked[:3], masked[1:]), route)
    everyone = lax.all_gather(present, ("row", "col"), tiled=True)
    first = (s * z_count + z) * rows - 8
    window = (first + jnp.arange(20)) % total
    near = jnp.take(everyone, window, axis=0).reshape(-1)
    return compute(z_count, z.reshape(1), near, masked, fw1, bw1, fw2, bw2, ends, cross)


def solution(mesh):
    return jax.shard_map(
        per_device,
        mesh=mesh,
        in_specs=(P(("groups", "row", "col"), None, None, None), P(("groups", "row", "col"), None)),
        out_specs=P(("groups", "row", "col"), None, None, None),
        check_vma=False,
    )
```

time: 502 us -> 132 us (0.26)
  the two profiles are of different devices: /device:TPU:25 before, /device:TPU:0 now
where the time goes in v1:
time: 132 us
  blocking collectives  55.1 us (42%)
  waiting for transfers between devices  40.9 us (31%)
  starting transfers between devices  17 us (13%)
  Pallas kernels  14 us (11%)
  other arithmetic  3.2 us (2%)
  local copies, waits for them, and re-layouts  1.89 us (1%)
    all_gather x1, blocking collectives, per_device(): everyone = lax.all_gather(present, ('row', 'col'), tiled=True)  55.1 us
    ppermute x4, waiting for transfers between devices, step(): return lax.ppermute(block, 'col', pairs)  40.9 us
    pallas_call x1, Pallas kernels, compute(): pl.pallas_call(functools.partial(kernel, z_count), out_shape=jax.ShapeDty...  14 us
    ppermute x4, starting transfers between devices, step(): return lax.ppermute(block, 'col', pairs)  13.8 us
    ppermute x2, starting transfers between devices, hop(): return lax.ppermute(block, ('row', 'col'), pairs)  3.27 us
  transfers between devices with their start and end apart: 6, of which 3 were waited for; matrix products, arithmetic and copies ran while one was open for 2% of the time, Pallas kernels for 0%

profile of v1, /device:TPU:0, one launch (start us, length us, event | category | flops | bytes accessed | tf_op | source)
XLA Modules:
  0.0 132.1 jit_solution(4757558228324646102)
XLA Ops:
  0.0 0.7 convert_element_type.3
  0.7 1.4 %broadcast_multiply_fusion.own = bf16[4,8,128,128]{3,2,1,0:T(8,128)(2,1)S(1)} fusion(bf16[4,8,128,128]{3,2,1,0:T(8,128)(2,1)} %param.2, bf16[4,8]{1,0:T(4,128)(2,1)S(1)} %convert_element_type.3), kind=kLoop, calls=%fused_computation.2 | loop fusion | flops 524288 | bytes 2097216 | tf_op jit(solution)/shard_map/mul | solution.py:121
  2.1 0.0 copy-start
  2.1 1.3 collective-permute-start.1
  3.4 6.6 %collective-permute-start = (bf16[4,8,128,128]{3,2,1,0:T(8,128)(2,1)S(1)}, bf16[4,8,128,128]{3,2,1,0:T(8,128)(2,1)}, u32[]{:S(2)}, u32[]{:S(2)}) collective-permute-start(bf16[4,8,128,128]{3,2,1,0:T(8,128)(2,1)S(1)} %broadcast_multiply_fusion.own), channel_id=1, source_target_pairs={{0,1},{1,2},{2,3},{4,5},{5,6},{6,7},{8,9},{9,10},{10,11},{12,13},{... | collective-permute-start | bytes 3145736 | tf_op jit(solution)/shard_map/ppermute | solution.py:125
  9.9 20.3 %collective-permute-done.1.bw1 = bf16[4,8,128,128]{3,2,1,0:T(8,128)(2,1)} collective-permute-done((bf16[4,8,128,128]{3,2,1,0:T(8,128)(2,1)S(1)}, bf16[4,8,128,128]{3,2,1,0:T(8,128)(2,1)}, u32[]{:S(2)}, u32[]{:S(2)}) %collective-permute-start.1) | collective-permute-done | bytes 1048608 | tf_op jit(solution)/shard_map/ppermute | solution.py:125
  30.3 1.3 collective-permute-start.3
  31.5 0.0 collective-permute-done.fw1
  31.5 4.6 %collective-permute-start.2 = (bf16[4,8,128,128]{3,2,1,0:T(8,128)(2,1)}, bf16[4,8,128,128]{3,2,1,0:T(8,128)(2,1)S(1)}, u32[]{:S(2)}, u32[]{:S(2)}) collective-permute-start(bf16[4,8,128,128]{3,2,1,0:T(8,128)(2,1)} %collective-permute-done.fw1), channel_id=1, source_target_pairs={{0,1},{1,2},{2,3},{4,5},{5,6},{6,7},{8,9},{9,10},{10,11},{12,13},{... | collective-permute-start | bytes 3145736 | tf_op jit(solution)/shard_map/ppermute | solution.py:125
  36.2 3.3 %collective-permute-start.4 = (bf16[4,8,128,128]{3,2,1,0:T(8,128)(2,1)S(1)}, bf16[4,8,128,128]{3,2,1,0:T(8,128)(2,1)}, u32[]{:S(2)}, u32[]{:S(2)}) collective-permute-start(bf16[4,8,128,128]{3,2,1,0:T(8,128)(2,1)S(1)} %broadcast_multiply_fusion.own), channel_id=1, source_target_pairs={{3,4},{0,15},{7,8},{4,3},{11,12},{8,7},{15,0},{12,11},{19,20},{16,... | collective-permute-start | bytes 3145736 | tf_op jit(solution)/shard_map/ppermute | solution.py:133
  39.4 17.4 %collective-permute-done.3.bw2 = bf16[4,8,128,128]{3,2,1,0:T(8,128)(2,1)S(1)} collective-permute-done((bf16[4,8,128,128]{3,2,1,0:T(8,128)(2,1)}, bf16[4,8,128,128]{3,2,1,0:T(8,128)(2,1)S(1)}, u32[]{:S(2)}, u32[]{:S(2)}) %collective-permute-start.3) | collective-permute-done | bytes 1048608 | tf_op jit(solution)/shard_map/ppermute | solution.py:125
  56.9 0.0 copy-start.1
  56.9 3.1 %collective-permute-done.2.fw2 = bf16[4,8,128,128]{3,2,1,0:T(8,128)(2,1)S(1)} collective-permute-done((bf16[4,8,128,128]{3,2,1,0:T(8,128)(2,1)}, bf16[4,8,128,128]{3,2,1,0:T(8,128)(2,1)S(1)}, u32[]{:S(2)}, u32[]{:S(2)}) %collective-permute-start.2) | collective-permute-done | bytes 1048608 | tf_op jit(solution)/shard_map/ppermute | solution.py:125
  60.0 0.0 copy-start.2
  60.0 1.0 slice_select_fusion
  61.1 0.0 copy-done
  61.1 0.0 copy-done.1
  61.1 0.0 collective-permute-start.5
  61.1 0.0 copy-start.3
  61.1 0.7 copy-done.3
  61.8 55.1 %all-gather = s32[16,4,8]{2,1,0:T(4,128)S(1)} all-gather(s32[1,4,8]{2,1,0:T(4,128)S(1)} %bitcast.6), channel_id=1, replica_groups=mesh['groups'=2,'row'=4,'col'=4] {'row','col'}, dimensions={0}, use_global_device_ids=true | all-gather | bytes 2176 | tf_op jit(solution)/shard_map/all_gather | solution.py:145
  116.8 0.6 gather_fusion
  117.4 0.1 broadcast_select_fusion
  117.5 0.6 select_n.55.present
  118.1 0.0 collective-permute-done.4.ends
  118.1 0.0 collective-permute-done.5.cross
  118.2 0.0 copy-done.2
  118.2 14.0 %shard_map.28 = bf16[4,8,128,128]{3,2,1,0:T(8,128)(2,1)} custom-call(s32[1]{0:T(128)} %bitcast.place, s32[160]{0:T(256)} %select_n.55.present, bf16[4,8,128,128]{3,2,1,0:T(8,128)(2,1)} %copy-done, bf16[4,8,128,128]{3,2,1,0:T(8,128)(2,1)} %collective-permute-done.fw1, bf16[4,8,128,128]{3,2,1,0:T(8,128)(2,1)} %collective-permute-done.1.bw1, ...), custom_call_target="tpu_custom_call" | custom-call | tf_op jit(solution)/shard_map/pallas_call | solution.py:103
  (3 shorter events, 0.0 us)
Async XLA Ops:
  2.1 59.0 %copy-start = (bf16[4,8,128,128]{3,2,1,0:T(8,128)(2,1)}, bf16[4,8,128,128]{3,2,1,0:T(8,128)(2,1)S(1)}, u32[]{:S(2)}) copy-start(bf16[4,8,128,128]{3,2,1,0:T(8,128)(2,1)S(1)} %broadcast_multiply_fusion.own) | copy-start | bytes 3145732
  2.1 28.2 %collective-permute-start.1 = (bf16[4,8,128,128]{3,2,1,0:T(8,128)(2,1)S(1)}, bf16[4,8,128,128]{3,2,1,0:T(8,128)(2,1)}, u32[]{:S(2)}, u32[]{:S(2)}) collective-permute-start(bf16[4,8,128,128]{3,2,1,0:T(8,128)(2,1)S(1)} %broadcast_multiply_fusion.own), channel_id=1, source_target_pairs={{1,0},{2,1},{3,2},{5,4},{6,5},{7,6},{9,8},{10,9},{11,10},{13,12},{... | collective-permute-start | bytes 3145736 | tf_op jit(solution)/shard_map/ppermute | solution.py:125
  3.4 28.2 %collective-permute-start = (bf16[4,8,128,128]{3,2,1,0:T(8,128)(2,1)S(1)}, bf16[4,8,128,128]{3,2,1,0:T(8,128)(2,1)}, u32[]{:S(2)}, u32[]{:S(2)}) collective-permute-start(bf16[4,8,128,128]{3,2,1,0:T(8,128)(2,1)S(1)} %broadcast_multiply_fusion.own), channel_id=1, source_target_pairs={{0,1},{1,2},{2,3},{4,5},{5,6},{6,7},{8,9},{9,10},{10,11},{12,13},{... | collective-permute-start | bytes 3145736 | tf_op jit(solution)/shard_map/ppermute | solution.py:125
  30.3 26.6 %collective-permute-start.3 = (bf16[4,8,128,128]{3,2,1,0:T(8,128)(2,1)}, bf16[4,8,128,128]{3,2,1,0:T(8,128)(2,1)S(1)}, u32[]{:S(2)}, u32[]{:S(2)}) collective-permute-start(bf16[4,8,128,128]{3,2,1,0:T(8,128)(2,1)} %collective-permute-done.1.bw1), channel_id=1, source_target_pairs={{1,0},{2,1},{3,2},{5,4},{6,5},{7,6},{9,8},{10,9},{11,10},{13,12},{... | collective-permute-start | bytes 3145736 | tf_op jit(solution)/shard_map/ppermute | solution.py:125
  31.5 28.5 %collective-permute-start.2 = (bf16[4,8,128,128]{3,2,1,0:T(8,128)(2,1)}, bf16[4,8,128,128]{3,2,1,0:T(8,128)(2,1)S(1)}, u32[]{:S(2)}, u32[]{:S(2)}) collective-permute-start(bf16[4,8,128,128]{3,2,1,0:T(8,128)(2,1)} %collective-permute-done.fw1), channel_id=1, source_target_pairs={{0,1},{1,2},{2,3},{4,5},{5,6},{6,7},{8,9},{9,10},{10,11},{12,13},{... | collective-permute-start | bytes 3145736 | tf_op jit(solution)/shard_map/ppermute | solution.py:125
  36.2 82.0 %collective-permute-start.4 = (bf16[4,8,128,128]{3,2,1,0:T(8,128)(2,1)S(1)}, bf16[4,8,128,128]{3,2,1,0:T(8,128)(2,1)}, u32[]{:S(2)}, u32[]{:S(2)}) collective-permute-start(bf16[4,8,128,128]{3,2,1,0:T(8,128)(2,1)S(1)} %broadcast_multiply_fusion.own), channel_id=1, source_target_pairs={{3,4},{0,15},{7,8},{4,3},{11,12},{8,7},{15,0},{12,11},{19,20},{16,... | collective-permute-start | bytes 3145736 | tf_op jit(solution)/shard_map/ppermute | solution.py:133
  56.9 4.2 %copy-start.1 = (bf16[4,8,128,128]{3,2,1,0:T(8,128)(2,1)}, bf16[4,8,128,128]{3,2,1,0:T(8,128)(2,1)S(1)}, u32[]{:S(2)}) copy-start(bf16[4,8,128,128]{3,2,1,0:T(8,128)(2,1)S(1)} %collective-permute-done.3.bw2) | copy-start | bytes 3145732
  60.0 58.1 %copy-start.2 = (bf16[4,8,128,128]{3,2,1,0:T(8,128)(2,1)}, bf16[4,8,128,128]{3,2,1,0:T(8,128)(2,1)S(1)}, u32[]{:S(2)}) copy-start(bf16[4,8,128,128]{3,2,1,0:T(8,128)(2,1)S(1)} %collective-permute-done.2.fw2) | copy-start | bytes 3145732
  61.1 57.1 %collective-permute-start.5 = (bf16[3,8,128,128]{3,2,1,0:T(8,128)(2,1)}, bf16[3,8,128,128]{3,2,1,0:T(8,128)(2,1)}, u32[]{:S(2)}, u32[]{:S(2)}) collective-permute-start(bf16[3,8,128,128]{3,2,1,0:T(8,128)(2,1)} %slice_select_fusion), channel_id=1, source_target_pairs={{0,4},{1,5},{2,14},{3,15},{4,8},{5,9},{6,2},{7,3},{8,12},{9,13},{1... | collective-permute-start | bytes 2359304 | tf_op jit(solution)/shard_map/ppermute | solution.py:133
  61.1 0.7 copy-start.3

commit v2 on v1

--- a/solution.py
+++ b/solution.py
@@ -16,8 +16,9 @@
     return pl.ds(a * B, n * B)
 
 
-def kernel(z_count, place, present, own, fw1, bw1, fw2, bw2, ends, cross, out, x_ref, y_ref):
+def kernel(z_count, place, own, fw1, bw1, fw2, bw2, ends, cross, out, x_ref, y_ref, w_ref):
     zero = jnp.zeros((B, B), jnp.bfloat16)
+    blk8 = pl.ds(8 * B, 16)
     for c in range(1, 9):
         x_ref[blk(0), blk(c)] = zero
     for c in range(11, 27):
@@ -30,8 +31,9 @@
 
     def put(ref, first, a, count):
         for r in range(count):
+            w_ref[a + r] = ref[first + r, blk8].astype(jnp.float32)
             for k in range(8):
-                u = ref[first + r, k]
+                u = ref[first + r, blk(k)]
                 x_ref[blk(a + r), blk(a + r + k)] = u
                 if 0 < k <= 18 - a - r:
                     x_ref[blk(a + r + k), blk(a + r)] = u.T
@@ -64,7 +66,7 @@
                     if off > 7 or j in (0, 19) or l in (0, 19):
                         y_ref[blk(j), blk(l - 8)] = zero
                     else:
-                        w = present[min(j, l) * 8 + off].astype(jnp.float32)
+                        w = w_ref[min(j, l), pl.ds(off, 1)]
                         y_ref[blk(j), blk(l - 8)] = (
                             s[dj * B : (dj + 1) * B, dl * B : (dl + 1) * B] * w
                         ).astype(jnp.bfloat16)
@@ -91,34 +93,37 @@
                     i, l = 2 * I + di, 2 * L + dl
                     off = l - i
                     if 0 <= off <= 7:
-                        w = present[i * 8 + off].astype(jnp.float32)
+                        w = w_ref[i, pl.ds(off, 1)]
                         sq = y_ref[blk(i), blk(l - 8)].astype(jnp.float32)
                         cube = w * c[di * B : (di + 1) * B, dl * B : (dl + 1) * B]
                         out[i - 8, off] = (3.0 * sq - 2.0 * cube).astype(jnp.bfloat16)
 
 
-def compute(z_count, place, present, *rows):
+def compute(z_count, place, *rows):
     smem = pl.BlockSpec(memory_space=pltpu.SMEM)
     vmem = pl.BlockSpec(memory_space=pltpu.VMEM)
     return pl.pallas_call(
         functools.partial(kernel, z_count),
-        out_shape=jax.ShapeDtypeStruct(rows[0].shape, jnp.bfloat16),
-        in_specs=[smem, smem] + [vmem] * len(rows),
+        out_shape=jax.ShapeDtypeStruct((4, 8, B, B), jnp.bfloat16),
+        in_specs=[smem] + [vmem] * len(rows),
         out_specs=vmem,
         scratch_shapes=[
             pltpu.VMEM((20 * B, 28 * B), jnp.bfloat16),
             pltpu.VMEM((20 * B, 12 * B), jnp.bfloat16),
+            pltpu.VMEM((20, 16, B), jnp.float32),
         ],
         compiler_params=pltpu.CompilerParams(vmem_limit_bytes=56 * 1024 * 1024),
-    )(place, present, *rows)
+    )(place, *rows)
 
 
 def per_device(upper, present):
     s_count, z_count = lax.axis_size("row"), lax.axis_size("col")
-    s, z = lax.axis_index("row"), lax.axis_index("col")
+    z = lax.axis_index("col")
     rows, wide = present.shape
-    total = rows * s_count * z_count
-    masked = upper * present.astype(jnp.bfloat16)[:, :, None, None]
+    weights = present.astype(jnp.bfloat16)[:, :, None, None]
+    blocks = (upper * weights).reshape(rows, wide * B, B)
+    pattern = jnp.broadcast_to(weights[:, :, 0], (rows, wide, B))
+    masked = jnp.concatenate([blocks, pattern, pattern], axis=1)
 
     def step(block, d, pairs=None):
         pairs = pairs or [(i, i + d) for i in range(z_count) if 0 <= i + d < z_count]
@@ -142,11 +147,7 @@
     else:
         route = [(last - 1, 1, 0), (last, 1, 1), (0, -1, last - 1), (1, -1, last)]
         cross = hop(jnp.where(z < 2, masked[:3], masked[1:]), route)
-    everyone = lax.all_gather(present, ("row", "col"), tiled=True)
-    first = (s * z_count + z) * rows - 8
-    window = (first + jnp.arange(20)) % total
-    near = jnp.take(everyone, window, axis=0).reshape(-1)
-    return compute(z_count, z.reshape(1), near, masked, fw1, bw1, fw2, bw2, ends, cross)
+    return compute(z_count, z.reshape(1), masked, fw1, bw1, fw2, bw2, ends, cross)
 
 
 def solution(mesh):

time: 132 us -> 108 us (0.82)
  the two profiles are of different devices: /device:TPU:0 before, /device:TPU:25 now
where the time goes in v2:
time: 108 us
  waiting for transfers between devices  49.7 us (46%)
  starting transfers between devices  41.2 us (38%)
  Pallas kernels  14 us (13%)
  other arithmetic  2.19 us (2%)
    ppermute x4, waiting for transfers between devices, step(): return lax.ppermute(block, 'col', pairs)  38.8 us
    ppermute x2, starting transfers between devices, hop(): return lax.ppermute(block, ('row', 'col'), pairs)  31.3 us
    pallas_call x1, Pallas kernels, compute(): pl.pallas_call(functools.partial(kernel, z_count), out_shape=jax.ShapeDty...  14 us
    ppermute x2, waiting for transfers between devices, hop(): return lax.ppermute(block, ('row', 'col'), pairs)  10.9 us
    ppermute x4, starting transfers between devices, step(): return lax.ppermute(block, 'col', pairs)  9.9 us
  transfers between devices with their start and end apart: 6, of which 5 were waited for; matrix products, arithmetic and copies ran while one was open for 0% of the time, Pallas kernels for 0%

profile of v2, /device:TPU:25, one launch (start us, length us, event | category | flops | bytes accessed | tf_op | source)
XLA Modules:
  0.0 108.2 jit_solution(4564723674048669462)
XLA Ops:
  0.0 0.7 convert_element_type.3
  0.7 1.4 %broadcast_multiply_fusion = bf16[4,8,128,128]{3,2,1,0:T(8,128)(2,1)S(1)} fusion(bf16[4,8,128,128]{3,2,1,0:T(8,128)(2,1)} %param.2, bf16[4,8]{1,0:T(4,128)(2,1)S(1)} %convert_element_type.3), kind=kLoop, calls=%fused_computation.2 | loop fusion | flops 524288 | bytes 2097216 | tf_op jit(solution)/shard_map/mul | solution.py:124
  2.1 0.1 broadcast_in_dim.2
  2.1 0.1 pad_maximum_fusion.own
  2.2 0.0 copy-start
  2.2 3.1 %collective-permute-start.1 = (bf16[4,1040,128]{2,1,0:T(8,128)(2,1)S(1)}, bf16[4,1040,128]{2,1,0:T(8,128)(2,1)}, u32[]{:S(2)}, u32[]{:S(2)}) collective-permute-start(bf16[4,1040,128]{2,1,0:T(8,128)(2,1)S(1)} %pad_maximum_fusion.own), channel_id=1, source_target_pairs={{1,0},{2,1},{3,2},{5,4},{6,5},{7,6},{9,8},{10,9},{11,10},{13,12},{... | collective-permute-start | bytes 3194888 | tf_op jit(solution)/shard_map/ppermute | solution.py:130
  5.3 1.3 %collective-permute-start = (bf16[4,1040,128]{2,1,0:T(8,128)(2,1)S(1)}, bf16[4,1040,128]{2,1,0:T(8,128)(2,1)}, u32[]{:S(2)}, u32[]{:S(2)}) collective-permute-start(bf16[4,1040,128]{2,1,0:T(8,128)(2,1)S(1)} %pad_maximum_fusion.own), channel_id=1, source_target_pairs={{0,1},{1,2},{2,3},{4,5},{5,6},{6,7},{8,9},{9,10},{10,11},{12,13},{... | collective-permute-start | bytes 3194888 | tf_op jit(solution)/shard_map/ppermute | solution.py:130
  6.6 19.9 %collective-permute-done.1.bw1 = bf16[4,1040,128]{2,1,0:T(8,128)(2,1)} collective-permute-done((bf16[4,1040,128]{2,1,0:T(8,128)(2,1)S(1)}, bf16[4,1040,128]{2,1,0:T(8,128)(2,1)}, u32[]{:S(2)}, u32[]{:S(2)}) %collective-permute-start.1) | collective-permute-done | bytes 1064992 | tf_op jit(solution)/shard_map/ppermute | solution.py:130
  26.5 4.3 %collective-permute-start.3 = (bf16[4,1040,128]{2,1,0:T(8,128)(2,1)}, bf16[4,1040,128]{2,1,0:T(8,128)(2,1)S(1)}, u32[]{:S(2)}, u32[]{:S(2)}) collective-permute-start(bf16[4,1040,128]{2,1,0:T(8,128)(2,1)} %collective-permute-done.1.bw1), channel_id=1, source_target_pairs={{1,0},{2,1},{3,2},{5,4},{6,5},{7,6},{9,8},{10,9},{11,10},{13,12},{... | collective-permute-start | bytes 3194888 | tf_op jit(solution)/shard_map/ppermute | solution.py:130
  30.7 0.6 collective-permute-done.fw1
  31.3 1.3 %collective-permute-start.2 = (bf16[4,1040,128]{2,1,0:T(8,128)(2,1)}, bf16[4,1040,128]{2,1,0:T(8,128)(2,1)S(1)}, u32[]{:S(2)}, u32[]{:S(2)}) collective-permute-start(bf16[4,1040,128]{2,1,0:T(8,128)(2,1)} %collective-permute-done.fw1), channel_id=1, source_target_pairs={{0,1},{1,2},{2,3},{4,5},{5,6},{6,7},{8,9},{9,10},{10,11},{12,13},{... | collective-permute-start | bytes 3194888 | tf_op jit(solution)/shard_map/ppermute | solution.py:130
  32.6 6.1 %collective-permute-start.4 = (bf16[4,1040,128]{2,1,0:T(8,128)(2,1)S(1)}, bf16[4,1040,128]{2,1,0:T(8,128)(2,1)}, u32[]{:S(2)}, u32[]{:S(2)}) collective-permute-start(bf16[4,1040,128]{2,1,0:T(8,128)(2,1)S(1)} %pad_maximum_fusion.own), channel_id=1, source_target_pairs={{3,4},{0,15},{7,8},{4,3},{11,12},{8,7},{15,0},{12,11},{19,20},{16,... | collective-permute-start | bytes 3194888 | tf_op jit(solution)/shard_map/ppermute | solution.py:138
  38.7 13.5 %collective-permute-done.3.bw2 = bf16[4,1040,128]{2,1,0:T(8,128)(2,1)S(1)} collective-permute-done((bf16[4,1040,128]{2,1,0:T(8,128)(2,1)}, bf16[4,1040,128]{2,1,0:T(8,128)(2,1)S(1)}, u32[]{:S(2)}, u32[]{:S(2)}) %collective-permute-start.3) | collective-permute-done | bytes 1064992 | tf_op jit(solution)/shard_map/ppermute | solution.py:130
  52.2 0.0 copy-start.1
  52.2 4.8 %collective-permute-done.2.fw2 = bf16[4,1040,128]{2,1,0:T(8,128)(2,1)S(1)} collective-permute-done((bf16[4,1040,128]{2,1,0:T(8,128)(2,1)}, bf16[4,1040,128]{2,1,0:T(8,128)(2,1)S(1)}, u32[]{:S(2)}, u32[]{:S(2)}) %collective-permute-start.2) | collective-permute-done | bytes 1064992 | tf_op jit(solution)/shard_map/ppermute | solution.py:130
  57.0 0.0 copy-start.2
  57.0 0.1 slice_select_fusion
  57.1 0.0 copy-done
  57.1 0.0 copy-done.1
  57.1 25.2 %collective-permute-start.5 = (bf16[3,1040,128]{2,1,0:T(8,128)(2,1)S(1)}, bf16[3,1040,128]{2,1,0:T(8,128)(2,1)S(1)}, u32[]{:S(2)}, u32[]{:S(2)}) collective-permute-start(bf16[3,1040,128]{2,1,0:T(8,128)(2,1)S(1)} %slice_select_fusion), channel_id=1, source_target_pairs={{0,4},{1,5},{2,14},{3,15},{4,8},{5,9},{6,2},{7,3},{8,12},{9,13},{1... | collective-permute-start | bytes 2396168 | tf_op jit(solution)/shard_map/ppermute | solution.py:138
  82.3 0.0 collective-permute-done.4.ends
  82.3 10.9 %collective-permute-done.5.cross = bf16[3,1040,128]{2,1,0:T(8,128)(2,1)S(1)} collective-permute-done((bf16[3,1040,128]{2,1,0:T(8,128)(2,1)S(1)}, bf16[3,1040,128]{2,1,0:T(8,128)(2,1)S(1)}, u32[]{:S(2)}, u32[]{:S(2)}) %collective-permute-start.5) | collective-permute-done | bytes 798752 | tf_op jit(solution)/shard_map/ppermute | solution.py:138
  93.2 0.0 copy-start.3
  93.2 0.0 copy-done.2
  93.2 0.9 copy-done.3
  94.1 14.0 %shard_map.28 = bf16[4,8,128,128]{3,2,1,0:T(8,128)(2,1)} custom-call(s32[1]{0:T(128)} %bitcast.place, bf16[4,1040,128]{2,1,0:T(8,128)(2,1)} %copy-done, bf16[4,1040,128]{2,1,0:T(8,128)(2,1)} %collective-permute-done.fw1, bf16[4,1040,128]{2,1,0:T(8,128)(2,1)} %collective-permute-done.1.bw1, bf16[4,1040,128]{2,1,0:T(8,128)(2,1)} %copy-done.2, ...), custom_call_target="tpu_custom_call" | custom-call | tf_op jit(solution)/shard_map/pallas_call | solution.py:105
Async XLA Ops:
  2.2 54.9 %copy-start = (bf16[4,1040,128]{2,1,0:T(8,128)(2,1)}, bf16[4,1040,128]{2,1,0:T(8,128)(2,1)S(1)}, u32[]{:S(2)}) copy-start(bf16[4,1040,128]{2,1,0:T(8,128)(2,1)S(1)} %pad_maximum_fusion.own) | copy-start | bytes 3194884
  2.2 24.2 %collective-permute-start.1 = (bf16[4,1040,128]{2,1,0:T(8,128)(2,1)S(1)}, bf16[4,1040,128]{2,1,0:T(8,128)(2,1)}, u32[]{:S(2)}, u32[]{:S(2)}) collective-permute-start(bf16[4,1040,128]{2,1,0:T(8,128)(2,1)S(1)} %pad_maximum_fusion.own), channel_id=1, source_target_pairs={{1,0},{2,1},{3,2},{5,4},{6,5},{7,6},{9,8},{10,9},{11,10},{13,12},{... | collective-permute-start | bytes 3194888 | tf_op jit(solution)/shard_map/ppermute | solution.py:130
  5.3 26.0 %collective-permute-start = (bf16[4,1040,128]{2,1,0:T(8,128)(2,1)S(1)}, bf16[4,1040,128]{2,1,0:T(8,128)(2,1)}, u32[]{:S(2)}, u32[]{:S(2)}) collective-permute-start(bf16[4,1040,128]{2,1,0:T(8,128)(2,1)S(1)} %pad_maximum_fusion.own), channel_id=1, source_target_pairs={{0,1},{1,2},{2,3},{4,5},{5,6},{6,7},{8,9},{9,10},{10,11},{12,13},{... | collective-permute-start | bytes 3194888 | tf_op jit(solution)/shard_map/ppermute | solution.py:130
  26.5 25.8 %collective-permute-start.3 = (bf16[4,1040,128]{2,1,0:T(8,128)(2,1)}, bf16[4,1040,128]{2,1,0:T(8,128)(2,1)S(1)}, u32[]{:S(2)}, u32[]{:S(2)}) collective-permute-start(bf16[4,1040,128]{2,1,0:T(8,128)(2,1)} %collective-permute-done.1.bw1), channel_id=1, source_target_pairs={{1,0},{2,1},{3,2},{5,4},{6,5},{7,6},{9,8},{10,9},{11,10},{13,12},{... | collective-permute-start | bytes 3194888 | tf_op jit(solution)/shard_map/ppermute | solution.py:130
  31.3 25.7 %collective-permute-start.2 = (bf16[4,1040,128]{2,1,0:T(8,128)(2,1)}, bf16[4,1040,128]{2,1,0:T(8,128)(2,1)S(1)}, u32[]{:S(2)}, u32[]{:S(2)}) collective-permute-start(bf16[4,1040,128]{2,1,0:T(8,128)(2,1)} %collective-permute-done.fw1), channel_id=1, source_target_pairs={{0,1},{1,2},{2,3},{4,5},{5,6},{6,7},{8,9},{9,10},{10,11},{12,13},{... | collective-permute-start | bytes 3194888 | tf_op jit(solution)/shard_map/ppermute | solution.py:130
  32.6 49.7 %collective-permute-start.4 = (bf16[4,1040,128]{2,1,0:T(8,128)(2,1)S(1)}, bf16[4,1040,128]{2,1,0:T(8,128)(2,1)}, u32[]{:S(2)}, u32[]{:S(2)}) collective-permute-start(bf16[4,1040,128]{2,1,0:T(8,128)(2,1)S(1)} %pad_maximum_fusion.own), channel_id=1, source_target_pairs={{3,4},{0,15},{7,8},{4,3},{11,12},{8,7},{15,0},{12,11},{19,20},{16,... | collective-permute-start | bytes 3194888 | tf_op jit(solution)/shard_map/ppermute | solution.py:138
  52.2 4.9 %copy-start.1 = (bf16[4,1040,128]{2,1,0:T(8,128)(2,1)}, bf16[4,1040,128]{2,1,0:T(8,128)(2,1)S(1)}, u32[]{:S(2)}) copy-start(bf16[4,1040,128]{2,1,0:T(8,128)(2,1)S(1)} %collective-permute-done.3.bw2) | copy-start | bytes 3194884
  57.0 36.2 %copy-start.2 = (bf16[4,1040,128]{2,1,0:T(8,128)(2,1)}, bf16[4,1040,128]{2,1,0:T(8,128)(2,1)S(1)}, u32[]{:S(2)}) copy-start(bf16[4,1040,128]{2,1,0:T(8,128)(2,1)S(1)} %collective-permute-done.2.fw2) | copy-start | bytes 3194884
  57.1 36.1 %collective-permute-start.5 = (bf16[3,1040,128]{2,1,0:T(8,128)(2,1)S(1)}, bf16[3,1040,128]{2,1,0:T(8,128)(2,1)S(1)}, u32[]{:S(2)}, u32[]{:S(2)}) collective-permute-start(bf16[3,1040,128]{2,1,0:T(8,128)(2,1)S(1)} %slice_select_fusion), channel_id=1, source_target_pairs={{0,4},{1,5},{2,14},{3,15},{4,8},{5,9},{6,2},{7,3},{8,12},{9,13},{1... | collective-permute-start | bytes 2396168 | tf_op jit(solution)/shard_map/ppermute | solution.py:138
  93.2 0.9 copy-start.3

commit v3 on v2

--- a/solution.py
+++ b/solution.py
@@ -16,7 +16,7 @@
     return pl.ds(a * B, n * B)
 
 
-def kernel(z_count, place, own, fw1, bw1, fw2, bw2, ends, cross, out, x_ref, y_ref, w_ref):
+def kernel(z_count, place, own, fw1a, fw1b, bw1a, bw1b, fw2a, fw2b, bw2a, bw2b, endsa, endsb, cross, out, x_ref, y_ref, w_ref):
     zero = jnp.zeros((B, B), jnp.bfloat16)
     blk8 = pl.ds(8 * B, 16)
     for c in range(1, 9):
@@ -41,10 +41,14 @@
     z = place[0]
     put(own, 0, 8, 4)
     for at_end, ref, end_ref, first, end_first, a, count in (
-        (z == 0, fw1, ends, 0, 0, 4, 4),
-        (z == z_count - 1, bw1, ends, 0, 0, 12, 4),
-        (z <= 1, fw2, cross, 1, 0, 1, 3),
-        (z >= z_count - 2, bw2, cross, 0, 0, 16, 3),
+        (z == 0, fw1a, endsa, 0, 0, 4, 2),
+        (z == 0, fw1b, endsb, 0, 0, 6, 2),
+        (z == z_count - 1, bw1a, endsa, 0, 0, 12, 2),
+        (z == z_count - 1, bw1b, endsb, 0, 0, 14, 2),
+        (z <= 1, fw2a, cross, 1, 0, 1, 1),
+        (z <= 1, fw2b, cross, 0, 1, 2, 2),
+        (z >= z_count - 2, bw2a, cross, 0, 0, 16, 2),
+        (z >= z_count - 2, bw2b, cross, 0, 2, 18, 1),
     ):
         pl.when(at_end)(functools.partial(put, end_ref, end_first, a, count))
         pl.when(jnp.logical_not(at_end))(functools.partial(put, ref, first, a, count))
@@ -137,17 +141,26 @@
         ]
         return lax.ppermute(block, ("row", "col"), pairs)
 
-    fw1, bw1 = step(masked, 1), step(masked, -1)
     last = z_count - 1
-    ends = hop(masked, [(last, 1, 0), (0, -1, last)])
-    fw2, bw2 = step(fw1, 1), step(bw1, -1)
+    inner = range(1, last)
+    parts = [masked[: rows // 2], masked[rows // 2 :]]
+    fw1 = [step(part, 1) for part in parts]
+    bw1 = [step(part, -1) for part in parts]
+    fw2 = [step(part, 1, [(i, i + 1) for i in inner]) for part in fw1]
+    bw2 = [step(part, -1, [(i, i - 1) for i in inner]) for part in bw1]
     if z_count == 4:
+        ends = [
+            hop(jnp.where(z < 2, down, up), [(1, 1, 0), (2, -1, 3)]) for down, up in zip(bw2, fw2)
+        ]
         route = [(0, 1, 0), (1, 1, 1), (2, -1, 2), (3, -1, 3)]
-        cross = hop(jnp.where(z < 2, bw2[1:], fw2[:3]), route)
+        below = jnp.concatenate([bw2[0][1:], bw2[1]])
+        above = jnp.concatenate([fw2[0], fw2[1][:1]])
+        cross = hop(jnp.where(z < 2, below, above), route)
     else:
+        ends = [hop(part, [(last, 1, 0), (0, -1, last)]) for part in parts]
         route = [(last - 1, 1, 0), (last, 1, 1), (0, -1, last - 1), (1, -1, last)]
         cross = hop(jnp.where(z < 2, masked[:3], masked[1:]), route)
-    return compute(z_count, z.reshape(1), masked, fw1, bw1, fw2, bw2, ends, cross)
+    return compute(z_count, z.reshape(1), masked, *fw1, *bw1, *fw2, *bw2, *ends, cross)
 
 
 def solution(mesh):

time: 108 us -> 94.9 us (0.88)
  starting transfers between devices: 41.2 us -> 19.4 us
  waiting for transfers between devices: 49.7 us -> 56 us
  local copies, waits for them, and re-layouts: 0.99 us -> 2.23 us
    ppermute x2 -> x3, starting transfers between devices: 31.3 us -> 5.97 us  [hop(): return lax.ppermute(block, ('row', 'col'), pairs)]
    ppermute x2 -> x3, waiting for transfers between devices: 10.9 us -> 20 us  [hop(): return lax.ppermute(block, ('row', 'col'), pairs)]
    ppermute x4 -> x8, starting transfers between devices: 9.9 us -> 13.4 us  [step(): return lax.ppermute(block, 'col', pairs)]
    ppermute x4 -> x8, waiting for transfers between devices: 38.8 us -> 35.9 us  [step(): return lax.ppermute(block, 'col', pairs)]
    unnamed x8 -> x20, local copies, waits for them, and re-layouts: 0.92 us -> 2.04 us
  transfers between devices with their start and end apart: 6 -> 11, of which waited for: 5 -> 8; matrix products, arithmetic and copies ran while one was open for 0% -> 0% of each run, Pallas kernels for 0% -> 0%
where the time goes in v3:
time: 94.9 us; the launch traced here: 94.5 us
  waiting for transfers between devices  56 us (59%)
  starting transfers between devices  19.4 us (20%)
  Pallas kernels  14.4 us (15%)
  other arithmetic  2.36 us (2%)
  local copies, waits for them, and re-layouts  2.23 us (2%)
    ppermute x8, waiting for transfers between devices, step(): return lax.ppermute(block, 'col', pairs)  35.9 us
    ppermute x3, waiting for transfers between devices, hop(): return lax.ppermute(block, ('row', 'col'), pairs)  20 us
    pallas_call x1, Pallas kernels, compute(): pl.pallas_call(functools.partial(kernel, z_count), out_shape=jax.ShapeDty...  14.4 us
    ppermute x8, starting transfers between devices, step(): return lax.ppermute(block, 'col', pairs)  13.4 us
    ppermute x3, starting transfers between devices, hop(): return lax.ppermute(block, ('row', 'col'), pairs)  5.97 us
    unnamed x20, local copies, waits for them, and re-layouts  2.04 us
  transfers between devices with their start and end apart: 11, of which 8 were waited for; matrix products, arithmetic and copies ran while one was open for 0% of the time, Pallas kernels for 0%

profile of v3, /device:TPU:25, one launch (start us, length us, event | category | flops | bytes accessed | tf_op | source)
XLA Modules:
  0.0 94.5 jit_solution(11049525279194311738)
XLA Ops:
  0.0 0.7 convert_element_type.3
  0.7 1.4 %broadcast_multiply_fusion = bf16[4,8,128,128]{3,2,1,0:T(8,128)(2,1)S(1)} fusion(bf16[4,8,128,128]{3,2,1,0:T(8,128)(2,1)} %param.2, bf16[4,8]{1,0:T(4,128)(2,1)S(1)} %convert_element_type.3), kind=kLoop, calls=%fused_computation.4 | loop fusion | flops 524288 | bytes 2097216 | tf_op jit(solution)/shard_map/mul | solution.py:128
  2.1 0.1 broadcast_in_dim.2
  2.1 0.1 pad_maximum_fusion.own
  2.2 0.0 copy-start
  2.2 0.1 fusion
  2.3 0.9 copy-done
  3.2 2.1 %collective-permute-start.3 = (bf16[2,1040,128]{2,1,0:T(8,128)(2,1)S(1)}, bf16[2,1040,128]{2,1,0:T(8,128)(2,1)S(1)}, u32[]{:S(2)}, u32[]{:S(2)}) collective-permute-start(bf16[2,1040,128]{2,1,0:T(8,128)(2,1)S(1)} %get-tuple-element.5), channel_id=1, source_target_pairs={{1,0},{2,1},{3,2},{5,4},{6,5},{7,6},{9,8},{10,9},{11,10},{13,12},{... | collective-permute-start | bytes 1597448 | tf_op jit(solution)/shard_map/ppermute | solution.py:134
  5.3 1.3 %collective-permute-start.1 = (bf16[2,1040,128]{2,1,0:T(8,128)(2,1)S(1)}, bf16[2,1040,128]{2,1,0:T(8,128)(2,1)S(1)}, u32[]{:S(2)}, u32[]{:S(2)}) collective-permute-start(bf16[2,1040,128]{2,1,0:T(8,128)(2,1)S(1)} %get-tuple-element.5), channel_id=1, source_target_pairs={{0,1},{1,2},{2,3},{4,5},{5,6},{6,7},{8,9},{9,10},{10,11},{12,13},{... | collective-permute-start | bytes 1597448 | tf_op jit(solution)/shard_map/ppermute | solution.py:134
  6.6 4.8 %collective-permute-start.2 = (bf16[2,1040,128]{2,1,0:T(8,128)(2,1)S(1)}, bf16[2,1040,128]{2,1,0:T(8,128)(2,1)}, u32[]{:S(2)}, u32[]{:S(2)}) collective-permute-start(bf16[2,1040,128]{2,1,0:T(8,128)(2,1)S(1)} %get-tuple-element.6), channel_id=1, source_target_pairs={{1,0},{2,1},{3,2},{5,4},{6,5},{7,6},{9,8},{10,9},{11,10},{13,12},{... | collective-permute-start | bytes 1597448 | tf_op jit(solution)/shard_map/ppermute | solution.py:134
  11.4 1.3 %collective-permute-start = (bf16[2,1040,128]{2,1,0:T(8,128)(2,1)S(1)}, bf16[2,1040,128]{2,1,0:T(8,128)(2,1)}, u32[]{:S(2)}, u32[]{:S(2)}) collective-permute-start(bf16[2,1040,128]{2,1,0:T(8,128)(2,1)S(1)} %get-tuple-element.6), channel_id=1, source_target_pairs={{0,1},{1,2},{2,3},{4,5},{5,6},{6,7},{8,9},{9,10},{10,11},{12,13},{... | collective-permute-start | bytes 1597448 | tf_op jit(solution)/shard_map/ppermute | solution.py:134
  12.7 3.3 %collective-permute-done.3.bw1b = bf16[2,1040,128]{2,1,0:T(8,128)(2,1)S(1)} collective-permute-done((bf16[2,1040,128]{2,1,0:T(8,128)(2,1)S(1)}, bf16[2,1040,128]{2,1,0:T(8,128)(2,1)S(1)}, u32[]{:S(2)}, u32[]{:S(2)}) %collective-permute-start.3) | collective-permute-done | bytes 532512 | tf_op jit(solution)/shard_map/ppermute | solution.py:134
  16.0 0.0 copy-start.6
  16.0 0.7 collective-permute-start.7
  16.7 3.1 %collective-permute-done.1.fw1b = bf16[2,1040,128]{2,1,0:T(8,128)(2,1)S(1)} collective-permute-done((bf16[2,1040,128]{2,1,0:T(8,128)(2,1)S(1)}, bf16[2,1040,128]{2,1,0:T(8,128)(2,1)S(1)}, u32[]{:S(2)}, u32[]{:S(2)}) %collective-permute-start.1) | collective-permute-done | bytes 532512 | tf_op jit(solution)/shard_map/ppermute | solution.py:134
  19.9 0.0 copy-start.7
  19.9 1.3 %collective-permute-start.5 = (bf16[2,1040,128]{2,1,0:T(8,128)(2,1)S(1)}, bf16[2,1040,128]{2,1,0:T(8,128)(2,1)S(1)}, u32[]{:S(2)}, u32[]{:S(2)}) collective-permute-start(bf16[2,1040,128]{2,1,0:T(8,128)(2,1)S(1)} %collective-permute-done.1.fw1b), channel_id=1, source_target_pairs={{1,2},{2,3},{5,6},{6,7},{9,10},{10,11},{13,14},{14,15},{17,18},{18... | collective-permute-start | bytes 1597448 | tf_op jit(solution)/shard_map/ppermute | solution.py:134
  21.1 6.3 %collective-permute-done.2.bw1a = bf16[2,1040,128]{2,1,0:T(8,128)(2,1)} collective-permute-done((bf16[2,1040,128]{2,1,0:T(8,128)(2,1)S(1)}, bf16[2,1040,128]{2,1,0:T(8,128)(2,1)}, u32[]{:S(2)}, u32[]{:S(2)}) %collective-permute-start.2) | collective-permute-done | bytes 532512 | tf_op jit(solution)/shard_map/ppermute | solution.py:134
  27.4 0.7 collective-permute-start.6
  28.1 3.2 %collective-permute-done.fw1a = bf16[2,1040,128]{2,1,0:T(8,128)(2,1)} collective-permute-done((bf16[2,1040,128]{2,1,0:T(8,128)(2,1)S(1)}, bf16[2,1040,128]{2,1,0:T(8,128)(2,1)}, u32[]{:S(2)}, u32[]{:S(2)}) %collective-permute-start) | collective-permute-done | bytes 532512 | tf_op jit(solution)/shard_map/ppermute | solution.py:134
  31.4 1.3 %collective-permute-start.4 = (bf16[2,1040,128]{2,1,0:T(8,128)(2,1)}, bf16[2,1040,128]{2,1,0:T(8,128)(2,1)S(1)}, u32[]{:S(2)}, u32[]{:S(2)}) collective-permute-start(bf16[2,1040,128]{2,1,0:T(8,128)(2,1)} %collective-permute-done.fw1a), channel_id=1, source_target_pairs={{1,2},{2,3},{5,6},{6,7},{9,10},{10,11},{13,14},{14,15},{17,18},{18... | collective-permute-start | bytes 1597448 | tf_op jit(solution)/shard_map/ppermute | solution.py:134
  32.7 0.0 collective-permute-done.7.bw2b
  32.7 0.0 copy-start.1
  32.7 10.0 %collective-permute-done.5.fw2b = bf16[2,1040,128]{2,1,0:T(8,128)(2,1)S(1)} collective-permute-done((bf16[2,1040,128]{2,1,0:T(8,128)(2,1)S(1)}, bf16[2,1040,128]{2,1,0:T(8,128)(2,1)S(1)}, u32[]{:S(2)}, u32[]{:S(2)}) %collective-permute-start.5) | collective-permute-done | bytes 532512 | tf_op jit(solution)/shard_map/ppermute | solution.py:134
  42.7 0.0 copy-start.3
  42.7 0.1 broadcast_select_fusion
  42.7 1.3 %collective-permute-start.9 = (bf16[2,1040,128]{2,1,0:T(8,128)(2,1)S(1)}, bf16[2,1040,128]{2,1,0:T(8,128)(2,1)S(1)}, u32[]{:S(2)}, u32[]{:S(2)}) collective-permute-start(bf16[2,1040,128]{2,1,0:T(8,128)(2,1)S(1)} %broadcast_select_fusion), channel_id=1, source_target_pairs={{1,4},{2,15},{5,8},{6,3},{9,12},{10,7},{13,0},{14,11},{17,20},{18,... | collective-permute-start | bytes 1597448 | tf_op jit(solution)/shard_map/ppermute | solution.py:142
  44.1 0.0 copy-done.6
  44.1 0.0 copy-done.7
  44.1 0.0 copy-done.3
  44.1 0.0 collective-permute-done.6.bw2a
  44.1 0.0 copy-start.4
  44.1 9.9 %collective-permute-done.4.fw2a = bf16[2,1040,128]{2,1,0:T(8,128)(2,1)S(1)} collective-permute-done((bf16[2,1040,128]{2,1,0:T(8,128)(2,1)}, bf16[2,1040,128]{2,1,0:T(8,128)(2,1)S(1)}, u32[]{:S(2)}, u32[]{:S(2)}) %collective-permute-start.4) | collective-permute-done | bytes 532512 | tf_op jit(solution)/shard_map/ppermute | solution.py:134
  54.1 0.0 copy-done.1
  54.1 0.0 copy-start.2
  54.1 0.1 maximum_select_fusion
  54.2 3.4 %collective-permute-start.10 = (bf16[3,1040,128]{2,1,0:T(8,128)(2,1)S(1)}, bf16[3,1040,128]{2,1,0:T(8,128)(2,1)S(1)}, u32[]{:S(2)}, u32[]{:S(2)}) collective-permute-start(bf16[3,1040,128]{2,1,0:T(8,128)(2,1)S(1)} %maximum_select_fusion), channel_id=1, source_target_pairs={{0,4},{1,5},{2,14},{3,15},{4,8},{5,9},{6,2},{7,3},{8,12},{9,13},{1... | collective-permute-start | bytes 2396168 | tf_op jit(solution)/shard_map/ppermute | solution.py:142
  57.6 0.0 copy-done.4
  57.6 0.0 copy-done.2
  57.6 0.1 broadcast_select_fusion.1
  57.7 1.3 %collective-permute-start.8 = (bf16[2,1040,128]{2,1,0:T(8,128)(2,1)S(1)}, bf16[2,1040,128]{2,1,0:T(8,128)(2,1)S(1)}, u32[]{:S(2)}, u32[]{:S(2)}) collective-permute-start(bf16[2,1040,128]{2,1,0:T(8,128)(2,1)S(1)} %broadcast_select_fusion.1), channel_id=1, source_target_pairs={{1,4},{2,15},{5,8},{6,3},{9,12},{10,7},{13,0},{14,11},{17,20},{18,... | collective-permute-start | bytes 1597448 | tf_op jit(solution)/shard_map/ppermute | solution.py:142
  59.0 10.1 %collective-permute-done.9.endsb = bf16[2,1040,128]{2,1,0:T(8,128)(2,1)S(1)} collective-permute-done((bf16[2,1040,128]{2,1,0:T(8,128)(2,1)S(1)}, bf16[2,1040,128]{2,1,0:T(8,128)(2,1)S(1)}, u32[]{:S(2)}, u32[]{:S(2)}) %collective-permute-start.9) | collective-permute-done | bytes 532512 | tf_op jit(solution)/shard_map/ppermute | solution.py:142
  69.1 0.0 copy-start.8
  69.1 9.9 %collective-permute-done.8.endsa = bf16[2,1040,128]{2,1,0:T(8,128)(2,1)S(1)} collective-permute-done((bf16[2,1040,128]{2,1,0:T(8,128)(2,1)S(1)}, bf16[2,1040,128]{2,1,0:T(8,128)(2,1)S(1)}, u32[]{:S(2)}, u32[]{:S(2)}) %collective-permute-start.8) | collective-permute-done | bytes 532512 | tf_op jit(solution)/shard_map/ppermute | solution.py:142
  79.0 0.0 copy-start.9
  79.0 0.0 collective-permute-done.10.cross
  79.0 0.0 copy-start.5
  79.0 0.0 copy-done.8
  79.0 0.8 copy-done.9
  79.8 0.3 copy-done.5
  80.1 14.4 %shard_map.28 = bf16[4,8,128,128]{3,2,1,0:T(8,128)(2,1)} custom-call(s32[1]{0:T(128)} %bitcast.place, bf16[4,1040,128]{2,1,0:T(8,128)(2,1)} %copy-done, bf16[2,1040,128]{2,1,0:T(8,128)(2,1)} %collective-permute-done.fw1a, bf16[2,1040,128]{2,1,0:T(8,128)(2,1)} %copy-done.7, bf16[2,1040,128]{2,1,0:T(8,128)(2,1)} %collective-permute-done.2.bw1a, ...), custom_call_target="tpu_custom_call" | custom-call | tf_op jit(solution)/shard_map/pallas_call | solution.py:109
  (2 shorter events, 0.0 us)
Async XLA Ops:
  2.2 1.0 %copy-start = (bf16[4,1040,128]{2,1,0:T(8,128)(2,1)}, bf16[4,1040,128]{2,1,0:T(8,128)(2,1)S(1)}, u32[]{:S(2)}) copy-start(bf16[4,1040,128]{2,1,0:T(8,128)(2,1)S(1)} %pad_maximum_fusion.own) | copy-start | bytes 3194884
  3.2 12.8 %collective-permute-start.3 = (bf16[2,1040,128]{2,1,0:T(8,128)(2,1)S(1)}, bf16[2,1040,128]{2,1,0:T(8,128)(2,1)S(1)}, u32[]{:S(2)}, u32[]{:S(2)}) collective-permute-start(bf16[2,1040,128]{2,1,0:T(8,128)(2,1)S(1)} %get-tuple-element.5), channel_id=1, source_target_pairs={{1,0},{2,1},{3,2},{5,4},{6,5},{7,6},{9,8},{10,9},{11,10},{13,12},{... | collective-permute-start | bytes 1597448 | tf_op jit(solution)/shard_map/ppermute | solution.py:134
  5.3 14.5 %collective-permute-start.1 = (bf16[2,1040,128]{2,1,0:T(8,128)(2,1)S(1)}, bf16[2,1040,128]{2,1,0:T(8,128)(2,1)S(1)}, u32[]{:S(2)}, u32[]{:S(2)}) collective-permute-start(bf16[2,1040,128]{2,1,0:T(8,128)(2,1)S(1)} %get-tuple-element.5), channel_id=1, source_target_pairs={{0,1},{1,2},{2,3},{4,5},{5,6},{6,7},{8,9},{9,10},{10,11},{12,13},{... | collective-permute-start | bytes 1597448 | tf_op jit(solution)/shard_map/ppermute | solution.py:134
  6.6 20.8 %collective-permute-start.2 = (bf16[2,1040,128]{2,1,0:T(8,128)(2,1)S(1)}, bf16[2,1040,128]{2,1,0:T(8,128)(2,1)}, u32[]{:S(2)}, u32[]{:S(2)}) collective-permute-start(bf16[2,1040,128]{2,1,0:T(8,128)(2,1)S(1)} %get-tuple-element.6), channel_id=1, source_target_pairs={{1,0},{2,1},{3,2},{5,4},{6,5},{7,6},{9,8},{10,9},{11,10},{13,12},{... | collective-permute-start | bytes 1597448 | tf_op jit(solution)/shard_map/ppermute | solution.py:134
  11.4 20.0 %collective-permute-start = (bf16[2,1040,128]{2,1,0:T(8,128)(2,1)S(1)}, bf16[2,1040,128]{2,1,0:T(8,128)(2,1)}, u32[]{:S(2)}, u32[]{:S(2)}) collective-permute-start(bf16[2,1040,128]{2,1,0:T(8,128)(2,1)S(1)} %get-tuple-element.6), channel_id=1, source_target_pairs={{0,1},{1,2},{2,3},{4,5},{5,6},{6,7},{8,9},{9,10},{10,11},{12,13},{... | collective-permute-start | bytes 1597448 | tf_op jit(solution)/shard_map/ppermute | solution.py:134
  16.0 28.0 %copy-start.6 = (bf16[2,1040,128]{2,1,0:T(8,128)(2,1)}, bf16[2,1040,128]{2,1,0:T(8,128)(2,1)S(1)}, u32[]{:S(2)}) copy-start(bf16[2,1040,128]{2,1,0:T(8,128)(2,1)S(1)} %collective-permute-done.3.bw1b) | copy-start | bytes 1597444
  16.0 16.6 %collective-permute-start.7 = (bf16[2,1040,128]{2,1,0:T(8,128)(2,1)S(1)}, bf16[2,1040,128]{2,1,0:T(8,128)(2,1)S(1)}, u32[]{:S(2)}, u32[]{:S(2)}) collective-permute-start(bf16[2,1040,128]{2,1,0:T(8,128)(2,1)S(1)} %collective-permute-done.3.bw1b), channel_id=1, source_target_pairs={{1,0},{2,1},{5,4},{6,5},{9,8},{10,9},{13,12},{14,13},{17,16},{18,1... | collective-permute-start | bytes 1597448 | tf_op jit(solution)/shard_map/ppermute | solution.py:134
  19.9 24.2 %copy-start.7 = (bf16[2,1040,128]{2,1,0:T(8,128)(2,1)}, bf16[2,1040,128]{2,1,0:T(8,128)(2,1)S(1)}, u32[]{:S(2)}) copy-start(bf16[2,1040,128]{2,1,0:T(8,128)(2,1)S(1)} %collective-permute-done.1.fw1b) | copy-start | bytes 1597444
  19.9 22.8 %collective-permute-start.5 = (bf16[2,1040,128]{2,1,0:T(8,128)(2,1)S(1)}, bf16[2,1040,128]{2,1,0:T(8,128)(2,1)S(1)}, u32[]{:S(2)}, u32[]{:S(2)}) collective-permute-start(bf16[2,1040,128]{2,1,0:T(8,128)(2,1)S(1)} %collective-permute-done.1.fw1b), channel_id=1, source_target_pairs={{1,2},{2,3},{5,6},{6,7},{9,10},{10,11},{13,14},{14,15},{17,18},{18... | collective-permute-start | bytes 1597448 | tf_op jit(solution)/shard_map/ppermute | solution.py:134
  27.4 16.7 %collective-permute-start.6 = (bf16[2,1040,128]{2,1,0:T(8,128)(2,1)}, bf16[2,1040,128]{2,1,0:T(8,128)(2,1)S(1)}, u32[]{:S(2)}, u32[]{:S(2)}) collective-permute-start(bf16[2,1040,128]{2,1,0:T(8,128)(2,1)} %collective-permute-done.2.bw1a), channel_id=1, source_target_pairs={{1,0},{2,1},{5,4},{6,5},{9,8},{10,9},{13,12},{14,13},{17,16},{18,1... | collective-permute-start | bytes 1597448 | tf_op jit(solution)/shard_map/ppermute | solution.py:134
  31.4 22.7 %collective-permute-start.4 = (bf16[2,1040,128]{2,1,0:T(8,128)(2,1)}, bf16[2,1040,128]{2,1,0:T(8,128)(2,1)S(1)}, u32[]{:S(2)}, u32[]{:S(2)}) collective-permute-start(bf16[2,1040,128]{2,1,0:T(8,128)(2,1)} %collective-permute-done.fw1a), channel_id=1, source_target_pairs={{1,2},{2,3},{5,6},{6,7},{9,10},{10,11},{13,14},{14,15},{17,18},{18... | collective-permute-start | bytes 1597448 | tf_op jit(solution)/shard_map/ppermute | solution.py:134
  32.7 21.4 %copy-start.1 = (bf16[2,1040,128]{2,1,0:T(8,128)(2,1)}, bf16[2,1040,128]{2,1,0:T(8,128)(2,1)S(1)}, u32[]{:S(2)}) copy-start(bf16[2,1040,128]{2,1,0:T(8,128)(2,1)S(1)} %collective-permute-done.7.bw2b) | copy-start | bytes 1597444
  42.7 1.4 %copy-start.3 = (bf16[2,1040,128]{2,1,0:T(8,128)(2,1)}, bf16[2,1040,128]{2,1,0:T(8,128)(2,1)S(1)}, u32[]{:S(2)}) copy-start(bf16[2,1040,128]{2,1,0:T(8,128)(2,1)S(1)} %collective-permute-done.5.fw2b) | copy-start | bytes 1597444
  42.7 26.3 %collective-permute-start.9 = (bf16[2,1040,128]{2,1,0:T(8,128)(2,1)S(1)}, bf16[2,1040,128]{2,1,0:T(8,128)(2,1)S(1)}, u32[]{:S(2)}, u32[]{:S(2)}) collective-permute-start(bf16[2,1040,128]{2,1,0:T(8,128)(2,1)S(1)} %broadcast_select_fusion), channel_id=1, source_target_pairs={{1,4},{2,15},{5,8},{6,3},{9,12},{10,7},{13,0},{14,11},{17,20},{18,... | collective-permute-start | bytes 1597448 | tf_op jit(solution)/shard_map/ppermute | solution.py:142
  44.1 13.5 %copy-start.4 = (bf16[2,1040,128]{2,1,0:T(8,128)(2,1)}, bf16[2,1040,128]{2,1,0:T(8,128)(2,1)S(1)}, u32[]{:S(2)}) copy-start(bf16[2,1040,128]{2,1,0:T(8,128)(2,1)S(1)} %collective-permute-done.6.bw2a) | copy-start | bytes 1597444
  54.1 3.5 %copy-start.2 = (bf16[2,1040,128]{2,1,0:T(8,128)(2,1)}, bf16[2,1040,128]{2,1,0:T(8,128)(2,1)S(1)}, u32[]{:S(2)}) copy-start(bf16[2,1040,128]{2,1,0:T(8,128)(2,1)S(1)} %collective-permute-done.4.fw2a) | copy-start | bytes 1597444
  54.2 24.8 %collective-permute-start.10 = (bf16[3,1040,128]{2,1,0:T(8,128)(2,1)S(1)}, bf16[3,1040,128]{2,1,0:T(8,128)(2,1)S(1)}, u32[]{:S(2)}, u32[]{:S(2)}) collective-permute-start(bf16[3,1040,128]{2,1,0:T(8,128)(2,1)S(1)} %maximum_select_fusion), channel_id=1, source_target_pairs={{0,4},{1,5},{2,14},{3,15},{4,8},{5,9},{6,2},{7,3},{8,12},{9,13},{1... | collective-permute-start | bytes 2396168 | tf_op jit(solution)/shard_map/ppermute | solution.py:142
  57.7 21.3 %collective-permute-start.8 = (bf16[2,1040,128]{2,1,0:T(8,128)(2,1)S(1)}, bf16[2,1040,128]{2,1,0:T(8,128)(2,1)S(1)}, u32[]{:S(2)}, u32[]{:S(2)}) collective-permute-start(bf16[2,1040,128]{2,1,0:T(8,128)(2,1)S(1)} %broadcast_select_fusion.1), channel_id=1, source_target_pairs={{1,4},{2,15},{5,8},{6,3},{9,12},{10,7},{13,0},{14,11},{17,20},{18,... | collective-permute-start | bytes 1597448 | tf_op jit(solution)/shard_map/ppermute | solution.py:142
  69.1 10.0 %copy-start.8 = (bf16[2,1040,128]{2,1,0:T(8,128)(2,1)}, bf16[2,1040,128]{2,1,0:T(8,128)(2,1)S(1)}, u32[]{:S(2)}) copy-start(bf16[2,1040,128]{2,1,0:T(8,128)(2,1)S(1)} %collective-permute-done.9.endsb) | copy-start | bytes 1597444
  79.0 0.8 copy-start.9
  79.0 1.1 %copy-start.5 = (bf16[3,1040,128]{2,1,0:T(8,128)(2,1)}, bf16[3,1040,128]{2,1,0:T(8,128)(2,1)S(1)}, u32[]{:S(2)}) copy-start(bf16[3,1040,128]{2,1,0:T(8,128)(2,1)S(1)} %collective-permute-done.10.cross) | copy-start | bytes 2396164

commit v4 on v3

v4 whole, which is shorter than its diff:
```python
import functools

import jax
import jax.numpy as jnp
from jax import lax
from jax.experimental import pallas as pl
from jax.experimental.pallas import tpu as pltpu
from jax.sharding import PartitionSpec as P

B = 128
NT = (((1,), (1,)), ((), ()))
NN = (((1,), (0,)), ((), ()))


def blk(a, n=1):
    return pl.ds(a * B, n * B)


def put(x_ref, w_ref, ref, first, a, count):
    for r in range(count):
        w_ref[a + r] = ref[first + r, pl.ds(8 * B, 16)].astype(jnp.float32)
        for k in range(8):
            u = ref[first + r, blk(k)]
            set_x(x_ref, a + r, a + r + k, u)
            if 0 < k <= 18 - a - r:
                set_x(x_ref, a + r + k, a + r, u.T)


def set_x(x_ref, a, b, value):
    x_ref[a // 2, blk(a % 2), blk(b - a // 2 * 2 + 7)] = value


def square(x_ref, y_ref, w_ref, pairs):
    zero = jnp.zeros((B, B), jnp.bfloat16)
    for L in pairs:
        for J in range(L - 4, L + 1):
            d = L - J
            s = lax.dot_general(
                x_ref[J, :, blk(2 * d, 16 - 2 * d)],
                x_ref[L, :, blk(0, 16 - 2 * d)],
                NT,
                preferred_element_type=jnp.float32,
            )
            for dj in range(2):
                for dl in range(2):
                    j, l = 2 * J + dj, 2 * L + dl
                    off = abs(l - j)
                    if off > 7 or j in (0, 19) or l in (0, 19):
                        y_ref[blk(j), blk(l - 8)] = zero
                    else:
                        w = w_ref[min(j, l), pl.ds(off, 1)]
                        y_ref[blk(j), blk(l - 8)] = (
                            s[dj * B : (dj + 1) * B, dl * B : (dl + 1) * B] * w
                        ).astype(jnp.bfloat16)


def purify(x_ref, y_ref, w_ref, out):
    for I in (4, 5):
        for L in range(I, I + 5):
            d = L - I
            k0 = 2 * L - 7
            n = min(2 * L, 2 * I + 8) - k0 + 1
            c = lax.dot_general(
                x_ref[I, :, blk(2 * d, n)],
                y_ref[blk(k0, n), blk(2 * L - 8, 2)],
                NN,
                preferred_element_type=jnp.float32,
            )
            if d < 4:
                n = 8 - 2 * d
                c += lax.dot_general(
                    x_ref[I, :, blk(2 * d + 8, n)],
                    y_ref[blk(2 * L, 2), blk(2 * L - 7, n)],
                    NT,
                    preferred_element_type=jnp.float32,
                )
            for di in range(2):
                for dl in range(2):
                    i, l = 2 * I + di, 2 * L + dl
                    off = l - i
                    if 0 <= off <= 7:
                        w = w_ref[i, pl.ds(off, 1)]
                        sq = y_ref[blk(i), blk(l - 8)].astype(jnp.float32)
                        cube = w * c[di * B : (di + 1) * B, dl * B : (dl + 1) * B]
                        out[i - 8, off] = (3.0 * sq - 2.0 * cube).astype(jnp.bfloat16)


def first_kernel(z_count, place, own, fw1a, fw1b, bw1a, bw1b, fw2a, fw2b, bw2a, bw2b, ends, x_ref, y_ref, w_ref):
    zero = jnp.zeros((B, B), jnp.bfloat16)
    for c in range(16):
        set_x(x_ref, 0, c - 7, zero)
        set_x(x_ref, 19, c + 11, zero)
    for a in range(1, 19):
        set_x(x_ref, a, a + 8 if a % 2 == 0 else a - 8, zero)
    z = place[0]
    last = z_count - 1
    take = functools.partial(put, x_ref, w_ref)
    take(own, 0, 8, 4)
    for here, ref, first, a, count in (
        (z == 0, ends, 0, 6, 2),
        (z > 0, fw1b, 0, 6, 2),
        (z > 0, fw1a, 0, 4, 2),
        (z == last, ends, 0, 12, 2),
        (z < last, bw1a, 0, 12, 2),
        (z < last, bw1b, 0, 14, 2),
        (z > 1, fw2a, 1, 1, 1),
        (z > 1, fw2b, 0, 2, 2),
        (z < last - 1, bw2a, 0, 16, 2),
        (z < last - 1, bw2b, 0, 18, 1),
    ):
        pl.when(here)(functools.partial(take, ref, first, a, count))
    low = z < z_count // 2
    pl.when(low)(functools.partial(square, x_ref, y_ref, w_ref, (7, 8, 9)))
    pl.when(jnp.logical_not(low))(functools.partial(square, x_ref, y_ref, w_ref, (4, 5, 6)))


def second_kernel(z_count, place, x_in, y_in, w_in, ends, cross, out, x_ref, y_ref, w_ref):
    z = place[0]
    last = z_count - 1
    take = functools.partial(put, x_ref, w_ref)
    for here, ref, first, a, count in (
        (z == 0, ends, 0, 4, 2),
        (z == last, ends, 0, 14, 2),
        (z <= 1, cross, 0, 1, 3),
        (z >= last - 1, cross, 0, 16, 3),
    ):
        pl.when(here)(functools.partial(take, ref, first, a, count))
    low = z < z_count // 2
    pl.when(low)(functools.partial(square, x_ref, y_ref, w_ref, (4, 5, 6)))
    pl.when(jnp.logical_not(low))(functools.partial(square, x_ref, y_ref, w_ref, (7, 8, 9)))
    purify(x_ref, y_ref, w_ref, out)


SMEM = pl.BlockSpec(memory_space=pltpu.SMEM)
VMEM = pl.BlockSpec(memory_space=pltpu.VMEM)
KEPT = [
    pltpu.VMEM((10, 2 * B, 16 * B), jnp.bfloat16),
    pltpu.VMEM((20 * B, 12 * B), jnp.bfloat16),
    pltpu.VMEM((20, 16, B), jnp.float32),
]


def compute(z_count, place, early, late):
    kept = pl.pallas_call(
        functools.partial(first_kernel, z_count),
        out_shape=KEPT,
        in_specs=[SMEM] + [VMEM] * len(early),
        out_specs=[VMEM] * 3,
        compiler_params=pltpu.CompilerParams(vmem_limit_bytes=24 * 1024 * 1024),
        cost_estimate=pl.CostEstimate(flops=6 * 10**9, bytes_accessed=6 * 10**6, transcendentals=0),
    )(place, *early)
    return pl.pallas_call(
        functools.partial(second_kernel, z_count),
        out_shape=[jax.ShapeDtypeStruct((4, 8, B, B), jnp.bfloat16)] + KEPT,
        in_specs=[SMEM] + [VMEM] * (3 + len(late)),
        out_specs=[VMEM] * 4,
        input_output_aliases={1: 1, 2: 2, 3: 3},
        compiler_params=pltpu.CompilerParams(vmem_limit_bytes=24 * 1024 * 1024),
        cost_estimate=pl.CostEstimate(flops=6 * 10**9, bytes_accessed=4 * 10**6, transcendentals=0),
    )(place, *kept, *late)[0]


def per_device(upper, present):
    s_count, z_count = lax.axis_size("row"), lax.axis_size("col")
    z = lax.axis_index("col")
    rows, wide = present.shape
    weights = present.astype(jnp.bfloat16)[:, :, None, None]
    blocks = (upper * weights).reshape(rows, wide * B, B)
    pattern = jnp.broadcast_to(weights[:, :, 0], (rows, wide, B))
    masked = jnp.concatenate([blocks, pattern, pattern], axis=1)

    def step(block, d, pairs=None):
        pairs = pairs or [(i, i + d) for i in range(z_count) if 0 <= i + d < z_count]
        return lax.ppermute(block, "col", pairs)

    def hop(block, route):
        pairs = [
            (i * z_count + a, (i + d) % s_count * z_count + b)
            for i in range(s_count)
            for a, d, b in route
        ]
        return lax.ppermute(block, ("row", "col"), pairs)

    last = z_count - 1
    inner = range(1, last)
    parts = [masked[: rows // 2], masked[rows // 2 :]]
    fw1 = [step(part, 1) for part in parts]
    bw1 = [step(part, -1) for part in parts]
    fw2 = [step(part, 1, [(i, i + 1) for i in inner]) for part in fw1]
    bw2 = [step(part, -1, [(i, i - 1) for i in inner]) for part in bw1]
    if z_count == 4:
        route = [(1, 1, 0), (2, -1, 3)]
        ends_first = hop(jnp.where(z < 2, bw2[1], fw2[0]), route)
        ends_last = hop(jnp.where(z < 2, bw2[0], fw2[1]), route)
        route = [(0, 1, 0), (1, 1, 1), (2, -1, 2), (3, -1, 3)]
        below = jnp.concatenate([bw2[0][1:], bw2[1]])
        above = jnp.concatenate([fw2[0], fw2[1][:1]])
        cross = hop(jnp.where(z < 2, below, above), route)
    else:
        route = [(last, 1, 0), (0, -1, last)]
        ends_first = hop(jnp.where(z == last, parts[1], parts[0]), route)
        ends_last = hop(jnp.where(z == last, parts[0], parts[1]), route)
        route = [(last - 1, 1, 0), (last, 1, 1), (0, -1, last - 1), (1, -1, last)]
        cross = hop(jnp.where(z < 2, masked[:3], masked[1:]), route)
    early = (masked, *fw1, *bw1, *fw2, *bw2, ends_first)
    return compute(z_count, z.reshape(1), early, (ends_last, cross))


def solution(mesh):
    return jax.shard_map(
        per_device,
        mesh=mesh,
        in_specs=(P(("groups", "row", "col"), None, None, None), P(("groups", "row", "col"), None)),
        out_specs=P(("groups", "row", "col"), None, None, None),
        check_vma=False,
    )
```

time: 94.9 us -> 86.5 us (0.911)
  waiting for transfers between devices: 56 us -> 48.8 us
  local copies, waits for them, and re-layouts: 2.23 us -> 0.18 us
  starting transfers between devices: 19.4 us -> 20.8 us
    ppermute x3, waiting for transfers between devices: 20 us -> 13.5 us  [hop(): return lax.ppermute(block, ('row', 'col'), pairs)]
    unnamed x20 -> x0, local copies, waits for them, and re-layouts: 2.04 us -> none
    ppermute x8, starting transfers between devices: 13.4 us -> 14.9 us  [step(): return lax.ppermute(block, 'col', pairs)]
    pallas_call x1 -> x2, Pallas kernels: 14.4 us -> 13.7 us  [the longest x1 7.25 us: compute(): pl.pallas_call(functools.partial(second_kernel, z_count), out_shape=[jax....]
  transfers between devices with their start and end apart: 11 -> 11, of which waited for: 8 -> 7; matrix products, arithmetic and copies ran while one was open for 0% -> 0% of each run, Pallas kernels for 0% -> 8%
where the time goes in v4:
time: 86.5 us; the launch traced here: 86.1 us
  waiting for transfers between devices  48.8 us (56%)
  starting transfers between devices  20.8 us (24%)
  Pallas kernels  13.7 us (16%)
  other arithmetic  2.39 us (3%)
    ppermute x8, waiting for transfers between devices, step(): return lax.ppermute(block, 'col', pairs)  35.4 us
    ppermute x8, starting transfers between devices, step(): return lax.ppermute(block, 'col', pairs)  14.9 us
    ppermute x3, waiting for transfers between devices, hop(): return lax.ppermute(block, ('row', 'col'), pairs)  13.5 us
    pallas_call x1, Pallas kernels, compute(): pl.pallas_call(functools.partial(second_kernel, z_count), out_shape=[jax....  7.25 us
    pallas_call x1, Pallas kernels, compute(): pl.pallas_call(functools.partial(first_kernel, z_count), out_shape=KEPT,...  6.49 us
    ppermute x3, starting transfers between devices, hop(): return lax.ppermute(block, ('row', 'col'), pairs)  5.97 us
  transfers between devices with their start and end apart: 11, of which 7 were waited for; matrix products, arithmetic and copies ran while one was open for 0% of the time, Pallas kernels for 8%

profile of v4, /device:TPU:25, one launch (start us, length us, event | category | flops | bytes accessed | tf_op | source)
XLA Modules:
  0.0 86.1 jit_solution(4753666941244191682)
XLA Ops:
  0.0 0.7 convert_element_type.3
  0.7 1.4 %broadcast_multiply_fusion = bf16[4,8,128,128]{3,2,1,0:T(8,128)(2,1)S(1)} fusion(bf16[4,8,128,128]{3,2,1,0:T(8,128)(2,1)} %param.2, bf16[4,8]{1,0:T(4,128)(2,1)S(1)} %convert_element_type.3), kind=kLoop, calls=%fused_computation.4 | loop fusion | flops 524288 | bytes 2097216 | tf_op jit(solution)/shard_map/mul | solution.py:168
  2.1 0.1 broadcast_in_dim.2
  2.1 0.1 pad_maximum_fusion.own
  2.2 0.1 fusion
  2.3 2.9 %collective-permute-start.3 = (bf16[2,1040,128]{2,1,0:T(8,128)(2,1)S(1)}, bf16[2,1040,128]{2,1,0:T(8,128)(2,1)}, u32[]{:S(2)}, u32[]{:S(2)}) collective-permute-start(bf16[2,1040,128]{2,1,0:T(8,128)(2,1)S(1)} %get-tuple-element.13), channel_id=1, source_target_pairs={{1,0},{2,1},{3,2},{5,4},{6,5},{7,6},{9,8},{10,9},{11,10},{13,12},{... | collective-permute-start | bytes 1597448 | tf_op jit(solution)/shard_map/ppermute | solution.py:174
  5.2 1.3 %collective-permute-start = (bf16[2,1040,128]{2,1,0:T(8,128)(2,1)S(1)}, bf16[2,1040,128]{2,1,0:T(8,128)(2,1)}, u32[]{:S(2)}, u32[]{:S(2)}) collective-permute-start(bf16[2,1040,128]{2,1,0:T(8,128)(2,1)S(1)} %get-tuple-element.14), channel_id=1, source_target_pairs={{0,1},{1,2},{2,3},{4,5},{5,6},{6,7},{8,9},{9,10},{10,11},{12,13},{... | collective-permute-start | bytes 1597448 | tf_op jit(solution)/shard_map/ppermute | solution.py:174
  6.5 1.3 %collective-permute-start.1 = (bf16[2,1040,128]{2,1,0:T(8,128)(2,1)S(1)}, bf16[2,1040,128]{2,1,0:T(8,128)(2,1)}, u32[]{:S(2)}, u32[]{:S(2)}) collective-permute-start(bf16[2,1040,128]{2,1,0:T(8,128)(2,1)S(1)} %get-tuple-element.13), channel_id=1, source_target_pairs={{0,1},{1,2},{2,3},{4,5},{5,6},{6,7},{8,9},{9,10},{10,11},{12,13},{... | collective-permute-start | bytes 1597448 | tf_op jit(solution)/shard_map/ppermute | solution.py:174
  7.8 5.5 %collective-permute-start.2 = (bf16[2,1040,128]{2,1,0:T(8,128)(2,1)S(1)}, bf16[2,1040,128]{2,1,0:T(8,128)(2,1)}, u32[]{:S(2)}, u32[]{:S(2)}) collective-permute-start(bf16[2,1040,128]{2,1,0:T(8,128)(2,1)S(1)} %get-tuple-element.14), channel_id=1, source_target_pairs={{1,0},{2,1},{3,2},{5,4},{6,5},{7,6},{9,8},{10,9},{11,10},{13,12},{... | collective-permute-start | bytes 1597448 | tf_op jit(solution)/shard_map/ppermute | solution.py:174
  13.2 1.9 %collective-permute-done.3.bw1b = bf16[2,1040,128]{2,1,0:T(8,128)(2,1)} collective-permute-done((bf16[2,1040,128]{2,1,0:T(8,128)(2,1)S(1)}, bf16[2,1040,128]{2,1,0:T(8,128)(2,1)}, u32[]{:S(2)}, u32[]{:S(2)}) %collective-permute-start.3) | collective-permute-done | bytes 532512 | tf_op jit(solution)/shard_map/ppermute | solution.py:174
  15.1 0.7 collective-permute-start.7
  15.8 4.0 %collective-permute-done.fw1a = bf16[2,1040,128]{2,1,0:T(8,128)(2,1)} collective-permute-done((bf16[2,1040,128]{2,1,0:T(8,128)(2,1)S(1)}, bf16[2,1040,128]{2,1,0:T(8,128)(2,1)}, u32[]{:S(2)}, u32[]{:S(2)}) %collective-permute-start) | collective-permute-done | bytes 532512 | tf_op jit(solution)/shard_map/ppermute | solution.py:174
  19.8 1.3 %collective-permute-start.4 = (bf16[2,1040,128]{2,1,0:T(8,128)(2,1)}, bf16[2,1040,128]{2,1,0:T(8,128)(2,1)S(1)}, u32[]{:S(2)}, u32[]{:S(2)}) collective-permute-start(bf16[2,1040,128]{2,1,0:T(8,128)(2,1)} %collective-permute-done.fw1a), channel_id=1, source_target_pairs={{1,2},{2,3},{5,6},{6,7},{9,10},{10,11},{13,14},{14,15},{17,18},{18... | collective-permute-start | bytes 1597448 | tf_op jit(solution)/shard_map/ppermute | solution.py:174
  21.1 10.1 %collective-permute-done.1.fw1b = bf16[2,1040,128]{2,1,0:T(8,128)(2,1)} collective-permute-done((bf16[2,1040,128]{2,1,0:T(8,128)(2,1)S(1)}, bf16[2,1040,128]{2,1,0:T(8,128)(2,1)}, u32[]{:S(2)}, u32[]{:S(2)}) %collective-permute-start.1) | collective-permute-done | bytes 532512 | tf_op jit(solution)/shard_map/ppermute | solution.py:174
  31.2 1.3 %collective-permute-start.5 = (bf16[2,1040,128]{2,1,0:T(8,128)(2,1)}, bf16[2,1040,128]{2,1,0:T(8,128)(2,1)S(1)}, u32[]{:S(2)}, u32[]{:S(2)}) collective-permute-start(bf16[2,1040,128]{2,1,0:T(8,128)(2,1)} %collective-permute-done.1.fw1b), channel_id=1, source_target_pairs={{1,2},{2,3},{5,6},{6,7},{9,10},{10,11},{13,14},{14,15},{17,18},{18... | collective-permute-start | bytes 1597448 | tf_op jit(solution)/shard_map/ppermute | solution.py:174
  32.5 0.0 collective-permute-done.2.bw1a
  32.5 0.7 collective-permute-start.6
  33.2 0.0 collective-permute-done.7.bw2b
  33.3 9.3 %collective-permute-done.4.fw2a = bf16[2,1040,128]{2,1,0:T(8,128)(2,1)S(1)} collective-permute-done((bf16[2,1040,128]{2,1,0:T(8,128)(2,1)}, bf16[2,1040,128]{2,1,0:T(8,128)(2,1)S(1)}, u32[]{:S(2)}, u32[]{:S(2)}) %collective-permute-start.4) | collective-permute-done | bytes 532512 | tf_op jit(solution)/shard_map/ppermute | solution.py:174
  42.5 0.1 broadcast_select_fusion.1
  42.6 1.3 %collective-permute-start.8 = (bf16[2,1040,128]{2,1,0:T(8,128)(2,1)S(1)}, bf16[2,1040,128]{2,1,0:T(8,128)(2,1)S(1)}, u32[]{:S(2)}, u32[]{:S(2)}) collective-permute-start(bf16[2,1040,128]{2,1,0:T(8,128)(2,1)S(1)} %broadcast_select_fusion.1), channel_id=1, source_target_pairs={{1,4},{2,15},{5,8},{6,3},{9,12},{10,7},{13,0},{14,11},{17,20},{18,... | collective-permute-start | bytes 1597448 | tf_op jit(solution)/shard_map/ppermute | solution.py:182
  43.9 10.0 %collective-permute-done.5.fw2b = bf16[2,1040,128]{2,1,0:T(8,128)(2,1)S(1)} collective-permute-done((bf16[2,1040,128]{2,1,0:T(8,128)(2,1)}, bf16[2,1040,128]{2,1,0:T(8,128)(2,1)S(1)}, u32[]{:S(2)}, u32[]{:S(2)}) %collective-permute-start.5) | collective-permute-done | bytes 532512 | tf_op jit(solution)/shard_map/ppermute | solution.py:174
  54.0 0.0 collective-permute-done.6.bw2a
  54.0 0.1 maximum_select_fusion
  54.2 3.4 %collective-permute-start.10 = (bf16[3,1040,128]{2,1,0:T(8,128)(2,1)S(1)}, bf16[3,1040,128]{2,1,0:T(8,128)(2,1)S(1)}, u32[]{:S(2)}, u32[]{:S(2)}) collective-permute-start(bf16[3,1040,128]{2,1,0:T(8,128)(2,1)S(1)} %maximum_select_fusion), channel_id=1, source_target_pairs={{0,4},{1,5},{2,14},{3,15},{4,8},{5,9},{6,2},{7,3},{8,12},{9,13},{1... | collective-permute-start | bytes 2396168 | tf_op jit(solution)/shard_map/ppermute | solution.py:182
  57.5 0.1 broadcast_select_fusion
  57.6 1.3 %collective-permute-start.9 = (bf16[2,1040,128]{2,1,0:T(8,128)(2,1)S(1)}, bf16[2,1040,128]{2,1,0:T(8,128)(2,1)S(1)}, u32[]{:S(2)}, u32[]{:S(2)}) collective-permute-start(bf16[2,1040,128]{2,1,0:T(8,128)(2,1)S(1)} %broadcast_select_fusion), channel_id=1, source_target_pairs={{1,4},{2,15},{5,8},{6,3},{9,12},{10,7},{13,0},{14,11},{17,20},{18,... | collective-permute-start | bytes 1597448 | tf_op jit(solution)/shard_map/ppermute | solution.py:182
  58.9 10.0 %collective-permute-done.8.ends = bf16[2,1040,128]{2,1,0:T(8,128)(2,1)S(1)} collective-permute-done((bf16[2,1040,128]{2,1,0:T(8,128)(2,1)S(1)}, bf16[2,1040,128]{2,1,0:T(8,128)(2,1)S(1)}, u32[]{:S(2)}, u32[]{:S(2)}) %collective-permute-start.8) | collective-permute-done | bytes 532512 | tf_op jit(solution)/shard_map/ppermute | solution.py:182
  68.9 6.5 %shard_map.28 = (bf16[10,256,2048]{2,1,0:T(8,128)(2,1)S(1)}, bf16[2560,1536]{1,0:T(8,128)(2,1)S(1)}, f32[20,16,128]{2,1,0:T(8,128)S(1)}) custom-call(s32[1]{0:T(128)} %bitcast.place, bf16[4,1040,128]{2,1,0:T(8,128)(2,1)S(1)} %pad_maximum_fusion.own, bf16[2,1040,128]{2,1,0:T(8,128)(2,1)} %collective-permute-done.fw1a, ...), custom_call_target="tpu_custom_call" | custom-call | flops 6000000000 | bytes 6000000 | tf_op jit(solution)/shard_map/pallas_call | solution.py:144
  75.4 3.4 %collective-permute-done.9.ends = bf16[2,1040,128]{2,1,0:T(8,128)(2,1)S(1)} collective-permute-done((bf16[2,1040,128]{2,1,0:T(8,128)(2,1)S(1)}, bf16[2,1040,128]{2,1,0:T(8,128)(2,1)S(1)}, u32[]{:S(2)}, u32[]{:S(2)}) %collective-permute-start.9) | collective-permute-done | bytes 532512 | tf_op jit(solution)/shard_map/ppermute | solution.py:182
  78.9 0.0 collective-permute-done.10.cross
  78.9 7.2 %shard_map.29 = (bf16[4,8,128,128]{3,2,1,0:T(8,128)(2,1)}, bf16[10,256,2048]{2,1,0:T(8,128)(2,1)S(1)}, bf16[2560,1536]{1,0:T(8,128)(2,1)S(1)}, f32[20,16,128]{2,1,0:T(8,128)S(1)}) custom-call(s32[1]{0:T(128)} %bitcast.place, bf16[10,256,2048]{2,1,0:T(8,128)(2,1)S(1)} %get-tuple-element.9.x_in, ...), custom_call_target="tpu_custom_call", output_to_operand_aliasing={{1}: (1, {}), {2}: (2, {}), {3}: (3, {})} | custom-call | flops 6000000000 | bytes 4000000 | tf_op jit(solution)/shard_map/pallas_call | solution.py:152
  (2 shorter events, 0.0 us)
Async XLA Ops:
  2.3 12.8 %collective-permute-start.3 = (bf16[2,1040,128]{2,1,0:T(8,128)(2,1)S(1)}, bf16[2,1040,128]{2,1,0:T(8,128)(2,1)}, u32[]{:S(2)}, u32[]{:S(2)}) collective-permute-start(bf16[2,1040,128]{2,1,0:T(8,128)(2,1)S(1)} %get-tuple-element.13), channel_id=1, source_target_pairs={{1,0},{2,1},{3,2},{5,4},{6,5},{7,6},{9,8},{10,9},{11,10},{13,12},{... | collective-permute-start | bytes 1597448 | tf_op jit(solution)/shard_map/ppermute | solution.py:174
  5.2 14.6 %collective-permute-start = (bf16[2,1040,128]{2,1,0:T(8,128)(2,1)S(1)}, bf16[2,1040,128]{2,1,0:T(8,128)(2,1)}, u32[]{:S(2)}, u32[]{:S(2)}) collective-permute-start(bf16[2,1040,128]{2,1,0:T(8,128)(2,1)S(1)} %get-tuple-element.14), channel_id=1, source_target_pairs={{0,1},{1,2},{2,3},{4,5},{5,6},{6,7},{8,9},{9,10},{10,11},{12,13},{... | collective-permute-start | bytes 1597448 | tf_op jit(solution)/shard_map/ppermute | solution.py:174
  6.5 24.8 %collective-permute-start.1 = (bf16[2,1040,128]{2,1,0:T(8,128)(2,1)S(1)}, bf16[2,1040,128]{2,1,0:T(8,128)(2,1)}, u32[]{:S(2)}, u32[]{:S(2)}) collective-permute-start(bf16[2,1040,128]{2,1,0:T(8,128)(2,1)S(1)} %get-tuple-element.13), channel_id=1, source_target_pairs={{0,1},{1,2},{2,3},{4,5},{5,6},{6,7},{8,9},{9,10},{10,11},{12,13},{... | collective-permute-start | bytes 1597448 | tf_op jit(solution)/shard_map/ppermute | solution.py:174
  7.8 24.8 %collective-permute-start.2 = (bf16[2,1040,128]{2,1,0:T(8,128)(2,1)S(1)}, bf16[2,1040,128]{2,1,0:T(8,128)(2,1)}, u32[]{:S(2)}, u32[]{:S(2)}) collective-permute-start(bf16[2,1040,128]{2,1,0:T(8,128)(2,1)S(1)} %get-tuple-element.14), channel_id=1, source_target_pairs={{1,0},{2,1},{3,2},{5,4},{6,5},{7,6},{9,8},{10,9},{11,10},{13,12},{... | collective-permute-start | bytes 1597448 | tf_op jit(solution)/shard_map/ppermute | solution.py:174
  15.1 18.1 %collective-permute-start.7 = (bf16[2,1040,128]{2,1,0:T(8,128)(2,1)}, bf16[2,1040,128]{2,1,0:T(8,128)(2,1)S(1)}, u32[]{:S(2)}, u32[]{:S(2)}) collective-permute-start(bf16[2,1040,128]{2,1,0:T(8,128)(2,1)} %collective-permute-done.3.bw1b), channel_id=1, source_target_pairs={{1,0},{2,1},{5,4},{6,5},{9,8},{10,9},{13,12},{14,13},{17,16},{18,1... | collective-permute-start | bytes 1597448 | tf_op jit(solution)/shard_map/ppermute | solution.py:174
  19.8 22.7 %collective-permute-start.4 = (bf16[2,1040,128]{2,1,0:T(8,128)(2,1)}, bf16[2,1040,128]{2,1,0:T(8,128)(2,1)S(1)}, u32[]{:S(2)}, u32[]{:S(2)}) collective-permute-start(bf16[2,1040,128]{2,1,0:T(8,128)(2,1)} %collective-permute-done.fw1a), channel_id=1, source_target_pairs={{1,2},{2,3},{5,6},{6,7},{9,10},{10,11},{13,14},{14,15},{17,18},{18... | collective-permute-start | bytes 1597448 | tf_op jit(solution)/shard_map/ppermute | solution.py:174
  31.2 22.7 %collective-permute-start.5 = (bf16[2,1040,128]{2,1,0:T(8,128)(2,1)}, bf16[2,1040,128]{2,1,0:T(8,128)(2,1)S(1)}, u32[]{:S(2)}, u32[]{:S(2)}) collective-permute-start(bf16[2,1040,128]{2,1,0:T(8,128)(2,1)} %collective-permute-done.1.fw1b), channel_id=1, source_target_pairs={{1,2},{2,3},{5,6},{6,7},{9,10},{10,11},{13,14},{14,15},{17,18},{18... | collective-permute-start | bytes 1597448 | tf_op jit(solution)/shard_map/ppermute | solution.py:174
  32.5 21.4 %collective-permute-start.6 = (bf16[2,1040,128]{2,1,0:T(8,128)(2,1)}, bf16[2,1040,128]{2,1,0:T(8,128)(2,1)S(1)}, u32[]{:S(2)}, u32[]{:S(2)}) collective-permute-start(bf16[2,1040,128]{2,1,0:T(8,128)(2,1)} %collective-permute-done.2.bw1a), channel_id=1, source_target_pairs={{1,0},{2,1},{5,4},{6,5},{9,8},{10,9},{13,12},{14,13},{17,16},{18,1... | collective-permute-start | bytes 1597448 | tf_op jit(solution)/shard_map/ppermute | solution.py:174
  42.6 26.3 %collective-permute-start.8 = (bf16[2,1040,128]{2,1,0:T(8,128)(2,1)S(1)}, bf16[2,1040,128]{2,1,0:T(8,128)(2,1)S(1)}, u32[]{:S(2)}, u32[]{:S(2)}) collective-permute-start(bf16[2,1040,128]{2,1,0:T(8,128)(2,1)S(1)} %broadcast_select_fusion.1), channel_id=1, source_target_pairs={{1,4},{2,15},{5,8},{6,3},{9,12},{10,7},{13,0},{14,11},{17,20},{18,... | collective-permute-start | bytes 1597448 | tf_op jit(solution)/shard_map/ppermute | solution.py:182
  54.2 24.7 %collective-permute-start.10 = (bf16[3,1040,128]{2,1,0:T(8,128)(2,1)S(1)}, bf16[3,1040,128]{2,1,0:T(8,128)(2,1)S(1)}, u32[]{:S(2)}, u32[]{:S(2)}) collective-permute-start(bf16[3,1040,128]{2,1,0:T(8,128)(2,1)S(1)} %maximum_select_fusion), channel_id=1, source_target_pairs={{0,4},{1,5},{2,14},{3,15},{4,8},{5,9},{6,2},{7,3},{8,12},{9,13},{1... | collective-permute-start | bytes 2396168 | tf_op jit(solution)/shard_map/ppermute | solution.py:182
  57.6 21.3 %collective-permute-start.9 = (bf16[2,1040,128]{2,1,0:T(8,128)(2,1)S(1)}, bf16[2,1040,128]{2,1,0:T(8,128)(2,1)S(1)}, u32[]{:S(2)}, u32[]{:S(2)}) collective-permute-start(bf16[2,1040,128]{2,1,0:T(8,128)(2,1)S(1)} %broadcast_select_fusion), channel_id=1, source_target_pairs={{1,4},{2,15},{5,8},{6,3},{9,12},{10,7},{13,0},{14,11},{17,20},{18,... | collective-permute-start | bytes 1597448 | tf_op jit(solution)/shard_map/ppermute | solution.py:182

commit v5 on v4

--- a/solution.py
+++ b/solution.py
@@ -16,13 +16,55 @@
     return pl.ds(a * B, n * B)
 
 
-def put(x_ref, w_ref, ref, first, a, count):
-    for r in range(count):
-        w_ref[a + r] = ref[first + r, pl.ds(8 * B, 16)].astype(jnp.float32)
-        for k in range(8):
-            u = ref[first + r, blk(k)]
+def triangles():
+    p = lax.broadcasted_iota(jnp.int32, (B, B), 0)
+    q = lax.broadcasted_iota(jnp.int32, (B, B), 1)
+    return p, q
+
+
+def pack(present, upper, _, *outs):
+    p, q = triangles()
+    right = lax.broadcasted_iota(jnp.int32, (1, B), 1) >= B // 2
+
+    def block(r, k):
+        w = present[r, k].astype(jnp.float32)
+        return upper[r, k].astype(jnp.float32) * w
+
+    for first, out in zip((0, 2), outs):
+        one, two = block(first, 0), block(first + 1, 0)
+        out[blk(0)] = jnp.where(p <= q, one, two).astype(jnp.bfloat16)
+        for r in range(2):
+            for k in range(1, 8):
+                out[blk(7 * r + k)] = block(first + r, k).astype(jnp.bfloat16)
+        lines = [
+            jnp.where(
+                right,
+                present[first + 1, k].astype(jnp.float32),
+                present[first, k].astype(jnp.float32),
+            )
+            for k in range(8)
+        ]
+        lines.append(jnp.sum(jnp.where(p == q, two, 0.0), axis=0, keepdims=True))
+        lines.append(jnp.zeros((7, B), jnp.float32))
+        out[pl.ds(15 * B, 16)] = jnp.concatenate(lines, axis=0).astype(jnp.bfloat16)
+
+
+def put(x_ref, w_ref, ref, a, rows=(0, 1)):
+    p, q = triangles()
+    mixed = ref[blk(0)].astype(jnp.float32)
+    turned = mixed.T
+    tail = ref[pl.ds(15 * B, 16)].astype(jnp.float32)
+    for r in rows:
+        w_ref[a + r] = jnp.broadcast_to(tail[:8, r * B // 2 : r * B // 2 + 1], (8, B))
+        if r == 0:
+            diagonal = jnp.where(p <= q, mixed, turned)
+        else:
+            diagonal = jnp.where(p > q, mixed, jnp.where(p < q, turned, tail[8:9]))
+        set_x(x_ref, a + r, a + r, diagonal.astype(jnp.bfloat16))
+        for k in range(1, 8):
+            u = ref[blk(7 * r + k)]
             set_x(x_ref, a + r, a + r + k, u)
-            if 0 < k <= 18 - a - r:
+            if k <= 18 - a - r:
                 set_x(x_ref, a + r + k, a + r, u.T)
 
 
@@ -85,7 +127,7 @@
                         out[i - 8, off] = (3.0 * sq - 2.0 * cube).astype(jnp.bfloat16)
 
 
-def first_kernel(z_count, place, own, fw1a, fw1b, bw1a, bw1b, fw2a, fw2b, bw2a, bw2b, ends, x_ref, y_ref, w_ref):
+def first_kernel(z_count, place, owna, ownb, fw1a, fw1b, bw1a, bw1b, fw2a, fw2b, bw2a, bw2b, ends, x_ref, y_ref, w_ref):
     zero = jnp.zeros((B, B), jnp.bfloat16)
     for c in range(16):
         set_x(x_ref, 0, c - 7, zero)
@@ -95,36 +137,39 @@
     z = place[0]
     last = z_count - 1
     take = functools.partial(put, x_ref, w_ref)
-    take(own, 0, 8, 4)
-    for here, ref, first, a, count in (
-        (z == 0, ends, 0, 6, 2),
-        (z > 0, fw1b, 0, 6, 2),
-        (z > 0, fw1a, 0, 4, 2),
-        (z == last, ends, 0, 12, 2),
-        (z < last, bw1a, 0, 12, 2),
-        (z < last, bw1b, 0, 14, 2),
-        (z > 1, fw2a, 1, 1, 1),
-        (z > 1, fw2b, 0, 2, 2),
-        (z < last - 1, bw2a, 0, 16, 2),
-        (z < last - 1, bw2b, 0, 18, 1),
+    take(owna, 8)
+    take(ownb, 10)
+    for here, ref, a, rows in (
+        (z == 0, ends, 6, (0, 1)),
+        (z > 0, fw1b, 6, (0, 1)),
+        (z > 0, fw1a, 4, (0, 1)),
+        (z == last, ends, 12, (0, 1)),
+        (z < last, bw1a, 12, (0, 1)),
+        (z < last, bw1b, 14, (0, 1)),
+        (z > 1, fw2a, 0, (1,)),
+        (z > 1, fw2b, 2, (0, 1)),
+        (z < last - 1, bw2a, 16, (0, 1)),
+        (z < last - 1, bw2b, 18, (0,)),
     ):
-        pl.when(here)(functools.partial(take, ref, first, a, count))
+        pl.when(here)(functools.partial(take, ref, a, rows))
     low = z < z_count // 2
     pl.when(low)(functools.partial(square, x_ref, y_ref, w_ref, (7, 8, 9)))
     pl.when(jnp.logical_not(low))(functools.partial(square, x_ref, y_ref, w_ref, (4, 5, 6)))
 
 
-def second_kernel(z_count, place, x_in, y_in, w_in, ends, cross, out, x_ref, y_ref, w_ref):
+def second_kernel(z_count, place, x_in, y_in, w_in, ends, cross_first, cross_last, out, x_ref, y_ref, w_ref):
     z = place[0]
     last = z_count - 1
     take = functools.partial(put, x_ref, w_ref)
-    for here, ref, first, a, count in (
-        (z == 0, ends, 0, 4, 2),
-        (z == last, ends, 0, 14, 2),
-        (z <= 1, cross, 0, 1, 3),
-        (z >= last - 1, cross, 0, 16, 3),
+    for here, ref, a, rows in (
+        (z == 0, ends, 4, (0, 1)),
+        (z == last, ends, 14, (0, 1)),
+        (z <= 1, cross_first, 2, (0, 1)),
+        (z <= 1, cross_last, 0, (1,)),
+        (z >= last - 1, cross_first, 16, (0, 1)),
+        (z >= last - 1, cross_last, 18, (0,)),
     ):
-        pl.when(here)(functools.partial(take, ref, first, a, count))
+        pl.when(here)(functools.partial(take, ref, a, rows))
     low = z < z_count // 2
     pl.when(low)(functools.partial(square, x_ref, y_ref, w_ref, (4, 5, 6)))
     pl.when(jnp.logical_not(low))(functools.partial(square, x_ref, y_ref, w_ref, (7, 8, 9)))
@@ -136,7 +181,7 @@
 KEPT = [
     pltpu.VMEM((10, 2 * B, 16 * B), jnp.bfloat16),
     pltpu.VMEM((20 * B, 12 * B), jnp.bfloat16),
-    pltpu.VMEM((20, 16, B), jnp.float32),
+    pltpu.VMEM((20, 8, B), jnp.float32),
 ]
 
 
@@ -160,15 +205,21 @@
     )(place, *kept, *late)[0]
 
 
+def packed(present, upper, before):
+    rows = upper.shape[2]
+    pair = jax.ShapeDtypeStruct((15 * rows + 16, rows), jnp.bfloat16)
+    return pl.pallas_call(
+        pack,
+        out_shape=[pair, pair],
+        in_specs=[SMEM, VMEM, pl.BlockSpec(memory_space=pl.ANY)],
+        out_specs=[VMEM, VMEM],
+        compiler_params=pltpu.CompilerParams(vmem_limit_bytes=8 * 1024 * 1024),
+    )(present, upper, before)
+
+
 def per_device(upper, present):
     s_count, z_count = lax.axis_size("row"), lax.axis_size("col")
     z = lax.axis_index("col")
-    rows, wide = present.shape
-    weights = present.astype(jnp.bfloat16)[:, :, None, None]
-    blocks = (upper * weights).reshape(rows, wide * B, B)
-    pattern = jnp.broadcast_to(weights[:, :, 0], (rows, wide, B))
-    masked = jnp.concatenate([blocks, pattern, pattern], axis=1)
-
     def step(block, d, pairs=None):
         pairs = pairs or [(i, i + d) for i in range(z_count) if 0 <= i + d < z_count]
         return lax.ppermute(block, "col", pairs)
@@ -183,27 +234,30 @@
 
     last = z_count - 1
     inner = range(1, last)
-    parts = [masked[: rows // 2], masked[rows // 2 :]]
-    fw1 = [step(part, 1) for part in parts]
-    bw1 = [step(part, -1) for part in parts]
+    parts = packed(present, upper, present)
+    again = packed(present, upper, parts[0])
+    fw1 = [step(parts[0], 1), step(again[1], 1)]
+    bw1 = [step(again[0], -1), step(parts[1], -1)]
     fw2 = [step(part, 1, [(i, i + 1) for i in inner]) for part in fw1]
     bw2 = [step(part, -1, [(i, i - 1) for i in inner]) for part in bw1]
     if z_count == 4:
-        route = [(1, 1, 0), (2, -1, 3)]
-        ends_first = hop(jnp.where(z < 2, bw2[1], fw2[0]), route)
-        ends_last = hop(jnp.where(z < 2, bw2[0], fw2[1]), route)
-        route = [(0, 1, 0), (1, 1, 1), (2, -1, 2), (3, -1, 3)]
-        below = jnp.concatenate([bw2[0][1:], bw2[1]])
-        above = jnp.concatenate([fw2[0], fw2[1][:1]])
-        cross = hop(jnp.where(z < 2, below, above), route)
+        to_end, beside = [(1, 1, 0), (2, -1, 3)], [(0, 1, 0), (1, 1, 1), (2, -1, 2), (3, -1, 3)]
+        sooner = jnp.where(z < 2, bw2[1], fw2[0])
+        ends_first = hop(sooner, to_end)
+        cross_first = hop(sooner, beside)
+        down, up = lax.optimization_barrier((bw2[0], fw2[1]))
+        later = jnp.where(z < 2, down, up)
+        ends_last = hop(later, to_end)
+        cross_last = hop(later, beside)
     else:
         route = [(last, 1, 0), (0, -1, last)]
         ends_first = hop(jnp.where(z == last, parts[1], parts[0]), route)
         ends_last = hop(jnp.where(z == last, parts[0], parts[1]), route)
         route = [(last - 1, 1, 0), (last, 1, 1), (0, -1, last - 1), (1, -1, last)]
-        cross = hop(jnp.where(z < 2, masked[:3], masked[1:]), route)
-    early = (masked, *fw1, *bw1, *fw2, *bw2, ends_first)
-    return compute(z_count, z.reshape(1), early, (ends_last, cross))
+        cross_first = hop(jnp.where(z < 2, parts[0], parts[1]), route)
+        cross_last = hop(jnp.where(z < 2, parts[1], parts[0]), route)
+    early = (*parts, *fw1, *bw1, *fw2, *bw2, ends_first)
+    return compute(z_count, z.reshape(1), early, (ends_last, cross_first, cross_last))
 
 
 def solution(mesh):

time: 86.5 us -> 81.5 us (0.942)
  waiting for transfers between devices: 48.8 us -> 40.2 us
  starting transfers between devices: 20.8 us -> 23.4 us
  other arithmetic: 2.39 us -> 0.12 us
  local copies, waits for them, and re-layouts: 0.18 us -> 1.91 us
  Pallas kernels: 13.7 us -> 15.3 us
    ppermute x8, waiting for transfers between devices: 35.4 us -> 28 us  [step(): return lax.ppermute(block, 'col', pairs)]
    ppermute x3 -> x4, starting transfers between devices: 5.97 us -> 9.34 us  [hop(): return lax.ppermute(block, ('row', 'col'), pairs)]
    unnamed x0 -> x4, local copies, waits for them, and re-layouts: none -> 1.91 us
    pallas_call x0 -> x2, Pallas kernels: none -> 1.56 us  [packed(): pl.pallas_call(pack, out_shape=[pair, pair], in_specs=[SMEM, VMEM, pl.Blo...]
    mul x1 -> x0, other arithmetic: 1.36 us -> none  [per_device(): blocks = (upper * weights).reshape(rows, wide * B, B)]
    ppermute x3 -> x4, waiting for transfers between devices: 13.5 us -> 12.2 us  [hop(): return lax.ppermute(block, ('row', 'col'), pairs)]
  transfers between devices with their start and end apart: 11 -> 12, of which waited for: 7 -> 7; matrix products, arithmetic and copies ran while one was open for 0% -> 0% of each run, Pallas kernels for 8% -> 9%
where the time goes in v5:
time: 81.5 us; the launch traced here: 81.1 us
  waiting for transfers between devices  40.2 us (49%)
  starting transfers between devices  23.4 us (29%)
  Pallas kernels  15.3 us (19%)
  local copies, waits for them, and re-layouts  1.91 us (2%)
    ppermute x8, waiting for transfers between devices, step(): return lax.ppermute(block, 'col', pairs)  28 us
    ppermute x8, starting transfers between devices, step(): return lax.ppermute(block, 'col', pairs)  14.1 us
    ppermute x4, waiting for transfers between devices, hop(): return lax.ppermute(block, ('row', 'col'), pairs)  12.2 us
    ppermute x4, starting transfers between devices, hop(): return lax.ppermute(block, ('row', 'col'), pairs)  9.34 us
    pallas_call x1, Pallas kernels, compute(): pl.pallas_call(functools.partial(second_kernel, z_count), out_shape=[jax....  7.31 us
    pallas_call x1, Pallas kernels, compute(): pl.pallas_call(functools.partial(first_kernel, z_count), out_shape=KEPT,...  6.39 us
    unnamed x4, local copies, waits for them, and re-layouts  1.91 us
  transfers between devices with their start and end apart: 12, of which 7 were waited for; matrix products, arithmetic and copies ran while one was open for 0% of the time, Pallas kernels for 9%

profile of v5, /device:TPU:25, one launch (start us, length us, event | category | flops | bytes accessed | tf_op | source)
XLA Modules:
  0.0 81.1 jit_solution(12495685181478204319)
XLA Ops:
  0.0 0.0 copy-start
  0.0 1.2 %copy-done = bf16[4,8,128,128]{3,2,1,0:T(8,128)(2,1)S(1)} copy-done((bf16[4,8,128,128]{3,2,1,0:T(8,128)(2,1)S(1)}, bf16[4,8,128,128]{3,2,1,0:T(8,128)(2,1)}, u32[]{:S(2)}) %copy-start) | copy-done | bytes 1048600
  1.2 0.0 copy-start.1
  1.2 0.7 copy-done.1
  1.9 0.8 shard_map.28
  2.7 2.1 %collective-permute-start.3 = (bf16[1936,128]{1,0:T(8,128)(2,1)S(1)}, bf16[1936,128]{1,0:T(8,128)(2,1)S(1)}, u32[]{:S(2)}, u32[]{:S(2)}) collective-permute-start(bf16[1936,128]{1,0:T(8,128)(2,1)S(1)} %get-tuple-element.16.ownb), channel_id=1, source_target_pairs={{1,0},{2,1},{3,2},{5,4},{6,5},{7,6},{9,8},{10,9},{11,10},{13,12},{... | collective-permute-start | bytes 1486856 | tf_op jit(solution)/shard_map/ppermute | solution.py:225
  4.8 1.3 %collective-permute-start = (bf16[1936,128]{1,0:T(8,128)(2,1)S(1)}, bf16[1936,128]{1,0:T(8,128)(2,1)}, u32[]{:S(2)}, u32[]{:S(2)}) collective-permute-start(bf16[1936,128]{1,0:T(8,128)(2,1)S(1)} %get-tuple-element.15._.owna), channel_id=1, source_target_pairs={{0,1},{1,2},{2,3},{4,5},{5,6},{6,7},{8,9},{9,10},{10,11},{12,13},{... | collective-permute-start | bytes 1486856 | tf_op jit(solution)/shard_map/ppermute | solution.py:225
  6.1 0.8 shard_map.29
  6.9 1.3 %collective-permute-start.1 = (bf16[1936,128]{1,0:T(8,128)(2,1)S(1)}, bf16[1936,128]{1,0:T(8,128)(2,1)}, u32[]{:S(2)}, u32[]{:S(2)}) collective-permute-start(bf16[1936,128]{1,0:T(8,128)(2,1)S(1)} %get-tuple-element.17), channel_id=1, source_target_pairs={{0,1},{1,2},{2,3},{4,5},{5,6},{6,7},{8,9},{9,10},{10,11},{12,13},{... | collective-permute-start | bytes 1486856 | tf_op jit(solution)/shard_map/ppermute | solution.py:225
  8.2 5.5 %collective-permute-start.2 = (bf16[1936,128]{1,0:T(8,128)(2,1)S(1)}, bf16[1936,128]{1,0:T(8,128)(2,1)}, u32[]{:S(2)}, u32[]{:S(2)}) collective-permute-start(bf16[1936,128]{1,0:T(8,128)(2,1)S(1)} %get-tuple-element.18), channel_id=1, source_target_pairs={{1,0},{2,1},{3,2},{5,4},{6,5},{7,6},{9,8},{10,9},{11,10},{13,12},{... | collective-permute-start | bytes 1486856 | tf_op jit(solution)/shard_map/ppermute | solution.py:225
  13.6 1.1 %collective-permute-done.3.bw1b = bf16[1936,128]{1,0:T(8,128)(2,1)S(1)} collective-permute-done((bf16[1936,128]{1,0:T(8,128)(2,1)S(1)}, bf16[1936,128]{1,0:T(8,128)(2,1)S(1)}, u32[]{:S(2)}, u32[]{:S(2)}) %collective-permute-start.3) | collective-permute-done | bytes 495648 | tf_op jit(solution)/shard_map/ppermute | solution.py:225
  14.7 0.7 collective-permute-start.7
  15.4 3.2 %collective-permute-done.fw1a = bf16[1936,128]{1,0:T(8,128)(2,1)} collective-permute-done((bf16[1936,128]{1,0:T(8,128)(2,1)S(1)}, bf16[1936,128]{1,0:T(8,128)(2,1)}, u32[]{:S(2)}, u32[]{:S(2)}) %collective-permute-start) | collective-permute-done | bytes 495648 | tf_op jit(solution)/shard_map/ppermute | solution.py:225
  18.7 1.3 %collective-permute-start.4 = (bf16[1936,128]{1,0:T(8,128)(2,1)}, bf16[1936,128]{1,0:T(8,128)(2,1)S(1)}, u32[]{:S(2)}, u32[]{:S(2)}) collective-permute-start(bf16[1936,128]{1,0:T(8,128)(2,1)} %collective-permute-done.fw1a), channel_id=1, source_target_pairs={{1,2},{2,3},{5,6},{6,7},{9,10},{10,11},{13,14},{14,15},{17,18},{18... | collective-permute-start | bytes 1486856 | tf_op jit(solution)/shard_map/ppermute | solution.py:225
  20.0 9.3 %collective-permute-done.1.fw1b = bf16[1936,128]{1,0:T(8,128)(2,1)} collective-permute-done((bf16[1936,128]{1,0:T(8,128)(2,1)S(1)}, bf16[1936,128]{1,0:T(8,128)(2,1)}, u32[]{:S(2)}, u32[]{:S(2)}) %collective-permute-start.1) | collective-permute-done | bytes 495648 | tf_op jit(solution)/shard_map/ppermute | solution.py:225
  29.3 1.3 %collective-permute-start.5 = (bf16[1936,128]{1,0:T(8,128)(2,1)}, bf16[1936,128]{1,0:T(8,128)(2,1)S(1)}, u32[]{:S(2)}, u32[]{:S(2)}) collective-permute-start(bf16[1936,128]{1,0:T(8,128)(2,1)} %collective-permute-done.1.fw1b), channel_id=1, source_target_pairs={{1,2},{2,3},{5,6},{6,7},{9,10},{10,11},{13,14},{14,15},{17,18},{18... | collective-permute-start | bytes 1486856 | tf_op jit(solution)/shard_map/ppermute | solution.py:225
  30.6 0.0 collective-permute-done.2.bw1a
  30.6 0.7 collective-permute-start.6
  31.3 0.0 collective-permute-done.7.bw2b
  31.3 8.5 %collective-permute-done.4.fw2a = bf16[1936,128]{1,0:T(8,128)(2,1)S(1)} collective-permute-done((bf16[1936,128]{1,0:T(8,128)(2,1)}, bf16[1936,128]{1,0:T(8,128)(2,1)S(1)}, u32[]{:S(2)}, u32[]{:S(2)}) %collective-permute-start.4) | collective-permute-done | bytes 495648 | tf_op jit(solution)/shard_map/ppermute | solution.py:225
  39.8 0.1 broadcast_select_fusion.1
  39.9 1.3 %collective-permute-start.8 = (bf16[1936,128]{1,0:T(8,128)(2,1)S(1)}, bf16[1936,128]{1,0:T(8,128)(2,1)S(1)}, u32[]{:S(2)}, u32[]{:S(2)}) collective-permute-start(bf16[1936,128]{1,0:T(8,128)(2,1)S(1)} %broadcast_select_fusion.1), channel_id=1, source_target_pairs={{1,4},{2,15},{5,8},{6,3},{9,12},{10,7},{13,0},{14,11},{17,20},{18,... | collective-permute-start | bytes 1486856 | tf_op jit(solution)/shard_map/ppermute | solution.py:233
  41.2 3.4 %collective-permute-start.10 = (bf16[1936,128]{1,0:T(8,128)(2,1)S(1)}, bf16[1936,128]{1,0:T(8,128)(2,1)S(1)}, u32[]{:S(2)}, u32[]{:S(2)}) collective-permute-start(bf16[1936,128]{1,0:T(8,128)(2,1)S(1)} %broadcast_select_fusion.1), channel_id=1, source_target_pairs={{0,4},{1,5},{2,14},{3,15},{4,8},{5,9},{6,2},{7,3},{8,12},{9,13},{1... | collective-permute-start | bytes 1486856 | tf_op jit(solution)/shard_map/ppermute | solution.py:233
  44.6 5.9 %collective-permute-done.5.fw2b = bf16[1936,128]{1,0:T(8,128)(2,1)S(1)} collective-permute-done((bf16[1936,128]{1,0:T(8,128)(2,1)}, bf16[1936,128]{1,0:T(8,128)(2,1)S(1)}, u32[]{:S(2)}, u32[]{:S(2)}) %collective-permute-start.5) | collective-permute-done | bytes 495648 | tf_op jit(solution)/shard_map/ppermute | solution.py:225
  50.4 0.0 collective-permute-done.6.bw2a
  50.4 0.1 broadcast_select_fusion
  50.5 3.4 %collective-permute-start.11 = (bf16[1936,128]{1,0:T(8,128)(2,1)S(1)}, bf16[1936,128]{1,0:T(8,128)(2,1)S(1)}, u32[]{:S(2)}, u32[]{:S(2)}) collective-permute-start(bf16[1936,128]{1,0:T(8,128)(2,1)S(1)} %broadcast_select_fusion), channel_id=1, source_target_pairs={{0,4},{1,5},{2,14},{3,15},{4,8},{5,9},{6,2},{7,3},{8,12},{9,13},{1... | collective-permute-start | bytes 1486856 | tf_op jit(solution)/shard_map/ppermute | solution.py:233
  53.9 1.3 %collective-permute-start.9 = (bf16[1936,128]{1,0:T(8,128)(2,1)S(1)}, bf16[1936,128]{1,0:T(8,128)(2,1)S(1)}, u32[]{:S(2)}, u32[]{:S(2)}) collective-permute-start(bf16[1936,128]{1,0:T(8,128)(2,1)S(1)} %broadcast_select_fusion), channel_id=1, source_target_pairs={{1,4},{2,15},{5,8},{6,3},{9,12},{10,7},{13,0},{14,11},{17,20},{18,... | collective-permute-start | bytes 1486856 | tf_op jit(solution)/shard_map/ppermute | solution.py:233
  55.2 9.5 %collective-permute-done.8.ends = bf16[1936,128]{1,0:T(8,128)(2,1)S(1)} collective-permute-done((bf16[1936,128]{1,0:T(8,128)(2,1)S(1)}, bf16[1936,128]{1,0:T(8,128)(2,1)S(1)}, u32[]{:S(2)}, u32[]{:S(2)}) %collective-permute-start.8) | collective-permute-done | bytes 495648 | tf_op jit(solution)/shard_map/ppermute | solution.py:233
  64.6 6.4 %shard_map.30 = (bf16[10,256,2048]{2,1,0:T(8,128)(2,1)S(1)}, bf16[2560,1536]{1,0:T(8,128)(2,1)S(1)}, f32[20,8,128]{2,1,0:T(8,128)S(1)}) custom-call(s32[1]{0:T(128)} %bitcast.place, bf16[1936,128]{1,0:T(8,128)(2,1)S(1)} %get-tuple-element.15._.owna, bf16[1936,128]{1,0:T(8,128)(2,1)S(1)} %get-tuple-element.16.ownb, ...), custom_call_target="tpu_custom_call" | custom-call | flops 6000000000 | bytes 6000000 | tf_op jit(solution)/shard_map/pallas_call | solution.py:189
  71.0 0.0 collective-permute-done.10.cross_first
  71.0 0.0 collective-permute-done.11.cross_last
  71.0 2.7 %collective-permute-done.9.ends = bf16[1936,128]{1,0:T(8,128)(2,1)S(1)} collective-permute-done((bf16[1936,128]{1,0:T(8,128)(2,1)S(1)}, bf16[1936,128]{1,0:T(8,128)(2,1)S(1)}, u32[]{:S(2)}, u32[]{:S(2)}) %collective-permute-start.9) | collective-permute-done | bytes 495648 | tf_op jit(solution)/shard_map/ppermute | solution.py:233
  73.8 7.3 %shard_map.31 = (bf16[4,8,128,128]{3,2,1,0:T(8,128)(2,1)}, bf16[10,256,2048]{2,1,0:T(8,128)(2,1)S(1)}, bf16[2560,1536]{1,0:T(8,128)(2,1)S(1)}, f32[20,8,128]{2,1,0:T(8,128)S(1)}) custom-call(s32[1]{0:T(128)} %bitcast.place, bf16[10,256,2048]{2,1,0:T(8,128)(2,1)S(1)} %get-tuple-element.19.x_in, ...), custom_call_target="tpu_custom_call", output_to_operand_aliasing={{1}: (1, {}), {2}: (2, {}), {3}: (3, {})} | custom-call | flops 6000000000 | bytes 4000000 | tf_op jit(solution)/shard_map/pallas_call | solution.py:197
Async XLA Ops:
  0.0 1.2 %copy-start = (bf16[4,8,128,128]{3,2,1,0:T(8,128)(2,1)S(1)}, bf16[4,8,128,128]{3,2,1,0:T(8,128)(2,1)}, u32[]{:S(2)}) copy-start(bf16[4,8,128,128]{3,2,1,0:T(8,128)(2,1)} %upper.3) | copy-start | bytes 3145732
  1.2 0.7 copy-start.1
  2.7 12.0 %collective-permute-start.3 = (bf16[1936,128]{1,0:T(8,128)(2,1)S(1)}, bf16[1936,128]{1,0:T(8,128)(2,1)S(1)}, u32[]{:S(2)}, u32[]{:S(2)}) collective-permute-start(bf16[1936,128]{1,0:T(8,128)(2,1)S(1)} %get-tuple-element.16.ownb), channel_id=1, source_target_pairs={{1,0},{2,1},{3,2},{5,4},{6,5},{7,6},{9,8},{10,9},{11,10},{13,12},{... | collective-permute-start | bytes 1486856 | tf_op jit(solution)/shard_map/ppermute | solution.py:225
  4.8 13.9 %collective-permute-start = (bf16[1936,128]{1,0:T(8,128)(2,1)S(1)}, bf16[1936,128]{1,0:T(8,128)(2,1)}, u32[]{:S(2)}, u32[]{:S(2)}) collective-permute-start(bf16[1936,128]{1,0:T(8,128)(2,1)S(1)} %get-tuple-element.15._.owna), channel_id=1, source_target_pairs={{0,1},{1,2},{2,3},{4,5},{5,6},{6,7},{8,9},{9,10},{10,11},{12,13},{... | collective-permute-start | bytes 1486856 | tf_op jit(solution)/shard_map/ppermute | solution.py:225
  6.9 22.4 %collective-permute-start.1 = (bf16[1936,128]{1,0:T(8,128)(2,1)S(1)}, bf16[1936,128]{1,0:T(8,128)(2,1)}, u32[]{:S(2)}, u32[]{:S(2)}) collective-permute-start(bf16[1936,128]{1,0:T(8,128)(2,1)S(1)} %get-tuple-element.17), channel_id=1, source_target_pairs={{0,1},{1,2},{2,3},{4,5},{5,6},{6,7},{8,9},{9,10},{10,11},{12,13},{... | collective-permute-start | bytes 1486856 | tf_op jit(solution)/shard_map/ppermute | solution.py:225
  8.2 22.4 %collective-permute-start.2 = (bf16[1936,128]{1,0:T(8,128)(2,1)S(1)}, bf16[1936,128]{1,0:T(8,128)(2,1)}, u32[]{:S(2)}, u32[]{:S(2)}) collective-permute-start(bf16[1936,128]{1,0:T(8,128)(2,1)S(1)} %get-tuple-element.18), channel_id=1, source_target_pairs={{1,0},{2,1},{3,2},{5,4},{6,5},{7,6},{9,8},{10,9},{11,10},{13,12},{... | collective-permute-start | bytes 1486856 | tf_op jit(solution)/shard_map/ppermute | solution.py:225
  14.7 16.6 %collective-permute-start.7 = (bf16[1936,128]{1,0:T(8,128)(2,1)S(1)}, bf16[1936,128]{1,0:T(8,128)(2,1)S(1)}, u32[]{:S(2)}, u32[]{:S(2)}) collective-permute-start(bf16[1936,128]{1,0:T(8,128)(2,1)S(1)} %collective-permute-done.3.bw1b), channel_id=1, source_target_pairs={{1,0},{2,1},{5,4},{6,5},{9,8},{10,9},{13,12},{14,13},{17,16},{18,1... | collective-permute-start | bytes 1486856 | tf_op jit(solution)/shard_map/ppermute | solution.py:225
  18.7 21.1 %collective-permute-start.4 = (bf16[1936,128]{1,0:T(8,128)(2,1)}, bf16[1936,128]{1,0:T(8,128)(2,1)S(1)}, u32[]{:S(2)}, u32[]{:S(2)}) collective-permute-start(bf16[1936,128]{1,0:T(8,128)(2,1)} %collective-permute-done.fw1a), channel_id=1, source_target_pairs={{1,2},{2,3},{5,6},{6,7},{9,10},{10,11},{13,14},{14,15},{17,18},{18... | collective-permute-start | bytes 1486856 | tf_op jit(solution)/shard_map/ppermute | solution.py:225
  29.3 21.1 %collective-permute-start.5 = (bf16[1936,128]{1,0:T(8,128)(2,1)}, bf16[1936,128]{1,0:T(8,128)(2,1)S(1)}, u32[]{:S(2)}, u32[]{:S(2)}) collective-permute-start(bf16[1936,128]{1,0:T(8,128)(2,1)} %collective-permute-done.1.fw1b), channel_id=1, source_target_pairs={{1,2},{2,3},{5,6},{6,7},{9,10},{10,11},{13,14},{14,15},{17,18},{18... | collective-permute-start | bytes 1486856 | tf_op jit(solution)/shard_map/ppermute | solution.py:225
  30.6 19.8 %collective-permute-start.6 = (bf16[1936,128]{1,0:T(8,128)(2,1)}, bf16[1936,128]{1,0:T(8,128)(2,1)S(1)}, u32[]{:S(2)}, u32[]{:S(2)}) collective-permute-start(bf16[1936,128]{1,0:T(8,128)(2,1)} %collective-permute-done.2.bw1a), channel_id=1, source_target_pairs={{1,0},{2,1},{5,4},{6,5},{9,8},{10,9},{13,12},{14,13},{17,16},{18,1... | collective-permute-start | bytes 1486856 | tf_op jit(solution)/shard_map/ppermute | solution.py:225
  39.9 24.7 %collective-permute-start.8 = (bf16[1936,128]{1,0:T(8,128)(2,1)S(1)}, bf16[1936,128]{1,0:T(8,128)(2,1)S(1)}, u32[]{:S(2)}, u32[]{:S(2)}) collective-permute-start(bf16[1936,128]{1,0:T(8,128)(2,1)S(1)} %broadcast_select_fusion.1), channel_id=1, source_target_pairs={{1,4},{2,15},{5,8},{6,3},{9,12},{10,7},{13,0},{14,11},{17,20},{18,... | collective-permute-start | bytes 1486856 | tf_op jit(solution)/shard_map/ppermute | solution.py:233
  41.2 29.8 %collective-permute-start.10 = (bf16[1936,128]{1,0:T(8,128)(2,1)S(1)}, bf16[1936,128]{1,0:T(8,128)(2,1)S(1)}, u32[]{:S(2)}, u32[]{:S(2)}) collective-permute-start(bf16[1936,128]{1,0:T(8,128)(2,1)S(1)} %broadcast_select_fusion.1), channel_id=1, source_target_pairs={{0,4},{1,5},{2,14},{3,15},{4,8},{5,9},{6,2},{7,3},{8,12},{9,13},{1... | collective-permute-start | bytes 1486856 | tf_op jit(solution)/shard_map/ppermute | solution.py:233
  50.5 20.5 %collective-permute-start.11 = (bf16[1936,128]{1,0:T(8,128)(2,1)S(1)}, bf16[1936,128]{1,0:T(8,128)(2,1)S(1)}, u32[]{:S(2)}, u32[]{:S(2)}) collective-permute-start(bf16[1936,128]{1,0:T(8,128)(2,1)S(1)} %broadcast_select_fusion), channel_id=1, source_target_pairs={{0,4},{1,5},{2,14},{3,15},{4,8},{5,9},{6,2},{7,3},{8,12},{9,13},{1... | collective-permute-start | bytes 1486856 | tf_op jit(solution)/shard_map/ppermute | solution.py:233
  53.9 19.9 %collective-permute-start.9 = (bf16[1936,128]{1,0:T(8,128)(2,1)S(1)}, bf16[1936,128]{1,0:T(8,128)(2,1)S(1)}, u32[]{:S(2)}, u32[]{:S(2)}) collective-permute-start(bf16[1936,128]{1,0:T(8,128)(2,1)S(1)} %broadcast_select_fusion), channel_id=1, source_target_pairs={{1,4},{2,15},{5,8},{6,3},{9,12},{10,7},{13,0},{14,11},{17,20},{18,... | collective-permute-start | bytes 1486856 | tf_op jit(solution)/shard_map/ppermute | solution.py:233

commit v6 on v5

v6 whole, which is shorter than its diff:
```python
import functools

import jax
import jax.numpy as jnp
from jax import lax
from jax.experimental import pallas as pl
from jax.experimental.pallas import tpu as pltpu
from jax.sharding import PartitionSpec as P

B = 128
NT = (((1,), (1,)), ((), ()))
NN = (((1,), (0,)), ((), ()))

MIXED = 7 * B
TAIL = 8 * B
SECOND = 8 * B + 16
PAIR = 15 * B + 16
ONE = SECOND

LOW = {1: 2, 2: 1, 3: 1, 4: 2, 5: 2, 6: 1, 7: 1}
HIGH = {12: 1, 13: 1, 14: 2, 15: 2, 16: 1, 17: 1, 18: 2}


def blk(a, n=1):
    return pl.ds(a * B, n * B)


def x_stage(late, J, m):
    return max(late.get(min(2 * J, m), 0), late.get(min(2 * J + 1, m), 0))


def square_terms(late, J, L):
    return [
        (m, max(x_stage(late, J, m), x_stage(late, L, m))) for m in range(2 * L - 7, 2 * J + 9)
    ]


def y_stage(late, J, L):
    return max(stage for _, stage in square_terms(late, min(J, L), max(J, L)))


def cube_terms(late, I, L):
    return [
        (j, max(x_stage(late, I, j), y_stage(late, j // 2, L))) for j in range(2 * L - 7, 2 * I + 9)
    ]


def runs(columns):
    found = []
    for m in columns:
        if found and found[-1][0] + found[-1][1] == m:
            found[-1][1] += 1
        else:
            found.append([m, 1])
    return found


def triangles():
    p = lax.broadcasted_iota(jnp.int32, (B, B), 0)
    q = lax.broadcasted_iota(jnp.int32, (B, B), 1)
    return p, q


def pack(present, upper, _, *outs):
    p, q = triangles()
    right = lax.broadcasted_iota(jnp.int32, (1, B), 1) >= B // 2

    def block(r, k):
        w = present[r, k].astype(jnp.float32)
        return upper[r, k].astype(jnp.float32) * w

    for first, out in zip((0, 2), outs):
        one, two = block(first, 0), block(first + 1, 0)
        out[pl.ds(MIXED, B)] = jnp.where(p <= q, one, two).astype(jnp.bfloat16)
        for r in range(2):
            for k in range(1, 8):
                out[pl.ds(SECOND * r + (k - 1) * B, B)] = block(first + r, k).astype(jnp.bfloat16)
        lines = [
            jnp.where(
                right,
                present[first + 1, k].astype(jnp.float32),
                present[first, k].astype(jnp.float32),
            )
            for k in range(8)
        ]
        lines.append(jnp.sum(jnp.where(p == q, two, 0.0), axis=0, keepdims=True))
        lines.append(jnp.zeros((7, B), jnp.float32))
        out[pl.ds(TAIL, 16)] = jnp.concatenate(lines, axis=0).astype(jnp.bfloat16)


def set_x(x_ref, a, b, value):
    x_ref[a // 2, blk(a % 2), blk(b - a // 2 * 2 + 7)] = value


def put(x_ref, w_ref, ref, a, rows=(0, 1), skip=0):
    p, q = triangles()
    mixed = ref[pl.ds(MIXED - skip, B)].astype(jnp.float32)
    turned = mixed.T
    tail = ref[pl.ds(TAIL - skip, 16)].astype(jnp.float32)
    for r in rows:
        w_ref[a + r] = jnp.broadcast_to(tail[:8, r * B // 2 : r * B // 2 + 1], (8, B))
        if r == 0:
            diagonal = jnp.where(p <= q, mixed, turned)
        else:
            diagonal = jnp.where(p > q, mixed, jnp.where(p < q, turned, tail[8:9]))
        set_x(x_ref, a + r, a + r, diagonal.astype(jnp.bfloat16))
        for k in range(1, 8):
            u = ref[pl.ds(SECOND * r - skip + (k - 1) * B, B)]
            set_x(x_ref, a + r, a + r + k, u)
            if k <= 18 - a - r:
                set_x(x_ref, a + r + k, a + r, u.T)


def square(late, now, x_ref, y_ref, w_ref, part_ref):
    zero = jnp.zeros((B, B), jnp.bfloat16)
    for L in range(4, 10):
        for J in range(L - 4, L + 1):
            terms = square_terms(late, J, L)
            end = max(stage for _, stage in terms)
            if now > end or (now == 0 and end > 0):
                continue
            mine = [m for m, stage in terms if (stage <= now if now < 2 else stage == 2)]
            s = None
            for m, n in runs(mine):
                t = lax.dot_general(
                    x_ref[J, :, blk(m - 2 * J + 7, n)],
                    x_ref[L, :, blk(m - 2 * L + 7, n)],
                    NT,
                    preferred_element_type=jnp.float32,
                )
                s = t if s is None else s + t
            place = L % 3 * 5 + J - L + 4
            if now < end:
                if s is not None:
                    part_ref[place] = s
                continue
            if now == 2 and len(mine) < len(terms):
                s = s + part_ref[place]
            for dj in range(2):
                for dl in range(2):
                    j, l = 2 * J + dj, 2 * L + dl
                    off = abs(l - j)
                    if off > 7 or j in (0, 19) or l in (0, 19):
                        y_ref[blk(j), blk(l - 8)] = zero
                    else:
                        w = w_ref[min(j, l), pl.ds(off, 1)]
                        y_ref[blk(j), blk(l - 8)] = (
                            s[dj * B : (dj + 1) * B, dl * B : (dl + 1) * B] * w
                        ).astype(jnp.bfloat16)


def purify(late, now, x_ref, y_ref, w_ref, part_ref, out, done):
    for I in (4, 5):
        for L in range(I, I + 5):
            terms = cube_terms(late, I, L)
            end = max(stage for _, stage in terms)
            mine = [j for j, stage in terms if (stage == 2) == (now == 2)]
            c = None
            for up in (True, False):
                for j, n in runs([j for j in mine if (j <= 2 * L) == up]):
                    left = x_ref[I, :, blk(j - 2 * I + 7, n)]
                    right = (
                        y_ref[blk(j, n), blk(2 * L - 8, 2)] if up else y_ref[blk(2 * L, 2), blk(j - 8, n)]
                    )
                    t = lax.dot_general(
                        left, right, NN if up else NT, preferred_element_type=jnp.float32
                    )
                    c = t if c is None else c + t
            place = (I - 4) * 5 + L - I
            if now < end:
                if c is not None:
                    part_ref[place] = c
                continue
            if now == 2 and end == 2 and len(mine) < len(terms):
                c = c + part_ref[place]
            for di in range(2):
                for dl in range(2):
                    i, l = 2 * I + di, 2 * L + dl
                    off = l - i
                    if not 0 <= off <= 7:
                        continue
                    if now == 2 and end < 2:
                        out[i - 8, off] = done[i - 8, off]
                        continue
                    w = w_ref[i, pl.ds(off, 1)]
                    sq = y_ref[blk(i), blk(l - 8)].astype(jnp.float32)
                    cube = w * c[di * B : (di + 1) * B, dl * B : (dl + 1) * B]
                    out[i - 8, off] = (3.0 * sq - 2.0 * cube).astype(jnp.bfloat16)


def take_all(x_ref, w_ref, pieces):
    for here, ref, a, rows, skip in pieces:
        pl.when(here)(functools.partial(put, x_ref, w_ref, ref, a, rows, skip))


def for_half(z, z_count, work):
    low = z < z_count // 2
    pl.when(low)(functools.partial(work, LOW))
    pl.when(jnp.logical_not(low))(functools.partial(work, HIGH))


def stage_0(z_count, place, owna, ownb, fw1a, fw1b, bw1a, bw1b, fw2a, fw2b, bw2a, bw2b, x_ref, y_ref, w_ref):
    zero = jnp.zeros((B, B), jnp.bfloat16)
    for c in range(16):
        set_x(x_ref, 0, c - 7, zero)
        set_x(x_ref, 19, c + 11, zero)
    for a in range(1, 19):
        set_x(x_ref, a, a + 8 if a % 2 == 0 else a - 8, zero)
    z = place[0]
    last = z_count - 1
    put(x_ref, w_ref, owna, 8)
    put(x_ref, w_ref, ownb, 10)
    both = (0, 1)
    take_all(
        x_ref,
        w_ref,
        (
            (z > 0, fw1a, 4, both, 0),
            (z > 0, fw1b, 6, both, 0),
            (z < last, bw1a, 12, both, 0),
            (z < last, bw1b, 14, both, 0),
            (z > 1, fw2a, 0, (1,), 0),
            (z > 1, fw2b, 2, both, 0),
            (z < last - 1, bw2a, 16, both, 0),
            (z < last - 1, bw2b, 18, (0,), 0),
        ),
    )

    def work(late):
        square(late, 0, x_ref, y_ref, w_ref, None)

    for_half(z, z_count, work)


def stage_1(z_count, place, x_in, y_in, w_in, ends, cross, x_ref, y_ref, w_ref, sums, cubes, done):
    z = place[0]
    last = z_count - 1
    both = (0, 1)
    take_all(
        x_ref,
        w_ref,
        (
            (z == 0, ends, 6, both, 0),
            (z == last, ends, 12, both, 0),
            (z <= 1, cross, 2, both, 0),
            (z >= last - 1, cross, 16, both, 0),
        ),
    )

    def work(late):
        square(late, 1, x_ref, y_ref, w_ref, sums)
        purify(late, 1, x_ref, y_ref, w_ref, cubes, done, None)

    for_half(z, z_count, work)


def stage_2(z_count, place, x_in, y_in, w_in, sums, cubes, done, ends, cross, out, x_ref, y_ref, w_ref):
    z = place[0]
    last = z_count - 1
    both = (0, 1)
    take_all(
        x_ref,
        w_ref,
        (
            (z == 0, ends, 4, both, 0),
            (z == last, ends, 14, both, 0),
            (z <= 1, cross, 0, (1,), MIXED),
            (z >= last - 1, cross, 18, (0,), 0),
        ),
    )

    def work(late):
        square(late, 2, x_ref, y_ref, w_ref, sums)
        purify(late, 2, x_ref, y_ref, w_ref, cubes, out, done)

    for_half(z, z_count, work)


SMEM = pl.BlockSpec(memory_space=pltpu.SMEM)
VMEM = pl.BlockSpec(memory_space=pltpu.VMEM)
KEPT = [
    pltpu.VMEM((10, 2 * B, 16 * B), jnp.bfloat16),
    pltpu.VMEM((20 * B, 12 * B), jnp.bfloat16),
    pltpu.VMEM((20, 8, B), jnp.float32),
]
PARTIAL = [
    pltpu.VMEM((15, 2 * B, 2 * B), jnp.float32),
    pltpu.VMEM((10, 2 * B, 2 * B), jnp.float32),
    pltpu.VMEM((4, 8, B, B), jnp.bfloat16),
]


def call(kernel, z_count, outs, aliases, flops, *operands):
    return pl.pallas_call(
        functools.partial(kernel, z_count),
        out_shape=outs,
        in_specs=[SMEM] + [VMEM] * (len(operands) - 1),
        out_specs=[VMEM] * len(outs),
        input_output_aliases=aliases,
        compiler_params=pltpu.CompilerParams(vmem_limit_bytes=16 * 1024 * 1024),
        cost_estimate=pl.CostEstimate(flops=flops, bytes_accessed=10**6, transcendentals=0),
    )(*operands)


def compute(z_count, place, rows_0, rows_1, rows_2):
    kept = call(stage_0, z_count, KEPT, {}, 10**9, place, *rows_0)
    got = call(stage_1, z_count, KEPT + PARTIAL, {1: 0, 2: 1, 3: 2}, 6 * 10**9, place, *kept, *rows_1)
    out = [jax.ShapeDtypeStruct((4, 8, B, B), jnp.bfloat16)]
    return call(stage_2, z_count, out + KEPT, {1: 1, 2: 2, 3: 3}, 6 * 10**9, place, *got, *rows_2)[0]


def packed(present, upper, before):
    rows = upper.shape[2]
    pair = jax.ShapeDtypeStruct((PAIR, rows), jnp.bfloat16)
    return pl.pallas_call(
        pack,
        out_shape=[pair, pair],
        in_specs=[SMEM, VMEM, pl.BlockSpec(memory_space=pl.ANY)],
        out_specs=[VMEM, VMEM],
        compiler_params=pltpu.CompilerParams(vmem_limit_bytes=8 * 1024 * 1024),
    )(present, upper, before)


def per_device(upper, present):
    s_count, z_count = lax.axis_size("row"), lax.axis_size("col")
    z = lax.axis_index("col")

    def step(block, d, pairs=None):
        pairs = pairs or [(i, i + d) for i in range(z_count) if 0 <= i + d < z_count]
        return lax.ppermute(block, "col", pairs)

    def hop(block, route):
        pairs = [
            (i * z_count + a, (i + d) % s_count * z_count + b)
            for i in range(s_count)
            for a, d, b in route
        ]
        return lax.ppermute(block, ("row", "col"), pairs)

    last = z_count - 1
    inner = range(1, last)
    parts = packed(present, upper, present)
    again = packed(present, upper, parts[0])
    fw1 = [step(parts[0], 1), step(again[1], 1)]
    bw1 = [step(again[0], -1), step(parts[1], -1)]
    fw2 = [step(part, 1, [(i, i + 1) for i in inner]) for part in fw1]
    bw2 = [step(part, -1, [(i, i - 1) for i in inner]) for part in bw1]
    if z_count == 4:
        to_end, beside = [(1, 1, 0), (2, -1, 3)], [(0, 1, 0), (1, 1, 1), (2, -1, 2), (3, -1, 3)]
        sooner = jnp.where(z < 2, bw2[1], fw2[0])
        ends_first = hop(sooner, to_end)
        cross_first = hop(sooner, beside)
        down, up = lax.optimization_barrier((bw2[0], fw2[1]))
        ends_last = hop(jnp.where(z < 2, down, up), to_end)
        cross_last = hop(jnp.where(z < 2, down[PAIR - ONE :], up[:ONE]), beside)
    else:
        route = [(last, 1, 0), (0, -1, last)]
        ends_first = hop(jnp.where(z == last, parts[1], parts[0]), route)
        ends_last = hop(jnp.where(z == last, parts[0], parts[1]), route)
        route = [(last - 1, 1, 0), (last, 1, 1), (0, -1, last - 1), (1, -1, last)]
        cross_first = hop(jnp.where(z < 2, parts[0], parts[1]), route)
        cross_last = hop(jnp.where(z < 2, parts[1][:ONE], parts[0][PAIR - ONE :]), route)
    rows = (*parts, *fw1, *bw1, *fw2, *bw2)
    return compute(z_count, z.reshape(1), rows, (ends_first, cross_first), (ends_last, cross_last))


def solution(mesh):
    return jax.shard_map(
        per_device,
        mesh=mesh,
        in_specs=(P(("groups", "row", "col"), None, None, None), P(("groups", "row", "col"), None)),
        out_specs=P(("groups", "row", "col"), None, None, None),
        check_vma=False,
    )
```

time: 81.5 us -> 78.8 us (0.967)
  waiting for transfers between devices: 40.2 us -> 36.7 us
    ppermute x4, waiting for transfers between devices: 12.2 us -> 8.63 us  [hop(): return lax.ppermute(block, ('row', 'col'), pairs)]
    pallas_call x2 -> x3, Pallas kernels: 13.7 us -> 14.5 us  [call(): pl.pallas_call(functools.partial(kernel, z_count), out_shape=outs, in_spe...]
  transfers between devices with their start and end apart: 12 -> 12, of which waited for: 7 -> 7; matrix products, arithmetic and copies ran while one was open for 0% -> 0% of each run, Pallas kernels for 9% -> 14%
where the time goes in v6:
time: 78.8 us; the launch traced here: 78.4 us
  waiting for transfers between devices  36.7 us (47%)
  starting transfers between devices  23.4 us (30%)
  Pallas kernels  16.1 us (20%)
  local copies, waits for them, and re-layouts  1.91 us (2%)
    ppermute x8, waiting for transfers between devices, step(): return lax.ppermute(block, 'col', pairs)  28.1 us
    pallas_call x3, Pallas kernels, call(): pl.pallas_call(functools.partial(kernel, z_count), out_shape=outs, in_spe...  14.5 us
    ppermute x8, starting transfers between devices, step(): return lax.ppermute(block, 'col', pairs)  14.1 us
    ppermute x4, starting transfers between devices, hop(): return lax.ppermute(block, ('row', 'col'), pairs)  9.34 us
    ppermute x4, waiting for transfers between devices, hop(): return lax.ppermute(block, ('row', 'col'), pairs)  8.63 us
    unnamed x4, local copies, waits for them, and re-layouts  1.91 us
  transfers between devices with their start and end apart: 12, of which 7 were waited for; matrix products, arithmetic and copies ran while one was open for 0% of the time, Pallas kernels for 14%

profile of v6, /device:TPU:25, one launch (start us, length us, event | category | flops | bytes accessed | tf_op | source)
XLA Modules:
  0.0 78.4 jit_solution(17421063858354453967)
XLA Ops:
  0.0 0.0 copy-start
  0.0 1.2 %copy-done = bf16[4,8,128,128]{3,2,1,0:T(8,128)(2,1)S(1)} copy-done((bf16[4,8,128,128]{3,2,1,0:T(8,128)(2,1)S(1)}, bf16[4,8,128,128]{3,2,1,0:T(8,128)(2,1)}, u32[]{:S(2)}) %copy-start) | copy-done | bytes 1048600
  1.2 0.0 copy-start.1
  1.2 0.7 copy-done.1
  1.9 0.8 shard_map.28
  2.7 2.1 %collective-permute-start.3 = (bf16[1936,128]{1,0:T(8,128)(2,1)S(1)}, bf16[1936,128]{1,0:T(8,128)(2,1)S(1)}, u32[]{:S(2)}, u32[]{:S(2)}) collective-permute-start(bf16[1936,128]{1,0:T(8,128)(2,1)S(1)} %get-tuple-element.22.ownb), channel_id=1, source_target_pairs={{1,0},{2,1},{3,2},{5,4},{6,5},{7,6},{9,8},{10,9},{11,10},{13,12},{... | collective-permute-start | bytes 1486856 | tf_op jit(solution)/shard_map/ppermute | solution.py:330
  4.8 1.3 %collective-permute-start = (bf16[1936,128]{1,0:T(8,128)(2,1)S(1)}, bf16[1936,128]{1,0:T(8,128)(2,1)}, u32[]{:S(2)}, u32[]{:S(2)}) collective-permute-start(bf16[1936,128]{1,0:T(8,128)(2,1)S(1)} %get-tuple-element.21._.owna), channel_id=1, source_target_pairs={{0,1},{1,2},{2,3},{4,5},{5,6},{6,7},{8,9},{9,10},{10,11},{12,13},{... | collective-permute-start | bytes 1486856 | tf_op jit(solution)/shard_map/ppermute | solution.py:330
  6.1 0.8 shard_map.29
  6.9 1.3 %collective-permute-start.1 = (bf16[1936,128]{1,0:T(8,128)(2,1)S(1)}, bf16[1936,128]{1,0:T(8,128)(2,1)}, u32[]{:S(2)}, u32[]{:S(2)}) collective-permute-start(bf16[1936,128]{1,0:T(8,128)(2,1)S(1)} %get-tuple-element.23), channel_id=1, source_target_pairs={{0,1},{1,2},{2,3},{4,5},{5,6},{6,7},{8,9},{9,10},{10,11},{12,13},{... | collective-permute-start | bytes 1486856 | tf_op jit(solution)/shard_map/ppermute | solution.py:330
  8.2 5.4 %collective-permute-start.2 = (bf16[1936,128]{1,0:T(8,128)(2,1)S(1)}, bf16[1936,128]{1,0:T(8,128)(2,1)}, u32[]{:S(2)}, u32[]{:S(2)}) collective-permute-start(bf16[1936,128]{1,0:T(8,128)(2,1)S(1)} %get-tuple-element.24), channel_id=1, source_target_pairs={{1,0},{2,1},{3,2},{5,4},{6,5},{7,6},{9,8},{10,9},{11,10},{13,12},{... | collective-permute-start | bytes 1486856 | tf_op jit(solution)/shard_map/ppermute | solution.py:330
  13.6 1.1 %collective-permute-done.3.bw1b = bf16[1936,128]{1,0:T(8,128)(2,1)S(1)} collective-permute-done((bf16[1936,128]{1,0:T(8,128)(2,1)S(1)}, bf16[1936,128]{1,0:T(8,128)(2,1)S(1)}, u32[]{:S(2)}, u32[]{:S(2)}) %collective-permute-start.3) | collective-permute-done | bytes 495648 | tf_op jit(solution)/shard_map/ppermute | solution.py:330
  14.7 0.7 collective-permute-start.7
  15.4 3.2 %collective-permute-done.fw1a = bf16[1936,128]{1,0:T(8,128)(2,1)} collective-permute-done((bf16[1936,128]{1,0:T(8,128)(2,1)S(1)}, bf16[1936,128]{1,0:T(8,128)(2,1)}, u32[]{:S(2)}, u32[]{:S(2)}) %collective-permute-start) | collective-permute-done | bytes 495648 | tf_op jit(solution)/shard_map/ppermute | solution.py:330
  18.7 1.3 %collective-permute-start.4 = (bf16[1936,128]{1,0:T(8,128)(2,1)}, bf16[1936,128]{1,0:T(8,128)(2,1)S(1)}, u32[]{:S(2)}, u32[]{:S(2)}) collective-permute-start(bf16[1936,128]{1,0:T(8,128)(2,1)} %collective-permute-done.fw1a), channel_id=1, source_target_pairs={{1,2},{2,3},{5,6},{6,7},{9,10},{10,11},{13,14},{14,15},{17,18},{18... | collective-permute-start | bytes 1486856 | tf_op jit(solution)/shard_map/ppermute | solution.py:330
  20.0 9.3 %collective-permute-done.1.fw1b = bf16[1936,128]{1,0:T(8,128)(2,1)} collective-permute-done((bf16[1936,128]{1,0:T(8,128)(2,1)S(1)}, bf16[1936,128]{1,0:T(8,128)(2,1)}, u32[]{:S(2)}, u32[]{:S(2)}) %collective-permute-start.1) | collective-permute-done | bytes 495648 | tf_op jit(solution)/shard_map/ppermute | solution.py:330
  29.3 1.3 %collective-permute-start.5 = (bf16[1936,128]{1,0:T(8,128)(2,1)}, bf16[1936,128]{1,0:T(8,128)(2,1)S(1)}, u32[]{:S(2)}, u32[]{:S(2)}) collective-permute-start(bf16[1936,128]{1,0:T(8,128)(2,1)} %collective-permute-done.1.fw1b), channel_id=1, source_target_pairs={{1,2},{2,3},{5,6},{6,7},{9,10},{10,11},{13,14},{14,15},{17,18},{18... | collective-permute-start | bytes 1486856 | tf_op jit(solution)/shard_map/ppermute | solution.py:330
  30.6 0.0 collective-permute-done.2.bw1a
  30.6 0.7 collective-permute-start.6
  31.3 0.0 collective-permute-done.7.bw2b
  31.3 8.5 %collective-permute-done.4.fw2a = bf16[1936,128]{1,0:T(8,128)(2,1)S(1)} collective-permute-done((bf16[1936,128]{1,0:T(8,128)(2,1)}, bf16[1936,128]{1,0:T(8,128)(2,1)S(1)}, u32[]{:S(2)}, u32[]{:S(2)}) %collective-permute-start.4) | collective-permute-done | bytes 495648 | tf_op jit(solution)/shard_map/ppermute | solution.py:330
  39.8 0.1 broadcast_select_fusion.1
  39.9 3.4 %collective-permute-start.9 = (bf16[1936,128]{1,0:T(8,128)(2,1)S(1)}, bf16[1936,128]{1,0:T(8,128)(2,1)S(1)}, u32[]{:S(2)}, u32[]{:S(2)}) collective-permute-start(bf16[1936,128]{1,0:T(8,128)(2,1)S(1)} %broadcast_select_fusion.1), channel_id=1, source_target_pairs={{0,4},{1,5},{2,14},{3,15},{4,8},{5,9},{6,2},{7,3},{8,12},{9,13},{1... | collective-permute-start | bytes 1486856 | tf_op jit(solution)/shard_map/ppermute | solution.py:338
  43.3 1.3 %collective-permute-start.8 = (bf16[1936,128]{1,0:T(8,128)(2,1)S(1)}, bf16[1936,128]{1,0:T(8,128)(2,1)S(1)}, u32[]{:S(2)}, u32[]{:S(2)}) collective-permute-start(bf16[1936,128]{1,0:T(8,128)(2,1)S(1)} %broadcast_select_fusion.1), channel_id=1, source_target_pairs={{1,4},{2,15},{5,8},{6,3},{9,12},{10,7},{13,0},{14,11},{17,20},{18,... | collective-permute-start | bytes 1486856 | tf_op jit(solution)/shard_map/ppermute | solution.py:338
  44.5 5.9 %collective-permute-done.5.fw2b = bf16[1936,128]{1,0:T(8,128)(2,1)S(1)} collective-permute-done((bf16[1936,128]{1,0:T(8,128)(2,1)}, bf16[1936,128]{1,0:T(8,128)(2,1)S(1)}, u32[]{:S(2)}, u32[]{:S(2)}) %collective-permute-start.5) | collective-permute-done | bytes 495648 | tf_op jit(solution)/shard_map/ppermute | solution.py:330
  50.4 0.0 collective-permute-done.6.bw2a
  50.5 3.4 %collective-permute-start.11 = (bf16[1040,128]{1,0:T(8,128)(2,1)S(1)}, bf16[1040,128]{1,0:T(8,128)(2,1)S(1)}, u32[]{:S(2)}, u32[]{:S(2)}) collective-permute-start(bf16[1040,128]{1,0:T(8,128)(2,1)S(1)} %slice_select_fusion), channel_id=1, source_target_pairs={{0,4},{1,5},{2,14},{3,15},{4,8},{5,9},{6,2},{7,3},{8,12},{9,13},{1... | collective-permute-start | bytes 798728 | tf_op jit(solution)/shard_map/ppermute | solution.py:338
  53.8 0.1 broadcast_select_fusion
  53.9 1.3 %collective-permute-start.10 = (bf16[1936,128]{1,0:T(8,128)(2,1)S(1)}, bf16[1936,128]{1,0:T(8,128)(2,1)S(1)}, u32[]{:S(2)}, u32[]{:S(2)}) collective-permute-start(bf16[1936,128]{1,0:T(8,128)(2,1)S(1)} %broadcast_select_fusion), channel_id=1, source_target_pairs={{1,4},{2,15},{5,8},{6,3},{9,12},{10,7},{13,0},{14,11},{17,20},{18,... | collective-permute-start | bytes 1486856 | tf_op jit(solution)/shard_map/ppermute | solution.py:338
  55.2 5.1 %shard_map.30 = (bf16[10,256,2048]{2,1,0:T(8,128)(2,1)S(1)}, bf16[2560,1536]{1,0:T(8,128)(2,1)S(1)}, f32[20,8,128]{2,1,0:T(8,128)S(1)}) custom-call(s32[1]{0:T(128)} %bitcast.place, bf16[1936,128]{1,0:T(8,128)(2,1)S(1)} %get-tuple-element.21._.owna, bf16[1936,128]{1,0:T(8,128)(2,1)S(1)} %get-tuple-element.22.ownb, ...), custom_call_target="tpu_custom_call" | custom-call | flops 1000000000 | bytes 1000000 | tf_op jit(solution)/shard_map/pallas_call | solution.py:294
  60.3 0.0 collective-permute-done.9.cross
  60.3 4.3 %collective-permute-done.8.ends = bf16[1936,128]{1,0:T(8,128)(2,1)S(1)} collective-permute-done((bf16[1936,128]{1,0:T(8,128)(2,1)S(1)}, bf16[1936,128]{1,0:T(8,128)(2,1)S(1)}, u32[]{:S(2)}, u32[]{:S(2)}) %collective-permute-start.8) | collective-permute-done | bytes 495648 | tf_op jit(solution)/shard_map/ppermute | solution.py:338
  64.6 4.8 %shard_map.31 = (bf16[10,256,2048]{2,1,0:T(8,128)(2,1)S(1)}, bf16[2560,1536]{1,0:T(8,128)(2,1)S(1)}, f32[20,8,128]{2,1,0:T(8,128)S(1)}, f32[15,256,256]{2,1,0:T(...) custom-call(s32[1]{0:T(128)} %bitcast.place, ...), custom_call_target="tpu_custom_call", output_to_operand_aliasing={{0}: (1, {}), {1}: (2, {}), {2}: (3, {})} | custom-call | flops 6000000000 | bytes 1000000 | tf_op jit(solution)/shard_map/pallas_call | solution.py:294
  69.4 0.0 collective-permute-done.11.cross
  69.4 4.3 %collective-permute-done.10.ends = bf16[1936,128]{1,0:T(8,128)(2,1)S(1)} collective-permute-done((bf16[1936,128]{1,0:T(8,128)(2,1)S(1)}, bf16[1936,128]{1,0:T(8,128)(2,1)S(1)}, u32[]{:S(2)}, u32[]{:S(2)}) %collective-permute-start.10) | collective-permute-done | bytes 495648 | tf_op jit(solution)/shard_map/ppermute | solution.py:338
  73.8 4.6 %shard_map.32 = (bf16[4,8,128,128]{3,2,1,0:T(8,128)(2,1)}, bf16[10,256,2048]{2,1,0:T(8,128)(2,1)S(1)}, bf16[2560,1536]{1,0:T(8,128)(2,1)S(1)}, f32[20,8,128]{2,1,0:T(8,128)S(1)}) custom-call(s32[1]{0:T(128)} %bitcast.place, bf16[10,256,2048]{2,1,0:T(8,128)(2,1)S(1)} %get-tuple-element.28.x_in, ...), custom_call_target="tpu_custom_call", output_to_operand_aliasing={{1}: (1, {}), {2}: (2, {}), {3}: (3, {})} | custom-call | flops 6000000000 | bytes 1000000 | tf_op jit(solution)/shard_map/pallas_call | solution.py:294
  (1 shorter events, 0.0 us)
Async XLA Ops:
  0.0 1.2 %copy-start = (bf16[4,8,128,128]{3,2,1,0:T(8,128)(2,1)S(1)}, bf16[4,8,128,128]{3,2,1,0:T(8,128)(2,1)}, u32[]{:S(2)}) copy-start(bf16[4,8,128,128]{3,2,1,0:T(8,128)(2,1)} %upper.3) | copy-start | bytes 3145732
  1.2 0.7 copy-start.1
  2.7 12.0 %collective-permute-start.3 = (bf16[1936,128]{1,0:T(8,128)(2,1)S(1)}, bf16[1936,128]{1,0:T(8,128)(2,1)S(1)}, u32[]{:S(2)}, u32[]{:S(2)}) collective-permute-start(bf16[1936,128]{1,0:T(8,128)(2,1)S(1)} %get-tuple-element.22.ownb), channel_id=1, source_target_pairs={{1,0},{2,1},{3,2},{5,4},{6,5},{7,6},{9,8},{10,9},{11,10},{13,12},{... | collective-permute-start | bytes 1486856 | tf_op jit(solution)/shard_map/ppermute | solution.py:330
  4.8 13.9 %collective-permute-start = (bf16[1936,128]{1,0:T(8,128)(2,1)S(1)}, bf16[1936,128]{1,0:T(8,128)(2,1)}, u32[]{:S(2)}, u32[]{:S(2)}) collective-permute-start(bf16[1936,128]{1,0:T(8,128)(2,1)S(1)} %get-tuple-element.21._.owna), channel_id=1, source_target_pairs={{0,1},{1,2},{2,3},{4,5},{5,6},{6,7},{8,9},{9,10},{10,11},{12,13},{... | collective-permute-start | bytes 1486856 | tf_op jit(solution)/shard_map/ppermute | solution.py:330
  6.9 22.4 %collective-permute-start.1 = (bf16[1936,128]{1,0:T(8,128)(2,1)S(1)}, bf16[1936,128]{1,0:T(8,128)(2,1)}, u32[]{:S(2)}, u32[]{:S(2)}) collective-permute-start(bf16[1936,128]{1,0:T(8,128)(2,1)S(1)} %get-tuple-element.23), channel_id=1, source_target_pairs={{0,1},{1,2},{2,3},{4,5},{5,6},{6,7},{8,9},{9,10},{10,11},{12,13},{... | collective-permute-start | bytes 1486856 | tf_op jit(solution)/shard_map/ppermute | solution.py:330
  8.2 22.4 %collective-permute-start.2 = (bf16[1936,128]{1,0:T(8,128)(2,1)S(1)}, bf16[1936,128]{1,0:T(8,128)(2,1)}, u32[]{:S(2)}, u32[]{:S(2)}) collective-permute-start(bf16[1936,128]{1,0:T(8,128)(2,1)S(1)} %get-tuple-element.24), channel_id=1, source_target_pairs={{1,0},{2,1},{3,2},{5,4},{6,5},{7,6},{9,8},{10,9},{11,10},{13,12},{... | collective-permute-start | bytes 1486856 | tf_op jit(solution)/shard_map/ppermute | solution.py:330
  14.7 16.6 %collective-permute-start.7 = (bf16[1936,128]{1,0:T(8,128)(2,1)S(1)}, bf16[1936,128]{1,0:T(8,128)(2,1)S(1)}, u32[]{:S(2)}, u32[]{:S(2)}) collective-permute-start(bf16[1936,128]{1,0:T(8,128)(2,1)S(1)} %collective-permute-done.3.bw1b), channel_id=1, source_target_pairs={{1,0},{2,1},{5,4},{6,5},{9,8},{10,9},{13,12},{14,13},{17,16},{18,1... | collective-permute-start | bytes 1486856 | tf_op jit(solution)/shard_map/ppermute | solution.py:330
  18.7 21.1 %collective-permute-start.4 = (bf16[1936,128]{1,0:T(8,128)(2,1)}, bf16[1936,128]{1,0:T(8,128)(2,1)S(1)}, u32[]{:S(2)}, u32[]{:S(2)}) collective-permute-start(bf16[1936,128]{1,0:T(8,128)(2,1)} %collective-permute-done.fw1a), channel_id=1, source_target_pairs={{1,2},{2,3},{5,6},{6,7},{9,10},{10,11},{13,14},{14,15},{17,18},{18... | collective-permute-start | bytes 1486856 | tf_op jit(solution)/shard_map/ppermute | solution.py:330
  29.3 21.1 %collective-permute-start.5 = (bf16[1936,128]{1,0:T(8,128)(2,1)}, bf16[1936,128]{1,0:T(8,128)(2,1)S(1)}, u32[]{:S(2)}, u32[]{:S(2)}) collective-permute-start(bf16[1936,128]{1,0:T(8,128)(2,1)} %collective-permute-done.1.fw1b), channel_id=1, source_target_pairs={{1,2},{2,3},{5,6},{6,7},{9,10},{10,11},{13,14},{14,15},{17,18},{18... | collective-permute-start | bytes 1486856 | tf_op jit(solution)/shard_map/ppermute | solution.py:330
  30.6 19.8 %collective-permute-start.6 = (bf16[1936,128]{1,0:T(8,128)(2,1)}, bf16[1936,128]{1,0:T(8,128)(2,1)S(1)}, u32[]{:S(2)}, u32[]{:S(2)}) collective-permute-start(bf16[1936,128]{1,0:T(8,128)(2,1)} %collective-permute-done.2.bw1a), channel_id=1, source_target_pairs={{1,0},{2,1},{5,4},{6,5},{9,8},{10,9},{13,12},{14,13},{17,16},{18,1... | collective-permute-start | bytes 1486856 | tf_op jit(solution)/shard_map/ppermute | solution.py:330
  39.9 20.5 %collective-permute-start.9 = (bf16[1936,128]{1,0:T(8,128)(2,1)S(1)}, bf16[1936,128]{1,0:T(8,128)(2,1)S(1)}, u32[]{:S(2)}, u32[]{:S(2)}) collective-permute-start(bf16[1936,128]{1,0:T(8,128)(2,1)S(1)} %broadcast_select_fusion.1), channel_id=1, source_target_pairs={{0,4},{1,5},{2,14},{3,15},{4,8},{5,9},{6,2},{7,3},{8,12},{9,13},{1... | collective-permute-start | bytes 1486856 | tf_op jit(solution)/shard_map/ppermute | solution.py:338
  43.3 21.4 %collective-permute-start.8 = (bf16[1936,128]{1,0:T(8,128)(2,1)S(1)}, bf16[1936,128]{1,0:T(8,128)(2,1)S(1)}, u32[]{:S(2)}, u32[]{:S(2)}) collective-permute-start(bf16[1936,128]{1,0:T(8,128)(2,1)S(1)} %broadcast_select_fusion.1), channel_id=1, source_target_pairs={{1,4},{2,15},{5,8},{6,3},{9,12},{10,7},{13,0},{14,11},{17,20},{18,... | collective-permute-start | bytes 1486856 | tf_op jit(solution)/shard_map/ppermute | solution.py:338
  50.5 19.0 %collective-permute-start.11 = (bf16[1040,128]{1,0:T(8,128)(2,1)S(1)}, bf16[1040,128]{1,0:T(8,128)(2,1)S(1)}, u32[]{:S(2)}, u32[]{:S(2)}) collective-permute-start(bf16[1040,128]{1,0:T(8,128)(2,1)S(1)} %slice_select_fusion), channel_id=1, source_target_pairs={{0,4},{1,5},{2,14},{3,15},{4,8},{5,9},{6,2},{7,3},{8,12},{9,13},{1... | collective-permute-start | bytes 798728 | tf_op jit(solution)/shard_map/ppermute | solution.py:338
  53.9 19.9 %collective-permute-start.10 = (bf16[1936,128]{1,0:T(8,128)(2,1)S(1)}, bf16[1936,128]{1,0:T(8,128)(2,1)S(1)}, u32[]{:S(2)}, u32[]{:S(2)}) collective-permute-start(bf16[1936,128]{1,0:T(8,128)(2,1)S(1)} %broadcast_select_fusion), channel_id=1, source_target_pairs={{1,4},{2,15},{5,8},{6,3},{9,12},{10,7},{13,0},{14,11},{17,20},{18,... | collective-permute-start | bytes 1486856 | tf_op jit(solution)/shard_map/ppermute | solution.py:338

commit v7 on v6

--- a/solution.py
+++ b/solution.py
@@ -61,7 +61,7 @@
     return p, q
 
 
-def pack(present, upper, _, *outs):
+def pack(place, present, upper, *outs):
     p, q = triangles()
     right = lax.broadcasted_iota(jnp.int32, (1, B), 1) >= B // 2
 
@@ -69,7 +69,8 @@
         w = present[r, k].astype(jnp.float32)
         return upper[r, k].astype(jnp.float32) * w
 
-    for first, out in zip((0, 2), outs):
+    odd = lax.rem(place[0], 2)
+    for first, out in zip((2 * odd, 2 - 2 * odd), outs):
         one, two = block(first, 0), block(first + 1, 0)
         out[pl.ds(MIXED, B)] = jnp.where(p <= q, one, two).astype(jnp.bfloat16)
         for r in range(2):
@@ -199,7 +200,7 @@
     pl.when(jnp.logical_not(low))(functools.partial(work, HIGH))
 
 
-def stage_0(z_count, place, owna, ownb, fw1a, fw1b, bw1a, bw1b, fw2a, fw2b, bw2a, bw2b, x_ref, y_ref, w_ref):
+def stage_0(z_count, place, own1, own2, a1, a2, b1, b2, ra1, ra2, rb1, rb2, x_ref, y_ref, w_ref):
     zero = jnp.zeros((B, B), jnp.bfloat16)
     for c in range(16):
         set_x(x_ref, 0, c - 7, zero)
@@ -208,23 +209,28 @@
         set_x(x_ref, a, a + 8 if a % 2 == 0 else a - 8, zero)
     z = place[0]
     last = z_count - 1
-    put(x_ref, w_ref, owna, 8)
-    put(x_ref, w_ref, ownb, 10)
     both = (0, 1)
-    take_all(
-        x_ref,
-        w_ref,
-        (
-            (z > 0, fw1a, 4, both, 0),
-            (z > 0, fw1b, 6, both, 0),
-            (z < last, bw1a, 12, both, 0),
-            (z < last, bw1b, 14, both, 0),
-            (z > 1, fw2a, 0, (1,), 0),
-            (z > 1, fw2b, 2, both, 0),
-            (z < last - 1, bw2a, 16, both, 0),
-            (z < last - 1, bw2b, 18, (0,), 0),
-        ),
-    )
+    even = lax.rem(z, 2) == 0
+    for here, (owna, ownb, fw1a, fw1b, bw1a, bw1b, fw2a, fw2b, bw2a, bw2b) in (
+        (even, (own1, own2, b1, b2, a2, a1, rb1, rb2, ra2, ra1)),
+        (jnp.logical_not(even), (own2, own1, a1, a2, b2, b1, ra1, ra2, rb2, rb1)),
+    ):
+        take_all(
+            x_ref,
+            w_ref,
+            (
+                (here, owna, 8, both, 0),
+                (here, ownb, 10, both, 0),
+                (here & (z > 0), fw1a, 4, both, 0),
+                (here & (z > 0), fw1b, 6, both, 0),
+                (here & (z < last), bw1a, 12, both, 0),
+                (here & (z < last), bw1b, 14, both, 0),
+                (here & (z > 1), fw2a, 0, (1,), 0),
+                (here & (z > 1), fw2b, 2, both, 0),
+                (here & (z < last - 1), bw2a, 16, both, 0),
+                (here & (z < last - 1), bw2b, 18, (0,), 0),
+            ),
+        )
 
     def work(late):
         square(late, 0, x_ref, y_ref, w_ref, None)
@@ -309,24 +315,32 @@
     return call(stage_2, z_count, out + KEPT, {1: 1, 2: 2, 3: 3}, 6 * 10**9, place, *got, *rows_2)[0]
 
 
-def packed(present, upper, before):
-    rows = upper.shape[2]
-    pair = jax.ShapeDtypeStruct((PAIR, rows), jnp.bfloat16)
+def copy_pairs(one, two, out_one, out_two):
+    out_one[...] = one[...]
+    out_two[...] = two[...]
+
+
+def pair_call(kernel, limit, specs, *operands):
+    pair = jax.ShapeDtypeStruct((PAIR, B), jnp.bfloat16)
     return pl.pallas_call(
-        pack,
+        kernel,
         out_shape=[pair, pair],
-        in_specs=[SMEM, VMEM, pl.BlockSpec(memory_space=pl.ANY)],
+        in_specs=specs,
         out_specs=[VMEM, VMEM],
-        compiler_params=pltpu.CompilerParams(vmem_limit_bytes=8 * 1024 * 1024),
-    )(present, upper, before)
+        compiler_params=pltpu.CompilerParams(vmem_limit_bytes=limit * 1024 * 1024),
+    )(*operands)
 
 
 def per_device(upper, present):
     s_count, z_count = lax.axis_size("row"), lax.axis_size("col")
     z = lax.axis_index("col")
-
-    def step(block, d, pairs=None):
-        pairs = pairs or [(i, i + d) for i in range(z_count) if 0 <= i + d < z_count]
+    place = z.reshape(1)
+    last = z_count - 1
+
+    def swap(block, odd, inner=False):
+        pairs = [(i, i + 1) for i in range(odd, last, 2)]
+        pairs += [(j, i) for i, j in pairs]
+        pairs = [pair for pair in pairs if not (inner and pair[0] in (0, last))]
         return lax.ppermute(block, "col", pairs)
 
     def hop(block, route):
@@ -337,31 +351,29 @@
         ]
         return lax.ppermute(block, ("row", "col"), pairs)
 
-    last = z_count - 1
-    inner = range(1, last)
-    parts = packed(present, upper, present)
-    again = packed(present, upper, parts[0])
-    fw1 = [step(parts[0], 1), step(again[1], 1)]
-    bw1 = [step(again[0], -1), step(parts[1], -1)]
-    fw2 = [step(part, 1, [(i, i + 1) for i in inner]) for part in fw1]
-    bw2 = [step(part, -1, [(i, i - 1) for i in inner]) for part in bw1]
+    own = pair_call(pack, 40, [SMEM, SMEM, VMEM], place, present, upper)
+    again = pair_call(copy_pairs, 8, [VMEM, VMEM], *own)
+    a1, b1 = swap(own[0], 0), swap(own[1], 1)
+    a2, b2 = swap(again[1], 0), swap(again[0], 1)
+    ra1, rb1 = swap(b1, 0, True), swap(a1, 1)
+    ra2, rb2 = swap(b2, 0, True), swap(a2, 1)
+    edge = (z == 0) | (z == last)
     if z_count == 4:
         to_end, beside = [(1, 1, 0), (2, -1, 3)], [(0, 1, 0), (1, 1, 1), (2, -1, 2), (3, -1, 3)]
-        sooner = jnp.where(z < 2, bw2[1], fw2[0])
-        ends_first = hop(sooner, to_end)
-        cross_first = hop(sooner, beside)
-        down, up = lax.optimization_barrier((bw2[0], fw2[1]))
-        ends_last = hop(jnp.where(z < 2, down, up), to_end)
-        cross_last = hop(jnp.where(z < 2, down[PAIR - ONE :], up[:ONE]), beside)
+        ends_first = hop(rb1, to_end)
+        cross_first = hop(jnp.where(edge, ra1, rb1), beside)
+        ends_last = hop(rb2, to_end)
+        later = jnp.where(edge, ra2, rb2)
+        cross_last = hop(jnp.where(z < 2, later[PAIR - ONE :], later[:ONE]), beside)
     else:
         route = [(last, 1, 0), (0, -1, last)]
-        ends_first = hop(jnp.where(z == last, parts[1], parts[0]), route)
-        ends_last = hop(jnp.where(z == last, parts[0], parts[1]), route)
+        ends_first, ends_last = hop(own[0], route), hop(own[1], route)
         route = [(last - 1, 1, 0), (last, 1, 1), (0, -1, last - 1), (1, -1, last)]
-        cross_first = hop(jnp.where(z < 2, parts[0], parts[1]), route)
-        cross_last = hop(jnp.where(z < 2, parts[1][:ONE], parts[0][PAIR - ONE :]), route)
-    rows = (*parts, *fw1, *bw1, *fw2, *bw2)
-    return compute(z_count, z.reshape(1), rows, (ends_first, cross_first), (ends_last, cross_last))
+        cross_first = hop(jnp.where(edge, own[0], own[1]), route)
+        later = jnp.where(edge, own[1], own[0])
+        cross_last = hop(jnp.where(z < 2, later[:ONE], later[PAIR - ONE :]), route)
+    rows = (*own, a1, a2, b1, b2, ra1, ra2, rb1, rb2)
+    return compute(z_count, place, rows, (ends_first, cross_first), (ends_last, cross_last))
 
 
 def solution(mesh):

time: 78.8 us -> 74.9 us (0.951)
  starting transfers between devices: 23.4 us -> 17 us
  waiting for transfers between devices: 36.7 us -> 39.9 us
    ppermute x8, starting transfers between devices: 14.1 us -> 8.95 us  [swap(): return lax.ppermute(block, 'col', pairs)]
    ppermute x8, waiting for transfers between devices: 28.1 us -> 30.9 us  [swap(): return lax.ppermute(block, 'col', pairs)]
    ppermute x4, starting transfers between devices: 9.34 us -> 8.05 us  [hop(): return lax.ppermute(block, ('row', 'col'), pairs)]
  transfers between devices with their start and end apart: 12 -> 12, of which waited for: 7 -> 6; matrix products, arithmetic and copies ran while one was open for 0% -> 0% of each run, Pallas kernels for 14% -> 13%
where the time goes in v7:
time: 74.9 us; the launch traced here: 74.5 us
  waiting for transfers between devices  39.9 us (53%)
  starting transfers between devices  17 us (23%)
  Pallas kernels  15.4 us (21%)
  local copies, waits for them, and re-layouts  1.91 us (3%)
    ppermute x8, waiting for transfers between devices, swap(): return lax.ppermute(block, 'col', pairs)  30.9 us
    pallas_call x3, Pallas kernels, call(): pl.pallas_call(functools.partial(kernel, z_count), out_shape=outs, in_spe...  14.5 us
    ppermute x8, starting transfers between devices, swap(): return lax.ppermute(block, 'col', pairs)  8.95 us
    ppermute x4, waiting for transfers between devices, hop(): return lax.ppermute(block, ('row', 'col'), pairs)  8.94 us
    ppermute x4, starting transfers between devices, hop(): return lax.ppermute(block, ('row', 'col'), pairs)  8.05 us
    unnamed x4, local copies, waits for them, and re-layouts  1.91 us
  transfers between devices with their start and end apart: 12, of which 6 were waited for; matrix products, arithmetic and copies ran while one was open for 0% of the time, Pallas kernels for 13%

profile of v7, /device:TPU:25, one launch (start us, length us, event | category | flops | bytes accessed | tf_op | source)
XLA Modules:
  0.0 74.5 jit_solution(17961090365970994274)
XLA Ops:
  0.0 0.0 copy-start
  0.0 1.2 %copy-done = bf16[4,8,128,128]{3,2,1,0:T(8,128)(2,1)S(1)} copy-done((bf16[4,8,128,128]{3,2,1,0:T(8,128)(2,1)S(1)}, bf16[4,8,128,128]{3,2,1,0:T(8,128)(2,1)}, u32[]{:S(2)}) %copy-start) | copy-done | bytes 1048600
  1.2 0.0 copy-start.1
  1.2 0.7 copy-done.1
  1.9 0.8 %shard_map.28 = (bf16[1936,128]{1,0:T(8,128)(2,1)S(1)}, bf16[1936,128]{1,0:T(8,128)(2,1)S(1)}) custom-call(s32[1]{0:T(128)} %bitcast.place, s32[4,8]{1,0:T(4,128)S(1)} %copy-done.1, bf16[4,8,128,128]{3,2,1,0:T(8,128)(2,1)S(1)} %copy-done), custom_call_target="tpu_custom_call" | custom-call | tf_op jit(solution)/shard_map/pallas_call | solution.py:325
  2.7 0.2 collective-permute-start
  2.9 1.4 %collective-permute-start.2 = (bf16[1936,128]{1,0:T(8,128)(2,1)S(1)}, bf16[1936,128]{1,0:T(8,128)(2,1)}, u32[]{:S(2)}, u32[]{:S(2)}) collective-permute-start(bf16[1936,128]{1,0:T(8,128)(2,1)S(1)} %get-tuple-element.20.two.own2), channel_id=1, source_target_pairs={{1,2},{2,1},{5,6},{6,5},{9,10},{10,9},{13,14},{14,13},{17,18},{18,... | collective-permute-start | bytes 1486856 | tf_op jit(solution)/shard_map/ppermute | solution.py:344
  4.4 0.1 shard_map.29
  4.4 1.8 %collective-permute-start.1 = (bf16[1936,128]{1,0:T(8,128)(2,1)S(1)}, bf16[1936,128]{1,0:T(8,128)(2,1)}, u32[]{:S(2)}, u32[]{:S(2)}) collective-permute-start(bf16[1936,128]{1,0:T(8,128)(2,1)S(1)} %get-tuple-element.21), channel_id=1, source_target_pairs={{0,1},{2,3},{1,0},{3,2},{4,5},{6,7},{5,4},{7,6},{8,9},{10,11},{9,8... | collective-permute-start | bytes 1486856 | tf_op jit(solution)/shard_map/ppermute | solution.py:344
  6.3 1.5 %collective-permute-start.3 = (bf16[1936,128]{1,0:T(8,128)(2,1)S(1)}, bf16[1936,128]{1,0:T(8,128)(2,1)}, u32[]{:S(2)}, u32[]{:S(2)}) collective-permute-start(bf16[1936,128]{1,0:T(8,128)(2,1)S(1)} %get-tuple-element.22), channel_id=1, source_target_pairs={{1,2},{2,1},{5,6},{6,5},{9,10},{10,9},{13,14},{14,13},{17,18},{18,... | collective-permute-start | bytes 1486856 | tf_op jit(solution)/shard_map/ppermute | solution.py:344
  7.8 7.2 %collective-permute-done.a1 = bf16[1936,128]{1,0:T(8,128)(2,1)S(1)} collective-permute-done((bf16[1936,128]{1,0:T(8,128)(2,1)S(1)}, bf16[1936,128]{1,0:T(8,128)(2,1)S(1)}, u32[]{:S(2)}, u32[]{:S(2)}) %collective-permute-start) | collective-permute-done | bytes 495648 | tf_op jit(solution)/shard_map/ppermute | solution.py:344
  14.9 0.7 collective-permute-start.6
  15.6 0.0 collective-permute-done.2.b1
  15.6 1.3 %collective-permute-start.4 = (bf16[1936,128]{1,0:T(8,128)(2,1)}, bf16[1936,128]{1,0:T(8,128)(2,1)S(1)}, u32[]{:S(2)}, u32[]{:S(2)}) collective-permute-start(bf16[1936,128]{1,0:T(8,128)(2,1)} %collective-permute-done.2.b1), channel_id=1, source_target_pairs={{2,3},{1,0},{6,7},{5,4},{10,11},{9,8},{14,15},{13,12},{18,19},{17,... | collective-permute-start | bytes 1486856 | tf_op jit(solution)/shard_map/ppermute | solution.py:344
  16.9 8.7 %collective-permute-done.1.a2 = bf16[1936,128]{1,0:T(8,128)(2,1)} collective-permute-done((bf16[1936,128]{1,0:T(8,128)(2,1)S(1)}, bf16[1936,128]{1,0:T(8,128)(2,1)}, u32[]{:S(2)}, u32[]{:S(2)}) %collective-permute-start.1) | collective-permute-done | bytes 495648 | tf_op jit(solution)/shard_map/ppermute | solution.py:344
  25.7 0.7 collective-permute-start.7
  26.4 0.0 collective-permute-done.3.b2
  26.4 1.3 %collective-permute-start.5 = (bf16[1936,128]{1,0:T(8,128)(2,1)}, bf16[1936,128]{1,0:T(8,128)(2,1)S(1)}, u32[]{:S(2)}, u32[]{:S(2)}) collective-permute-start(bf16[1936,128]{1,0:T(8,128)(2,1)} %collective-permute-done.3.b2), channel_id=1, source_target_pairs={{2,3},{1,0},{6,7},{5,4},{10,11},{9,8},{14,15},{13,12},{18,19},{17,... | collective-permute-start | bytes 1486856 | tf_op jit(solution)/shard_map/ppermute | solution.py:344
  27.7 0.0 collective-permute-done.6.rb1
  27.7 8.5 %collective-permute-done.4.ra1 = bf16[1936,128]{1,0:T(8,128)(2,1)S(1)} collective-permute-done((bf16[1936,128]{1,0:T(8,128)(2,1)}, bf16[1936,128]{1,0:T(8,128)(2,1)S(1)}, u32[]{:S(2)}, u32[]{:S(2)}) %collective-permute-start.4) | collective-permute-done | bytes 495648 | tf_op jit(solution)/shard_map/ppermute | solution.py:344
  36.2 0.1 broadcast_select_fusion.1
  36.2 2.7 %collective-permute-start.9 = (bf16[1936,128]{1,0:T(8,128)(2,1)S(1)}, bf16[1936,128]{1,0:T(8,128)(2,1)S(1)}, u32[]{:S(2)}, u32[]{:S(2)}) collective-permute-start(bf16[1936,128]{1,0:T(8,128)(2,1)S(1)} %broadcast_select_fusion.1), channel_id=1, source_target_pairs={{0,4},{1,5},{2,14},{3,15},{4,8},{5,9},{6,2},{7,3},{8,12},{9,13},{1... | collective-permute-start | bytes 1486856 | tf_op jit(solution)/shard_map/ppermute | solution.py:352
  39.0 1.3 %collective-permute-start.8 = (bf16[1936,128]{1,0:T(8,128)(2,1)S(1)}, bf16[1936,128]{1,0:T(8,128)(2,1)S(1)}, u32[]{:S(2)}, u32[]{:S(2)}) collective-permute-start(bf16[1936,128]{1,0:T(8,128)(2,1)S(1)} %collective-permute-done.6.rb1), channel_id=1, source_target_pairs={{1,4},{2,15},{5,8},{6,3},{9,12},{10,7},{13,0},{14,11},{17,20},{18,... | collective-permute-start | bytes 1486856 | tf_op jit(solution)/shard_map/ppermute | solution.py:352
  40.3 0.0 collective-permute-done.7.rb2
  40.3 6.5 %collective-permute-done.5.ra2 = bf16[1936,128]{1,0:T(8,128)(2,1)S(1)} collective-permute-done((bf16[1936,128]{1,0:T(8,128)(2,1)}, bf16[1936,128]{1,0:T(8,128)(2,1)S(1)}, u32[]{:S(2)}, u32[]{:S(2)}) %collective-permute-start.5) | collective-permute-done | bytes 495648 | tf_op jit(solution)/shard_map/ppermute | solution.py:344
  46.8 0.1 broadcast_select_fusion
  46.9 2.7 %collective-permute-start.11 = (bf16[1040,128]{1,0:T(8,128)(2,1)S(1)}, bf16[1040,128]{1,0:T(8,128)(2,1)S(1)}, u32[]{:S(2)}, u32[]{:S(2)}) collective-permute-start(bf16[1040,128]{1,0:T(8,128)(2,1)S(1)} %slice_select_fusion), channel_id=1, source_target_pairs={{0,4},{1,5},{2,14},{3,15},{4,8},{5,9},{6,2},{7,3},{8,12},{9,13},{1... | collective-permute-start | bytes 798728 | tf_op jit(solution)/shard_map/ppermute | solution.py:352
  49.7 1.3 %collective-permute-start.10 = (bf16[1936,128]{1,0:T(8,128)(2,1)S(1)}, bf16[1936,128]{1,0:T(8,128)(2,1)S(1)}, u32[]{:S(2)}, u32[]{:S(2)}) collective-permute-start(bf16[1936,128]{1,0:T(8,128)(2,1)S(1)} %collective-permute-done.7.rb2), channel_id=1, source_target_pairs={{1,4},{2,15},{5,8},{6,3},{9,12},{10,7},{13,0},{14,11},{17,20},{18,... | collective-permute-start | bytes 1486856 | tf_op jit(solution)/shard_map/ppermute | solution.py:352
  50.9 5.1 %shard_map.30 = (bf16[10,256,2048]{2,1,0:T(8,128)(2,1)S(1)}, bf16[2560,1536]{1,0:T(8,128)(2,1)S(1)}, f32[20,8,128]{2,1,0:T(8,128)S(1)}) custom-call(s32[1]{0:T(128)} %bitcast.place, bf16[1936,128]{1,0:T(8,128)(2,1)S(1)} %get-tuple-element.19.one.own1, bf16[1936,128]{1,0:T(8,128)(2,1)S(1)} %get-tuple-element.20.two.own2, ...), custom_call_target="tpu_custom_call" | custom-call | flops 1000000000 | bytes 1000000 | tf_op jit(solution)/shard_map/pallas_call | solution.py:300
  56.1 4.3 %collective-permute-done.8.ends = bf16[1936,128]{1,0:T(8,128)(2,1)S(1)} collective-permute-done((bf16[1936,128]{1,0:T(8,128)(2,1)S(1)}, bf16[1936,128]{1,0:T(8,128)(2,1)S(1)}, u32[]{:S(2)}, u32[]{:S(2)}) %collective-permute-start.8) | collective-permute-done | bytes 495648 | tf_op jit(solution)/shard_map/ppermute | solution.py:352
  60.4 0.0 collective-permute-done.9.cross
  60.4 4.8 %shard_map.31 = (bf16[10,256,2048]{2,1,0:T(8,128)(2,1)S(1)}, bf16[2560,1536]{1,0:T(8,128)(2,1)S(1)}, f32[20,8,128]{2,1,0:T(8,128)S(1)}, f32[15,256,256]{2,1,0:T(...) custom-call(s32[1]{0:T(128)} %bitcast.place, ...), custom_call_target="tpu_custom_call", output_to_operand_aliasing={{0}: (1, {}), {1}: (2, {}), {2}: (3, {})} | custom-call | flops 6000000000 | bytes 1000000 | tf_op jit(solution)/shard_map/pallas_call | solution.py:300
  65.2 0.0 collective-permute-done.11.cross
  65.2 4.7 %collective-permute-done.10.ends = bf16[1936,128]{1,0:T(8,128)(2,1)S(1)} collective-permute-done((bf16[1936,128]{1,0:T(8,128)(2,1)S(1)}, bf16[1936,128]{1,0:T(8,128)(2,1)S(1)}, u32[]{:S(2)}, u32[]{:S(2)}) %collective-permute-start.10) | collective-permute-done | bytes 495648 | tf_op jit(solution)/shard_map/ppermute | solution.py:352
  69.8 4.6 %shard_map.32 = (bf16[4,8,128,128]{3,2,1,0:T(8,128)(2,1)}, bf16[10,256,2048]{2,1,0:T(8,128)(2,1)S(1)}, bf16[2560,1536]{1,0:T(8,128)(2,1)S(1)}, f32[20,8,128]{2,1,0:T(8,128)S(1)}) custom-call(s32[1]{0:T(128)} %bitcast.place, bf16[10,256,2048]{2,1,0:T(8,128)(2,1)S(1)} %get-tuple-element.26.x_in, ...), custom_call_target="tpu_custom_call", output_to_operand_aliasing={{1}: (1, {}), {2}: (2, {}), {3}: (3, {})} | custom-call | flops 6000000000 | bytes 1000000 | tf_op jit(solution)/shard_map/pallas_call | solution.py:300
  (1 shorter events, 0.0 us)
Async XLA Ops:
  0.0 1.2 %copy-start = (bf16[4,8,128,128]{3,2,1,0:T(8,128)(2,1)S(1)}, bf16[4,8,128,128]{3,2,1,0:T(8,128)(2,1)}, u32[]{:S(2)}) copy-start(bf16[4,8,128,128]{3,2,1,0:T(8,128)(2,1)} %upper.1) | copy-start | bytes 3145732
  1.2 0.7 copy-start.1
  2.7 12.2 %collective-permute-start = (bf16[1936,128]{1,0:T(8,128)(2,1)S(1)}, bf16[1936,128]{1,0:T(8,128)(2,1)S(1)}, u32[]{:S(2)}, u32[]{:S(2)}) collective-permute-start(bf16[1936,128]{1,0:T(8,128)(2,1)S(1)} %get-tuple-element.19.one.own1), channel_id=1, source_target_pairs={{0,1},{2,3},{1,0},{3,2},{4,5},{6,7},{5,4},{7,6},{8,9},{10,11},{9,8... | collective-permute-start | bytes 1486856 | tf_op jit(solution)/shard_map/ppermute | solution.py:344
  2.9 12.7 %collective-permute-start.2 = (bf16[1936,128]{1,0:T(8,128)(2,1)S(1)}, bf16[1936,128]{1,0:T(8,128)(2,1)}, u32[]{:S(2)}, u32[]{:S(2)}) collective-permute-start(bf16[1936,128]{1,0:T(8,128)(2,1)S(1)} %get-tuple-element.20.two.own2), channel_id=1, source_target_pairs={{1,2},{2,1},{5,6},{6,5},{9,10},{10,9},{13,14},{14,13},{17,18},{18,... | collective-permute-start | bytes 1486856 | tf_op jit(solution)/shard_map/ppermute | solution.py:344
  4.4 21.2 %collective-permute-start.1 = (bf16[1936,128]{1,0:T(8,128)(2,1)S(1)}, bf16[1936,128]{1,0:T(8,128)(2,1)}, u32[]{:S(2)}, u32[]{:S(2)}) collective-permute-start(bf16[1936,128]{1,0:T(8,128)(2,1)S(1)} %get-tuple-element.21), channel_id=1, source_target_pairs={{0,1},{2,3},{1,0},{3,2},{4,5},{6,7},{5,4},{7,6},{8,9},{10,11},{9,8... | collective-permute-start | bytes 1486856 | tf_op jit(solution)/shard_map/ppermute | solution.py:344
  6.3 20.1 %collective-permute-start.3 = (bf16[1936,128]{1,0:T(8,128)(2,1)S(1)}, bf16[1936,128]{1,0:T(8,128)(2,1)}, u32[]{:S(2)}, u32[]{:S(2)}) collective-permute-start(bf16[1936,128]{1,0:T(8,128)(2,1)S(1)} %get-tuple-element.22), channel_id=1, source_target_pairs={{1,2},{2,1},{5,6},{6,5},{9,10},{10,9},{13,14},{14,13},{17,18},{18,... | collective-permute-start | bytes 1486856 | tf_op jit(solution)/shard_map/ppermute | solution.py:344
  14.9 12.7 %collective-permute-start.6 = (bf16[1936,128]{1,0:T(8,128)(2,1)S(1)}, bf16[1936,128]{1,0:T(8,128)(2,1)S(1)}, u32[]{:S(2)}, u32[]{:S(2)}) collective-permute-start(bf16[1936,128]{1,0:T(8,128)(2,1)S(1)} %collective-permute-done.a1), channel_id=1, source_target_pairs={{1,2},{2,1},{5,6},{6,5},{9,10},{10,9},{13,14},{14,13},{17,18},{18,... | collective-permute-start | bytes 1486856 | tf_op jit(solution)/shard_map/ppermute | solution.py:344
  15.6 20.5 %collective-permute-start.4 = (bf16[1936,128]{1,0:T(8,128)(2,1)}, bf16[1936,128]{1,0:T(8,128)(2,1)S(1)}, u32[]{:S(2)}, u32[]{:S(2)}) collective-permute-start(bf16[1936,128]{1,0:T(8,128)(2,1)} %collective-permute-done.2.b1), channel_id=1, source_target_pairs={{2,3},{1,0},{6,7},{5,4},{10,11},{9,8},{14,15},{13,12},{18,19},{17,... | collective-permute-start | bytes 1486856 | tf_op jit(solution)/shard_map/ppermute | solution.py:344
  25.7 14.6 %collective-permute-start.7 = (bf16[1936,128]{1,0:T(8,128)(2,1)}, bf16[1936,128]{1,0:T(8,128)(2,1)S(1)}, u32[]{:S(2)}, u32[]{:S(2)}) collective-permute-start(bf16[1936,128]{1,0:T(8,128)(2,1)} %collective-permute-done.1.a2), channel_id=1, source_target_pairs={{1,2},{2,1},{5,6},{6,5},{9,10},{10,9},{13,14},{14,13},{17,18},{18,... | collective-permute-start | bytes 1486856 | tf_op jit(solution)/shard_map/ppermute | solution.py:344
  26.4 20.4 %collective-permute-start.5 = (bf16[1936,128]{1,0:T(8,128)(2,1)}, bf16[1936,128]{1,0:T(8,128)(2,1)S(1)}, u32[]{:S(2)}, u32[]{:S(2)}) collective-permute-start(bf16[1936,128]{1,0:T(8,128)(2,1)} %collective-permute-done.3.b2), channel_id=1, source_target_pairs={{2,3},{1,0},{6,7},{5,4},{10,11},{9,8},{14,15},{13,12},{18,19},{17,... | collective-permute-start | bytes 1486856 | tf_op jit(solution)/shard_map/ppermute | solution.py:344
  36.2 24.1 %collective-permute-start.9 = (bf16[1936,128]{1,0:T(8,128)(2,1)S(1)}, bf16[1936,128]{1,0:T(8,128)(2,1)S(1)}, u32[]{:S(2)}, u32[]{:S(2)}) collective-permute-start(bf16[1936,128]{1,0:T(8,128)(2,1)S(1)} %broadcast_select_fusion.1), channel_id=1, source_target_pairs={{0,4},{1,5},{2,14},{3,15},{4,8},{5,9},{6,2},{7,3},{8,12},{9,13},{1... | collective-permute-start | bytes 1486856 | tf_op jit(solution)/shard_map/ppermute | solution.py:352
  39.0 21.4 %collective-permute-start.8 = (bf16[1936,128]{1,0:T(8,128)(2,1)S(1)}, bf16[1936,128]{1,0:T(8,128)(2,1)S(1)}, u32[]{:S(2)}, u32[]{:S(2)}) collective-permute-start(bf16[1936,128]{1,0:T(8,128)(2,1)S(1)} %collective-permute-done.6.rb1), channel_id=1, source_target_pairs={{1,4},{2,15},{5,8},{6,3},{9,12},{10,7},{13,0},{14,11},{17,20},{18,... | collective-permute-start | bytes 1486856 | tf_op jit(solution)/shard_map/ppermute | solution.py:352
  46.9 18.2 %collective-permute-start.11 = (bf16[1040,128]{1,0:T(8,128)(2,1)S(1)}, bf16[1040,128]{1,0:T(8,128)(2,1)S(1)}, u32[]{:S(2)}, u32[]{:S(2)}) collective-permute-start(bf16[1040,128]{1,0:T(8,128)(2,1)S(1)} %slice_select_fusion), channel_id=1, source_target_pairs={{0,4},{1,5},{2,14},{3,15},{4,8},{5,9},{6,2},{7,3},{8,12},{9,13},{1... | collective-permute-start | bytes 798728 | tf_op jit(solution)/shard_map/ppermute | solution.py:352
  49.7 20.2 %collective-permute-start.10 = (bf16[1936,128]{1,0:T(8,128)(2,1)S(1)}, bf16[1936,128]{1,0:T(8,128)(2,1)S(1)}, u32[]{:S(2)}, u32[]{:S(2)}) collective-permute-start(bf16[1936,128]{1,0:T(8,128)(2,1)S(1)} %collective-permute-done.7.rb2), channel_id=1, source_target_pairs={{1,4},{2,15},{5,8},{6,3},{9,12},{10,7},{13,0},{14,11},{17,20},{18,... | collective-permute-start | bytes 1486856 | tf_op jit(solution)/shard_map/ppermute | solution.py:352

commit v8 on v7

--- a/solution.py
+++ b/solution.py
@@ -17,8 +17,8 @@
 PAIR = 15 * B + 16
 ONE = SECOND
 
-LOW = {1: 2, 2: 1, 3: 1, 4: 2, 5: 2, 6: 1, 7: 1}
-HIGH = {12: 1, 13: 1, 14: 2, 15: 2, 16: 1, 17: 1, 18: 2}
+LOW = {1: 1, 2: 1, 3: 1, 4: 2, 5: 2, 6: 1, 7: 1}
+HIGH = {12: 1, 13: 1, 14: 2, 15: 2, 16: 1, 17: 1, 18: 1}
 
 
 def blk(a, n=1):
@@ -61,7 +61,7 @@
     return p, q
 
 
-def pack(place, present, upper, *outs):
+def pack(present, upper, *outs):
     p, q = triangles()
     right = lax.broadcasted_iota(jnp.int32, (1, B), 1) >= B // 2
 
@@ -69,7 +69,7 @@
         w = present[r, k].astype(jnp.float32)
         return upper[r, k].astype(jnp.float32) * w
 
-    odd = lax.rem(place[0], 2)
+    odd = lax.rem(lax.axis_index("col"), 2)
     for first, out in zip((2 * odd, 2 - 2 * odd), outs):
         one, two = block(first, 0), block(first + 1, 0)
         out[pl.ds(MIXED, B)] = jnp.where(p <= q, one, two).astype(jnp.bfloat16)
@@ -150,7 +150,7 @@
                         ).astype(jnp.bfloat16)
 
 
-def purify(late, now, x_ref, y_ref, w_ref, part_ref, out, done):
+def purify(late, now, x_ref, y_ref, w_ref, part_ref, ready, send=None):
     for I in (4, 5):
         for L in range(I, I + 5):
             terms = cube_terms(late, I, L)
@@ -175,18 +175,21 @@
             if now == 2 and end == 2 and len(mine) < len(terms):
                 c = c + part_ref[place]
             for di in range(2):
-                for dl in range(2):
-                    i, l = 2 * I + di, 2 * L + dl
-                    off = l - i
-                    if not 0 <= off <= 7:
-                        continue
+                i = 2 * I + di
+                offsets = [off for off in (2 * L - i, 2 * L + 1 - i) if 0 <= off <= 7]
+                if not offsets:
+                    continue
+                for off in offsets:
                     if now == 2 and end < 2:
-                        out[i - 8, off] = done[i - 8, off]
-                        continue
+                        break
+                    l = i + off
+                    dl = l - 2 * L
                     w = w_ref[i, pl.ds(off, 1)]
                     sq = y_ref[blk(i), blk(l - 8)].astype(jnp.float32)
                     cube = w * c[di * B : (di + 1) * B, dl * B : (dl + 1) * B]
-                    out[i - 8, off] = (3.0 * sq - 2.0 * cube).astype(jnp.bfloat16)
+                    ready[i - 8, off] = (3.0 * sq - 2.0 * cube).astype(jnp.bfloat16)
+                if send is not None:
+                    send(end < 2, (place, di), i - 8, offsets[0], len(offsets))
 
 
 def take_all(x_ref, w_ref, pieces):
@@ -200,14 +203,14 @@
     pl.when(jnp.logical_not(low))(functools.partial(work, HIGH))
 
 
-def stage_0(z_count, place, own1, own2, a1, a2, b1, b2, ra1, ra2, rb1, rb2, x_ref, y_ref, w_ref):
+def stage_0(z_count, own1, own2, a1, a2, b1, b2, ra1, ra2, rb1, rb2, x_ref, y_ref, w_ref):
     zero = jnp.zeros((B, B), jnp.bfloat16)
     for c in range(16):
         set_x(x_ref, 0, c - 7, zero)
         set_x(x_ref, 19, c + 11, zero)
     for a in range(1, 19):
         set_x(x_ref, a, a + 8 if a % 2 == 0 else a - 8, zero)
-    z = place[0]
+    z = lax.axis_index("col")
     last = z_count - 1
     both = (0, 1)
     even = lax.rem(z, 2) == 0
@@ -238,8 +241,8 @@
     for_half(z, z_count, work)
 
 
-def stage_1(z_count, place, x_in, y_in, w_in, ends, cross, x_ref, y_ref, w_ref, sums, cubes, done):
-    z = place[0]
+def stage_1(z_count, x_in, y_in, w_in, ends, cross, line, x_ref, y_ref, w_ref, sums, cubes, done):
+    z = lax.axis_index("col")
     last = z_count - 1
     both = (0, 1)
     take_all(
@@ -250,18 +253,20 @@
             (z == last, ends, 12, both, 0),
             (z <= 1, cross, 2, both, 0),
             (z >= last - 1, cross, 16, both, 0),
+            (z <= 1, line, 0, (1,), MIXED),
+            (z >= last - 1, line, 18, (0,), 0),
         ),
     )
 
     def work(late):
         square(late, 1, x_ref, y_ref, w_ref, sums)
-        purify(late, 1, x_ref, y_ref, w_ref, cubes, done, None)
+        purify(late, 1, x_ref, y_ref, w_ref, cubes, done)
 
     for_half(z, z_count, work)
 
 
-def stage_2(z_count, place, x_in, y_in, w_in, sums, cubes, done, ends, cross, out, x_ref, y_ref, w_ref):
-    z = place[0]
+def stage_2(z_count, x_in, y_in, w_in, sums, cubes, done, ends, x_ref, y_ref, w_ref, out, ready, sems):
+    z = lax.axis_index("col")
     last = z_count - 1
     both = (0, 1)
     take_all(
@@ -270,14 +275,24 @@
         (
             (z == 0, ends, 4, both, 0),
             (z == last, ends, 14, both, 0),
-            (z <= 1, cross, 0, (1,), MIXED),
-            (z >= last - 1, cross, 18, (0,), 0),
         ),
     )
 
     def work(late):
+        copies = []
+
+        def send(early, place, i, offset, count):
+            part = pl.ds(offset, count)
+            copy = pltpu.make_async_copy(
+                (done if early else ready).at[i, part], out.at[i, part], sems.at[place]
+            )
+            copy.start()
+            copies.append(copy)
+
         square(late, 2, x_ref, y_ref, w_ref, sums)
-        purify(late, 2, x_ref, y_ref, w_ref, cubes, out, done)
+        purify(late, 2, x_ref, y_ref, w_ref, cubes, ready, send)
+        for copy in copies:
+            copy.wait()
 
     for_half(z, z_count, work)
 
@@ -296,23 +311,28 @@
 ]
 
 
-def call(kernel, z_count, outs, aliases, flops, *operands):
+def call(kernel, z_count, outs, specs, aliases, scratch, flops, *operands):
     return pl.pallas_call(
         functools.partial(kernel, z_count),
         out_shape=outs,
-        in_specs=[SMEM] + [VMEM] * (len(operands) - 1),
-        out_specs=[VMEM] * len(outs),
+        in_specs=[VMEM] * len(operands),
+        out_specs=specs,
         input_output_aliases=aliases,
+        scratch_shapes=scratch,
         compiler_params=pltpu.CompilerParams(vmem_limit_bytes=16 * 1024 * 1024),
         cost_estimate=pl.CostEstimate(flops=flops, bytes_accessed=10**6, transcendentals=0),
     )(*operands)
 
 
-def compute(z_count, place, rows_0, rows_1, rows_2):
-    kept = call(stage_0, z_count, KEPT, {}, 10**9, place, *rows_0)
-    got = call(stage_1, z_count, KEPT + PARTIAL, {1: 0, 2: 1, 3: 2}, 6 * 10**9, place, *kept, *rows_1)
-    out = [jax.ShapeDtypeStruct((4, 8, B, B), jnp.bfloat16)]
-    return call(stage_2, z_count, out + KEPT, {1: 1, 2: 2, 3: 3}, 6 * 10**9, place, *got, *rows_2)[0]
+def compute(z_count, rows_0, rows_1, rows_2):
+    kept = call(stage_0, z_count, KEPT, [VMEM] * 3, {}, [], 10**9, *rows_0)
+    aliases = {0: 0, 1: 1, 2: 2}
+    outs = KEPT + PARTIAL
+    got = call(stage_1, z_count, outs, [VMEM] * 6, aliases, [], 6 * 10**9, *kept, *rows_1)
+    outs = KEPT + [jax.ShapeDtypeStruct((4, 8, B, B), jnp.bfloat16)]
+    specs = [VMEM] * 3 + [pl.BlockSpec(memory_space=pl.ANY)]
+    scratch = [pltpu.VMEM((4, 8, B, B), jnp.bfloat16), pltpu.SemaphoreType.DMA((10, 2))]
+    return call(stage_2, z_count, outs, specs, aliases, scratch, 6 * 10**9, *got, *rows_2)[3]
 
 
 def copy_pairs(one, two, out_one, out_two):
@@ -334,7 +354,6 @@
 def per_device(upper, present):
     s_count, z_count = lax.axis_size("row"), lax.axis_size("col")
     z = lax.axis_index("col")
-    place = z.reshape(1)
     last = z_count - 1
 
     def swap(block, odd, inner=False):
@@ -351,7 +370,7 @@
         ]
         return lax.ppermute(block, ("row", "col"), pairs)
 
-    own = pair_call(pack, 40, [SMEM, SMEM, VMEM], place, present, upper)
+    own = pair_call(pack, 60, [SMEM, VMEM], present, upper)
     again = pair_call(copy_pairs, 8, [VMEM, VMEM], *own)
     a1, b1 = swap(own[0], 0), swap(own[1], 1)
     a2, b2 = swap(again[1], 0), swap(again[0], 1)
@@ -373,7 +392,7 @@
         later = jnp.where(edge, own[1], own[0])
         cross_last = hop(jnp.where(z < 2, later[:ONE], later[PAIR - ONE :]), route)
     rows = (*own, a1, a2, b1, b2, ra1, ra2, rb1, rb2)
-    return compute(z_count, place, rows, (ends_first, cross_first), (ends_last, cross_last))
+    return compute(z_count, rows, (ends_first, cross_first, cross_last), (ends_last,))
 
 
 def solution(mesh):

time: 74.9 us -> 74.2 us (level)
  waiting for transfers between devices: 39.9 us -> 35.7 us
  local copies, waits for them, and re-layouts: 1.91 us -> 4.12 us
  Pallas kernels: 15.4 us -> 16.4 us
    ppermute x4, waiting for transfers between devices: 8.94 us -> 6.65 us  [hop(): return lax.ppermute(block, ('row', 'col'), pairs)]
    unnamed x4 -> x8, local copies, waits for them, and re-layouts: 1.91 us -> 4.12 us
    ppermute x8, waiting for transfers between devices: 30.9 us -> 29.1 us  [swap(): return lax.ppermute(block, 'col', pairs)]
    pallas_call x2, Pallas kernels: 0.85 us -> 2.37 us  [pair_call(): pl.pallas_call(kernel, out_shape=[pair, pair], in_specs=specs, out_specs=...]
  transfers between devices with their start and end apart: 12 -> 12, of which waited for: 6 -> 7; matrix products, arithmetic and copies ran while one was open for 0% -> 0% of each run, Pallas kernels for 13% -> 14%
where the time goes in v8:
time: 74.2 us; the launch traced here: 73.7 us
  waiting for transfers between devices  35.7 us (48%)
  starting transfers between devices  16.9 us (23%)
  Pallas kernels  16.4 us (22%)
  local copies, waits for them, and re-layouts  4.12 us (6%)
    ppermute x8, waiting for transfers between devices, swap(): return lax.ppermute(block, 'col', pairs)  29.1 us
    pallas_call x3, Pallas kernels, call(): pl.pallas_call(functools.partial(kernel, z_count), out_shape=outs, in_spe...  14.1 us
    ppermute x8, starting transfers between devices, swap(): return lax.ppermute(block, 'col', pairs)  8.84 us
    ppermute x4, starting transfers between devices, hop(): return lax.ppermute(block, ('row', 'col'), pairs)  8.05 us
    ppermute x4, waiting for transfers between devices, hop(): return lax.ppermute(block, ('row', 'col'), pairs)  6.65 us
    unnamed x8, local copies, waits for them, and re-layouts  4.12 us
    pallas_call x2, Pallas kernels, pair_call(): pl.pallas_call(kernel, out_shape=[pair, pair], in_specs=specs, out_specs=...  2.37 us
  transfers between devices with their start and end apart: 12, of which 7 were waited for; matrix products, arithmetic and copies ran while one was open for 0% of the time, Pallas kernels for 14%

profile of v8, /device:TPU:25, one launch (start us, length us, event | category | flops | bytes accessed | tf_op | source)
XLA Modules:
  0.0 73.7 jit_solution(14619442170555286675)
XLA Ops:
  0.0 2.3 %shard_map.28 = (bf16[1936,128]{1,0:T(8,128)(2,1)}, bf16[1936,128]{1,0:T(8,128)(2,1)}) custom-call(s32[4,8]{1,0:T(4,128)} %present.1, bf16[4,8,128,128]{3,2,1,0:T(8,128)(2,1)} %upper.1), custom_call_target="tpu_custom_call" | custom-call | tf_op jit(solution)/shard_map/pallas_call | solution.py:345
  2.3 0.2 collective-permute-start
  2.5 0.7 collective-permute-start.2
  3.2 0.0 copy-start
  3.2 1.0 %copy-done = bf16[1936,128]{1,0:T(8,128)(2,1)S(1)} copy-done((bf16[1936,128]{1,0:T(8,128)(2,1)S(1)}, bf16[1936,128]{1,0:T(8,128)(2,1)}, u32[]{:S(2)}) %copy-start) | copy-done | bytes 495640
  4.2 0.0 copy-start.2
  4.2 1.0 %copy-done.2 = bf16[1936,128]{1,0:T(8,128)(2,1)S(1)} copy-done((bf16[1936,128]{1,0:T(8,128)(2,1)S(1)}, bf16[1936,128]{1,0:T(8,128)(2,1)}, u32[]{:S(2)}) %copy-start.2) | copy-done | bytes 495640
  5.2 0.1 shard_map.29
  5.3 2.6 %collective-permute-start.1 = (bf16[1936,128]{1,0:T(8,128)(2,1)S(1)}, bf16[1936,128]{1,0:T(8,128)(2,1)S(1)}, u32[]{:S(2)}, u32[]{:S(2)}) collective-permute-start(bf16[1936,128]{1,0:T(8,128)(2,1)S(1)} %get-tuple-element.21), channel_id=1, source_target_pairs={{0,1},{2,3},{1,0},{3,2},{4,5},{6,7},{5,4},{7,6},{8,9},{10,11},{9,8... | collective-permute-start | bytes 1486856 | tf_op jit(solution)/shard_map/ppermute | solution.py:363
  7.9 1.5 %collective-permute-start.3 = (bf16[1936,128]{1,0:T(8,128)(2,1)S(1)}, bf16[1936,128]{1,0:T(8,128)(2,1)}, u32[]{:S(2)}, u32[]{:S(2)}) collective-permute-start(bf16[1936,128]{1,0:T(8,128)(2,1)S(1)} %get-tuple-element.22), channel_id=1, source_target_pairs={{1,2},{2,1},{5,6},{6,5},{9,10},{10,9},{13,14},{14,13},{17,18},{18,... | collective-permute-start | bytes 1486856 | tf_op jit(solution)/shard_map/ppermute | solution.py:363
  9.3 5.3 %collective-permute-done.a1 = bf16[1936,128]{1,0:T(8,128)(2,1)S(1)} collective-permute-done((bf16[1936,128]{1,0:T(8,128)(2,1)}, bf16[1936,128]{1,0:T(8,128)(2,1)S(1)}, u32[]{:S(2)}, u32[]{:S(2)}) %collective-permute-start) | collective-permute-done | bytes 495648 | tf_op jit(solution)/shard_map/ppermute | solution.py:363
  14.7 0.7 collective-permute-start.6
  15.4 0.0 collective-permute-done.2.b1
  15.4 1.3 %collective-permute-start.4 = (bf16[1936,128]{1,0:T(8,128)(2,1)S(1)}, bf16[1936,128]{1,0:T(8,128)(2,1)S(1)}, u32[]{:S(2)}, u32[]{:S(2)}) collective-permute-start(bf16[1936,128]{1,0:T(8,128)(2,1)S(1)} %collective-permute-done.2.b1), channel_id=1, source_target_pairs={{2,3},{1,0},{6,7},{5,4},{10,11},{9,8},{14,15},{13,12},{18,19},{17,... | collective-permute-start | bytes 1486856 | tf_op jit(solution)/shard_map/ppermute | solution.py:363
  16.7 8.6 %collective-permute-done.1.a2 = bf16[1936,128]{1,0:T(8,128)(2,1)S(1)} collective-permute-done((bf16[1936,128]{1,0:T(8,128)(2,1)S(1)}, bf16[1936,128]{1,0:T(8,128)(2,1)S(1)}, u32[]{:S(2)}, u32[]{:S(2)}) %collective-permute-start.1) | collective-permute-done | bytes 495648 | tf_op jit(solution)/shard_map/ppermute | solution.py:363
  25.3 0.7 collective-permute-start.7
  26.0 0.0 collective-permute-done.3.b2
  26.0 1.3 %collective-permute-start.5 = (bf16[1936,128]{1,0:T(8,128)(2,1)}, bf16[1936,128]{1,0:T(8,128)(2,1)S(1)}, u32[]{:S(2)}, u32[]{:S(2)}) collective-permute-start(bf16[1936,128]{1,0:T(8,128)(2,1)} %collective-permute-done.3.b2), channel_id=1, source_target_pairs={{2,3},{1,0},{6,7},{5,4},{10,11},{9,8},{14,15},{13,12},{18,19},{17,... | collective-permute-start | bytes 1486856 | tf_op jit(solution)/shard_map/ppermute | solution.py:363
  27.3 0.0 collective-permute-done.6.rb1
  27.3 8.6 %collective-permute-done.4.ra1 = bf16[1936,128]{1,0:T(8,128)(2,1)S(1)} collective-permute-done((bf16[1936,128]{1,0:T(8,128)(2,1)S(1)}, bf16[1936,128]{1,0:T(8,128)(2,1)S(1)}, u32[]{:S(2)}, u32[]{:S(2)}) %collective-permute-start.4) | collective-permute-done | bytes 495648 | tf_op jit(solution)/shard_map/ppermute | solution.py:363
  35.9 0.1 broadcast_select_fusion.1
  36.0 2.7 %collective-permute-start.9 = (bf16[1936,128]{1,0:T(8,128)(2,1)S(1)}, bf16[1936,128]{1,0:T(8,128)(2,1)S(1)}, u32[]{:S(2)}, u32[]{:S(2)}) collective-permute-start(bf16[1936,128]{1,0:T(8,128)(2,1)S(1)} %broadcast_select_fusion.1), channel_id=1, source_target_pairs={{0,4},{1,5},{2,14},{3,15},{4,8},{5,9},{6,2},{7,3},{8,12},{9,13},{1... | collective-permute-start | bytes 1486856 | tf_op jit(solution)/shard_map/ppermute | solution.py:371
  38.7 1.3 %collective-permute-start.8 = (bf16[1936,128]{1,0:T(8,128)(2,1)S(1)}, bf16[1936,128]{1,0:T(8,128)(2,1)S(1)}, u32[]{:S(2)}, u32[]{:S(2)}) collective-permute-start(bf16[1936,128]{1,0:T(8,128)(2,1)S(1)} %collective-permute-done.6.rb1), channel_id=1, source_target_pairs={{1,4},{2,15},{5,8},{6,3},{9,12},{10,7},{13,0},{14,11},{17,20},{18,... | collective-permute-start | bytes 1486856 | tf_op jit(solution)/shard_map/ppermute | solution.py:371
  40.0 0.0 collective-permute-done.7.rb2
  40.0 6.5 %collective-permute-done.5.ra2 = bf16[1936,128]{1,0:T(8,128)(2,1)S(1)} collective-permute-done((bf16[1936,128]{1,0:T(8,128)(2,1)}, bf16[1936,128]{1,0:T(8,128)(2,1)S(1)}, u32[]{:S(2)}, u32[]{:S(2)}) %collective-permute-start.5) | collective-permute-done | bytes 495648 | tf_op jit(solution)/shard_map/ppermute | solution.py:363
  46.6 0.1 broadcast_select_fusion
  46.7 2.7 %collective-permute-start.10 = (bf16[1040,128]{1,0:T(8,128)(2,1)S(1)}, bf16[1040,128]{1,0:T(8,128)(2,1)S(1)}, u32[]{:S(2)}, u32[]{:S(2)}) collective-permute-start(bf16[1040,128]{1,0:T(8,128)(2,1)S(1)} %slice_select_fusion), channel_id=1, source_target_pairs={{0,4},{1,5},{2,14},{3,15},{4,8},{5,9},{6,2},{7,3},{8,12},{9,13},{1... | collective-permute-start | bytes 798728 | tf_op jit(solution)/shard_map/ppermute | solution.py:371
  49.4 1.3 %collective-permute-start.11 = (bf16[1936,128]{1,0:T(8,128)(2,1)S(1)}, bf16[1936,128]{1,0:T(8,128)(2,1)S(1)}, u32[]{:S(2)}, u32[]{:S(2)}) collective-permute-start(bf16[1936,128]{1,0:T(8,128)(2,1)S(1)} %collective-permute-done.7.rb2), channel_id=1, source_target_pairs={{1,4},{2,15},{5,8},{6,3},{9,12},{10,7},{13,0},{14,11},{17,20},{18,... | collective-permute-start | bytes 1486856 | tf_op jit(solution)/shard_map/ppermute | solution.py:371
  50.7 0.0 copy-start.1
  50.7 1.0 %copy-done.1 = bf16[1936,128]{1,0:T(8,128)(2,1)S(1)} copy-done((bf16[1936,128]{1,0:T(8,128)(2,1)S(1)}, bf16[1936,128]{1,0:T(8,128)(2,1)}, u32[]{:S(2)}) %copy-start.1) | copy-done | bytes 495640
  51.7 0.0 copy-start.3
  51.7 1.0 %copy-done.3 = bf16[1936,128]{1,0:T(8,128)(2,1)S(1)} copy-done((bf16[1936,128]{1,0:T(8,128)(2,1)S(1)}, bf16[1936,128]{1,0:T(8,128)(2,1)}, u32[]{:S(2)}) %copy-start.3) | copy-done | bytes 495640
  52.8 4.8 %shard_map.30 = (bf16[10,256,2048]{2,1,0:T(8,128)(2,1)S(1)}, bf16[2560,1536]{1,0:T(8,128)(2,1)S(1)}, f32[20,8,128]{2,1,0:T(8,128)S(1)}) custom-call(bf16[1936,128]{1,0:T(8,128)(2,1)S(1)} %copy-done.1, bf16[1936,128]{1,0:T(8,128)(2,1)S(1)} %copy-done.3, bf16[1936,128]{1,0:T(8,128)(2,1)S(1)} %collective-permute-done.a1, ...), custom_call_target="tpu_custom_call" | custom-call | flops 1000000000 | bytes 1000000 | tf_op jit(solution)/shard_map/pallas_call | solution.py:315
  57.6 0.1 collective-permute-done.10.line
  57.8 2.4 %collective-permute-done.8.ends = bf16[1936,128]{1,0:T(8,128)(2,1)S(1)} collective-permute-done((bf16[1936,128]{1,0:T(8,128)(2,1)S(1)}, bf16[1936,128]{1,0:T(8,128)(2,1)S(1)}, u32[]{:S(2)}, u32[]{:S(2)}) %collective-permute-start.8) | collective-permute-done | bytes 495648 | tf_op jit(solution)/shard_map/ppermute | solution.py:371
  60.1 0.0 collective-permute-done.9.cross
  60.1 5.3 %shard_map.31 = (bf16[10,256,2048]{2,1,0:T(8,128)(2,1)S(1)}, bf16[2560,1536]{1,0:T(8,128)(2,1)S(1)}, f32[20,8,128]{2,1,0:T(8,128)S(1)}, f32[15,256,256]{2,1,0:T(...) custom-call(bf16[10,256,2048]{2,1,0:T(8,128)(2,1)S(1)} %get-tuple-el, ...), custom_call_target="tpu_custom_call", output_to_operand_aliasing={{0}: (0, {}), {1}: (1, {}), {2}: (2, {})} | custom-call | flops 6000000000 | bytes 1000000 | tf_op jit(solution)/shard_map/pallas_call | solution.py:315
  65.4 4.2 %collective-permute-done.11.ends = bf16[1936,128]{1,0:T(8,128)(2,1)S(1)} collective-permute-done((bf16[1936,128]{1,0:T(8,128)(2,1)S(1)}, bf16[1936,128]{1,0:T(8,128)(2,1)S(1)}, u32[]{:S(2)}, u32[]{:S(2)}) %collective-permute-start.11) | collective-permute-done | bytes 495648 | tf_op jit(solution)/shard_map/ppermute | solution.py:371
  69.6 3.9 %shard_map.32 = (bf16[10,256,2048]{2,1,0:T(8,128)(2,1)S(1)}, bf16[2560,1536]{1,0:T(8,128)(2,1)S(1)}, f32[20,8,128]{2,1,0:T(8,128)S(1)}, bf16[4,8,128,128]{3,2,1,0:T(8,128)(2,1)}) custom-call(bf16[10,256,2048]{2,1,0:T(8,128)(2,1)S(1)} %get-tuple-element.26.x_in, ...), custom_call_target="tpu_custom_call", output_to_operand_aliasing={{0}: (0, {}), {1}: (1, {}), {2}: (2, {})} | custom-call | flops 6000000000 | bytes 1000000 | tf_op jit(solution)/shard_map/pallas_call | solution.py:315
  (1 shorter events, 0.0 us)
Async XLA Ops:
  2.3 12.4 %collective-permute-start = (bf16[1936,128]{1,0:T(8,128)(2,1)}, bf16[1936,128]{1,0:T(8,128)(2,1)S(1)}, u32[]{:S(2)}, u32[]{:S(2)}) collective-permute-start(bf16[1936,128]{1,0:T(8,128)(2,1)} %get-tuple-element.19.one.own1), channel_id=1, source_target_pairs={{0,1},{2,3},{1,0},{3,2},{4,5},{6,7},{5,4},{7,6},{8,9},{10,11},{9,8... | collective-permute-start | bytes 1486856 | tf_op jit(solution)/shard_map/ppermute | solution.py:363
  2.5 12.9 %collective-permute-start.2 = (bf16[1936,128]{1,0:T(8,128)(2,1)}, bf16[1936,128]{1,0:T(8,128)(2,1)S(1)}, u32[]{:S(2)}, u32[]{:S(2)}) collective-permute-start(bf16[1936,128]{1,0:T(8,128)(2,1)} %get-tuple-element.20.two.own2), channel_id=1, source_target_pairs={{1,2},{2,1},{5,6},{6,5},{9,10},{10,9},{13,14},{14,13},{17,18},{18,... | collective-permute-start | bytes 1486856 | tf_op jit(solution)/shard_map/ppermute | solution.py:363
  3.2 1.0 %copy-start = (bf16[1936,128]{1,0:T(8,128)(2,1)S(1)}, bf16[1936,128]{1,0:T(8,128)(2,1)}, u32[]{:S(2)}) copy-start(bf16[1936,128]{1,0:T(8,128)(2,1)} %get-tuple-element.19.one.own1) | copy-start | bytes 1486852
  4.2 1.0 %copy-start.2 = (bf16[1936,128]{1,0:T(8,128)(2,1)S(1)}, bf16[1936,128]{1,0:T(8,128)(2,1)}, u32[]{:S(2)}) copy-start(bf16[1936,128]{1,0:T(8,128)(2,1)} %get-tuple-element.20.two.own2) | copy-start | bytes 1486852
  5.3 20.0 %collective-permute-start.1 = (bf16[1936,128]{1,0:T(8,128)(2,1)S(1)}, bf16[1936,128]{1,0:T(8,128)(2,1)S(1)}, u32[]{:S(2)}, u32[]{:S(2)}) collective-permute-start(bf16[1936,128]{1,0:T(8,128)(2,1)S(1)} %get-tuple-element.21), channel_id=1, source_target_pairs={{0,1},{2,3},{1,0},{3,2},{4,5},{6,7},{5,4},{7,6},{8,9},{10,11},{9,8... | collective-permute-start | bytes 1486856 | tf_op jit(solution)/shard_map/ppermute | solution.py:363
  7.9 18.1 %collective-permute-start.3 = (bf16[1936,128]{1,0:T(8,128)(2,1)S(1)}, bf16[1936,128]{1,0:T(8,128)(2,1)}, u32[]{:S(2)}, u32[]{:S(2)}) collective-permute-start(bf16[1936,128]{1,0:T(8,128)(2,1)S(1)} %get-tuple-element.22), channel_id=1, source_target_pairs={{1,2},{2,1},{5,6},{6,5},{9,10},{10,9},{13,14},{14,13},{17,18},{18,... | collective-permute-start | bytes 1486856 | tf_op jit(solution)/shard_map/ppermute | solution.py:363
  14.7 12.6 %collective-permute-start.6 = (bf16[1936,128]{1,0:T(8,128)(2,1)S(1)}, bf16[1936,128]{1,0:T(8,128)(2,1)S(1)}, u32[]{:S(2)}, u32[]{:S(2)}) collective-permute-start(bf16[1936,128]{1,0:T(8,128)(2,1)S(1)} %collective-permute-done.a1), channel_id=1, source_target_pairs={{1,2},{2,1},{5,6},{6,5},{9,10},{10,9},{13,14},{14,13},{17,18},{18,... | collective-permute-start | bytes 1486856 | tf_op jit(solution)/shard_map/ppermute | solution.py:363
  15.4 20.5 %collective-permute-start.4 = (bf16[1936,128]{1,0:T(8,128)(2,1)S(1)}, bf16[1936,128]{1,0:T(8,128)(2,1)S(1)}, u32[]{:S(2)}, u32[]{:S(2)}) collective-permute-start(bf16[1936,128]{1,0:T(8,128)(2,1)S(1)} %collective-permute-done.2.b1), channel_id=1, source_target_pairs={{2,3},{1,0},{6,7},{5,4},{10,11},{9,8},{14,15},{13,12},{18,19},{17,... | collective-permute-start | bytes 1486856 | tf_op jit(solution)/shard_map/ppermute | solution.py:363
  25.3 14.7 %collective-permute-start.7 = (bf16[1936,128]{1,0:T(8,128)(2,1)S(1)}, bf16[1936,128]{1,0:T(8,128)(2,1)S(1)}, u32[]{:S(2)}, u32[]{:S(2)}) collective-permute-start(bf16[1936,128]{1,0:T(8,128)(2,1)S(1)} %collective-permute-done.1.a2), channel_id=1, source_target_pairs={{1,2},{2,1},{5,6},{6,5},{9,10},{10,9},{13,14},{14,13},{17,18},{18,... | collective-permute-start | bytes 1486856 | tf_op jit(solution)/shard_map/ppermute | solution.py:363
  26.0 20.5 %collective-permute-start.5 = (bf16[1936,128]{1,0:T(8,128)(2,1)}, bf16[1936,128]{1,0:T(8,128)(2,1)S(1)}, u32[]{:S(2)}, u32[]{:S(2)}) collective-permute-start(bf16[1936,128]{1,0:T(8,128)(2,1)} %collective-permute-done.3.b2), channel_id=1, source_target_pairs={{2,3},{1,0},{6,7},{5,4},{10,11},{9,8},{14,15},{13,12},{18,19},{17,... | collective-permute-start | bytes 1486856 | tf_op jit(solution)/shard_map/ppermute | solution.py:363
  36.0 24.1 %collective-permute-start.9 = (bf16[1936,128]{1,0:T(8,128)(2,1)S(1)}, bf16[1936,128]{1,0:T(8,128)(2,1)S(1)}, u32[]{:S(2)}, u32[]{:S(2)}) collective-permute-start(bf16[1936,128]{1,0:T(8,128)(2,1)S(1)} %broadcast_select_fusion.1), channel_id=1, source_target_pairs={{0,4},{1,5},{2,14},{3,15},{4,8},{5,9},{6,2},{7,3},{8,12},{9,13},{1... | collective-permute-start | bytes 1486856 | tf_op jit(solution)/shard_map/ppermute | solution.py:371
  38.7 21.4 %collective-permute-start.8 = (bf16[1936,128]{1,0:T(8,128)(2,1)S(1)}, bf16[1936,128]{1,0:T(8,128)(2,1)S(1)}, u32[]{:S(2)}, u32[]{:S(2)}) collective-permute-start(bf16[1936,128]{1,0:T(8,128)(2,1)S(1)} %collective-permute-done.6.rb1), channel_id=1, source_target_pairs={{1,4},{2,15},{5,8},{6,3},{9,12},{10,7},{13,0},{14,11},{17,20},{18,... | collective-permute-start | bytes 1486856 | tf_op jit(solution)/shard_map/ppermute | solution.py:371
  46.7 11.1 %collective-permute-start.10 = (bf16[1040,128]{1,0:T(8,128)(2,1)S(1)}, bf16[1040,128]{1,0:T(8,128)(2,1)S(1)}, u32[]{:S(2)}, u32[]{:S(2)}) collective-permute-start(bf16[1040,128]{1,0:T(8,128)(2,1)S(1)} %slice_select_fusion), channel_id=1, source_target_pairs={{0,4},{1,5},{2,14},{3,15},{4,8},{5,9},{6,2},{7,3},{8,12},{9,13},{1... | collective-permute-start | bytes 798728 | tf_op jit(solution)/shard_map/ppermute | solution.py:371
  49.4 20.2 %collective-permute-start.11 = (bf16[1936,128]{1,0:T(8,128)(2,1)S(1)}, bf16[1936,128]{1,0:T(8,128)(2,1)S(1)}, u32[]{:S(2)}, u32[]{:S(2)}) collective-permute-start(bf16[1936,128]{1,0:T(8,128)(2,1)S(1)} %collective-permute-done.7.rb2), channel_id=1, source_target_pairs={{1,4},{2,15},{5,8},{6,3},{9,12},{10,7},{13,0},{14,11},{17,20},{18,... | collective-permute-start | bytes 1486856 | tf_op jit(solution)/shard_map/ppermute | solution.py:371
  50.7 1.0 %copy-start.1 = (bf16[1936,128]{1,0:T(8,128)(2,1)S(1)}, bf16[1936,128]{1,0:T(8,128)(2,1)}, u32[]{:S(2)}) copy-start(bf16[1936,128]{1,0:T(8,128)(2,1)} %get-tuple-element.19.one.own1) | copy-start | bytes 1486852
  51.7 1.0 %copy-start.3 = (bf16[1936,128]{1,0:T(8,128)(2,1)S(1)}, bf16[1936,128]{1,0:T(8,128)(2,1)}, u32[]{:S(2)}) copy-start(bf16[1936,128]{1,0:T(8,128)(2,1)} %get-tuple-element.20.two.own2) | copy-start | bytes 1486852

commit v9 on v8

--- a/solution.py
+++ b/solution.py
@@ -61,7 +61,7 @@
     return p, q
 
 
-def pack(present, upper, *outs):
+def pack(present, upper_hbm, one, two, upper, sems):
     p, q = triangles()
     right = lax.broadcasted_iota(jnp.int32, (1, B), 1) >= B // 2
 
@@ -70,7 +70,14 @@
         return upper[r, k].astype(jnp.float32) * w
 
     odd = lax.rem(lax.axis_index("col"), 2)
-    for first, out in zip((2 * odd, 2 - 2 * odd), outs):
+    halves = (2 * odd, 2 - 2 * odd)
+    copies = []
+    for n, first in enumerate(halves):
+        part = pl.ds(first, 2)
+        copies.append(pltpu.make_async_copy(upper_hbm.at[part], upper.at[part], sems.at[n]))
+        copies[-1].start()
+    for first, out, copy in zip(halves, (one, two), copies):
+        copy.wait()
         one, two = block(first, 0), block(first + 1, 0)
         out[pl.ds(MIXED, B)] = jnp.where(p <= q, one, two).astype(jnp.bfloat16)
         for r in range(2):
@@ -152,6 +159,7 @@
 
 def purify(late, now, x_ref, y_ref, w_ref, part_ref, ready, send=None):
     for I in (4, 5):
+        complete = {}
         for L in range(I, I + 5):
             terms = cube_terms(late, I, L)
             end = max(stage for _, stage in terms)
@@ -188,8 +196,10 @@
                     sq = y_ref[blk(i), blk(l - 8)].astype(jnp.float32)
                     cube = w * c[di * B : (di + 1) * B, dl * B : (dl + 1) * B]
                     ready[i - 8, off] = (3.0 * sq - 2.0 * cube).astype(jnp.bfloat16)
-                if send is not None:
-                    send(end < 2, (place, di), i - 8, offsets[0], len(offsets))
+                complete.setdefault((i - 8, end < 2), []).extend(offsets)
+        if send is not None:
+            for (i, early), offsets in complete.items():
+                send(i, int(early), min(offsets), len(offsets))
 
 
 def take_all(x_ref, w_ref, pieces):
@@ -281,10 +291,10 @@
     def work(late):
         copies = []
 
-        def send(early, place, i, offset, count):
+        def send(i, early, offset, count):
             part = pl.ds(offset, count)
             copy = pltpu.make_async_copy(
-                (done if early else ready).at[i, part], out.at[i, part], sems.at[place]
+                (done if early else ready).at[i, part], out.at[i, part], sems.at[i, early]
             )
             copy.start()
             copies.append(copy)
@@ -331,7 +341,7 @@
     got = call(stage_1, z_count, outs, [VMEM] * 6, aliases, [], 6 * 10**9, *kept, *rows_1)
     outs = KEPT + [jax.ShapeDtypeStruct((4, 8, B, B), jnp.bfloat16)]
     specs = [VMEM] * 3 + [pl.BlockSpec(memory_space=pl.ANY)]
-    scratch = [pltpu.VMEM((4, 8, B, B), jnp.bfloat16), pltpu.SemaphoreType.DMA((10, 2))]
+    scratch = [pltpu.VMEM((4, 8, B, B), jnp.bfloat16), pltpu.SemaphoreType.DMA((4, 2))]
     return call(stage_2, z_count, outs, specs, aliases, scratch, 6 * 10**9, *got, *rows_2)[3]
 
 
@@ -340,15 +350,28 @@
     out_two[...] = two[...]
 
 
-def pair_call(kernel, limit, specs, *operands):
-    pair = jax.ShapeDtypeStruct((PAIR, B), jnp.bfloat16)
+PAIRS = [pltpu.VMEM((PAIR, B), jnp.bfloat16)] * 2
+
+
+def packed(present, upper):
     return pl.pallas_call(
-        kernel,
-        out_shape=[pair, pair],
-        in_specs=specs,
+        pack,
+        out_shape=PAIRS,
+        in_specs=[SMEM, pl.BlockSpec(memory_space=pltpu.HBM)],
         out_specs=[VMEM, VMEM],
-        compiler_params=pltpu.CompilerParams(vmem_limit_bytes=limit * 1024 * 1024),
-    )(*operands)
+        scratch_shapes=[pltpu.VMEM(upper.shape, upper.dtype), pltpu.SemaphoreType.DMA((2,))],
+        compiler_params=pltpu.CompilerParams(vmem_limit_bytes=56 * 1024 * 1024),
+    )(present, upper)
+
+
+def copied(pairs):
+    return pl.pallas_call(
+        copy_pairs,
+        out_shape=PAIRS,
+        in_specs=[VMEM, VMEM],
+        out_specs=[VMEM, VMEM],
+        compiler_params=pltpu.CompilerParams(vmem_limit_bytes=8 * 1024 * 1024),
+    )(*pairs)
 
 
 def per_device(upper, present):
@@ -370,8 +393,8 @@
         ]
         return lax.ppermute(block, ("row", "col"), pairs)
 
-    own = pair_call(pack, 60, [SMEM, VMEM], present, upper)
-    again = pair_call(copy_pairs, 8, [VMEM, VMEM], *own)
+    own = packed(present, upper)
+    again = copied(own)
     a1, b1 = swap(own[0], 0), swap(own[1], 1)
     a2, b2 = swap(again[1], 0), swap(again[0], 1)
     ra1, rb1 = swap(b1, 0, True), swap(a1, 1)

time: 74.2 us -> 73.6 us (level)
  local copies, waits for them, and re-layouts: 4.12 us -> 0 us
  waiting for transfers between devices: 35.7 us -> 39.4 us
    unnamed x8 -> x0, local copies, waits for them, and re-layouts: 4.12 us -> none
    ppermute x8, waiting for transfers between devices: 29.1 us -> 30.9 us  [swap(): return lax.ppermute(block, 'col', pairs)]
    ppermute x4, waiting for transfers between devices: 6.65 us -> 8.42 us  [hop(): return lax.ppermute(block, ('row', 'col'), pairs)]
where the time goes in v9:
time: 73.6 us; the launch traced here: 73.3 us
  waiting for transfers between devices  39.4 us (54%)
  starting transfers between devices  17 us (23%)
  Pallas kernels  16.5 us (22%)
    ppermute x8, waiting for transfers between devices, swap(): return lax.ppermute(block, 'col', pairs)  30.9 us
    pallas_call x3, Pallas kernels, call(): pl.pallas_call(functools.partial(kernel, z_count), out_shape=outs, in_spe...  14.4 us
    ppermute x8, starting transfers between devices, swap(): return lax.ppermute(block, 'col', pairs)  8.93 us
    ppermute x4, waiting for transfers between devices, hop(): return lax.ppermute(block, ('row', 'col'), pairs)  8.42 us
    ppermute x4, starting transfers between devices, hop(): return lax.ppermute(block, ('row', 'col'), pairs)  8.05 us
    pallas_call x1, Pallas kernels, packed(): pl.pallas_call(pack, out_shape=PAIRS, in_specs=[SMEM, pl.BlockSpec(memory...  2.02 us
  transfers between devices with their start and end apart: 12, of which 7 were waited for; matrix products, arithmetic and copies ran while one was open for 0% of the time, Pallas kernels for 14%

profile of v9, /device:TPU:25, one launch (start us, length us, event | category | flops | bytes accessed | tf_op | source)
XLA Modules:
  0.0 73.3 jit_solution(5386354511720064468)
XLA Ops:
  0.0 2.0 %shard_map.28 = (bf16[1936,128]{1,0:T(8,128)(2,1)S(1)}, bf16[1936,128]{1,0:T(8,128)(2,1)S(1)}) custom-call(s32[4,8]{1,0:T(4,128)} %present.1, bf16[4,8,128,128]{3,2,1,0:T(8,128)(2,1)} %upper_hbm.1), custom_call_target="tpu_custom_call" | custom-call | tf_op jit(solution)/shard_map/pallas_call | solution.py:357
  2.0 0.2 collective-permute-start
  2.3 1.5 %collective-permute-start.2 = (bf16[1936,128]{1,0:T(8,128)(2,1)S(1)}, bf16[1936,128]{1,0:T(8,128)(2,1)}, u32[]{:S(2)}, u32[]{:S(2)}) collective-permute-start(bf16[1936,128]{1,0:T(8,128)(2,1)S(1)} %get-tuple-element.20.two.own2), channel_id=1, source_target_pairs={{1,2},{2,1},{5,6},{6,5},{9,10},{10,9},{13,14},{14,13},{17,18},{18,... | collective-permute-start | bytes 1486856 | tf_op jit(solution)/shard_map/ppermute | solution.py:386
  3.7 0.1 shard_map.29
  3.8 1.8 %collective-permute-start.1 = (bf16[1936,128]{1,0:T(8,128)(2,1)S(1)}, bf16[1936,128]{1,0:T(8,128)(2,1)}, u32[]{:S(2)}, u32[]{:S(2)}) collective-permute-start(bf16[1936,128]{1,0:T(8,128)(2,1)S(1)} %get-tuple-element.21), channel_id=1, source_target_pairs={{0,1},{2,3},{1,0},{3,2},{4,5},{6,7},{5,4},{7,6},{8,9},{10,11},{9,8... | collective-permute-start | bytes 1486856 | tf_op jit(solution)/shard_map/ppermute | solution.py:386
  5.6 1.5 %collective-permute-start.3 = (bf16[1936,128]{1,0:T(8,128)(2,1)S(1)}, bf16[1936,128]{1,0:T(8,128)(2,1)}, u32[]{:S(2)}, u32[]{:S(2)}) collective-permute-start(bf16[1936,128]{1,0:T(8,128)(2,1)S(1)} %get-tuple-element.22), channel_id=1, source_target_pairs={{1,2},{2,1},{5,6},{6,5},{9,10},{10,9},{13,14},{14,13},{17,18},{18,... | collective-permute-start | bytes 1486856 | tf_op jit(solution)/shard_map/ppermute | solution.py:386
  7.1 7.2 %collective-permute-done.a1 = bf16[1936,128]{1,0:T(8,128)(2,1)S(1)} collective-permute-done((bf16[1936,128]{1,0:T(8,128)(2,1)S(1)}, bf16[1936,128]{1,0:T(8,128)(2,1)S(1)}, u32[]{:S(2)}, u32[]{:S(2)}) %collective-permute-start) | collective-permute-done | bytes 495648 | tf_op jit(solution)/shard_map/ppermute | solution.py:386
  14.3 0.7 collective-permute-start.6
  15.0 0.0 collective-permute-done.2.b1
  15.0 1.3 %collective-permute-start.4 = (bf16[1936,128]{1,0:T(8,128)(2,1)}, bf16[1936,128]{1,0:T(8,128)(2,1)S(1)}, u32[]{:S(2)}, u32[]{:S(2)}) collective-permute-start(bf16[1936,128]{1,0:T(8,128)(2,1)} %collective-permute-done.2.b1), channel_id=1, source_target_pairs={{2,3},{1,0},{6,7},{5,4},{10,11},{9,8},{14,15},{13,12},{18,19},{17,... | collective-permute-start | bytes 1486856 | tf_op jit(solution)/shard_map/ppermute | solution.py:386
  16.3 8.7 %collective-permute-done.1.a2 = bf16[1936,128]{1,0:T(8,128)(2,1)} collective-permute-done((bf16[1936,128]{1,0:T(8,128)(2,1)S(1)}, bf16[1936,128]{1,0:T(8,128)(2,1)}, u32[]{:S(2)}, u32[]{:S(2)}) %collective-permute-start.1) | collective-permute-done | bytes 495648 | tf_op jit(solution)/shard_map/ppermute | solution.py:386
  25.0 0.7 collective-permute-start.7
  25.7 0.0 collective-permute-done.3.b2
  25.7 1.3 %collective-permute-start.5 = (bf16[1936,128]{1,0:T(8,128)(2,1)}, bf16[1936,128]{1,0:T(8,128)(2,1)S(1)}, u32[]{:S(2)}, u32[]{:S(2)}) collective-permute-start(bf16[1936,128]{1,0:T(8,128)(2,1)} %collective-permute-done.3.b2), channel_id=1, source_target_pairs={{2,3},{1,0},{6,7},{5,4},{10,11},{9,8},{14,15},{13,12},{18,19},{17,... | collective-permute-start | bytes 1486856 | tf_op jit(solution)/shard_map/ppermute | solution.py:386
  27.0 0.0 collective-permute-done.6.rb1
  27.0 8.5 %collective-permute-done.4.ra1 = bf16[1936,128]{1,0:T(8,128)(2,1)S(1)} collective-permute-done((bf16[1936,128]{1,0:T(8,128)(2,1)}, bf16[1936,128]{1,0:T(8,128)(2,1)S(1)}, u32[]{:S(2)}, u32[]{:S(2)}) %collective-permute-start.4) | collective-permute-done | bytes 495648 | tf_op jit(solution)/shard_map/ppermute | solution.py:386
  35.5 0.1 broadcast_select_fusion.1
  35.6 2.7 %collective-permute-start.9 = (bf16[1936,128]{1,0:T(8,128)(2,1)S(1)}, bf16[1936,128]{1,0:T(8,128)(2,1)S(1)}, u32[]{:S(2)}, u32[]{:S(2)}) collective-permute-start(bf16[1936,128]{1,0:T(8,128)(2,1)S(1)} %broadcast_select_fusion.1), channel_id=1, source_target_pairs={{0,4},{1,5},{2,14},{3,15},{4,8},{5,9},{6,2},{7,3},{8,12},{9,13},{1... | collective-permute-start | bytes 1486856 | tf_op jit(solution)/shard_map/ppermute | solution.py:394
  38.3 1.3 %collective-permute-start.8 = (bf16[1936,128]{1,0:T(8,128)(2,1)S(1)}, bf16[1936,128]{1,0:T(8,128)(2,1)S(1)}, u32[]{:S(2)}, u32[]{:S(2)}) collective-permute-start(bf16[1936,128]{1,0:T(8,128)(2,1)S(1)} %collective-permute-done.6.rb1), channel_id=1, source_target_pairs={{1,4},{2,15},{5,8},{6,3},{9,12},{10,7},{13,0},{14,11},{17,20},{18,... | collective-permute-start | bytes 1486856 | tf_op jit(solution)/shard_map/ppermute | solution.py:394
  39.6 0.0 collective-permute-done.7.rb2
  39.6 6.5 %collective-permute-done.5.ra2 = bf16[1936,128]{1,0:T(8,128)(2,1)S(1)} collective-permute-done((bf16[1936,128]{1,0:T(8,128)(2,1)}, bf16[1936,128]{1,0:T(8,128)(2,1)S(1)}, u32[]{:S(2)}, u32[]{:S(2)}) %collective-permute-start.5) | collective-permute-done | bytes 495648 | tf_op jit(solution)/shard_map/ppermute | solution.py:386
  46.1 0.1 broadcast_select_fusion
  46.2 2.7 %collective-permute-start.10 = (bf16[1040,128]{1,0:T(8,128)(2,1)S(1)}, bf16[1040,128]{1,0:T(8,128)(2,1)S(1)}, u32[]{:S(2)}, u32[]{:S(2)}) collective-permute-start(bf16[1040,128]{1,0:T(8,128)(2,1)S(1)} %slice_select_fusion), channel_id=1, source_target_pairs={{0,4},{1,5},{2,14},{3,15},{4,8},{5,9},{6,2},{7,3},{8,12},{9,13},{1... | collective-permute-start | bytes 798728 | tf_op jit(solution)/shard_map/ppermute | solution.py:394
  49.0 1.3 %collective-permute-start.11 = (bf16[1936,128]{1,0:T(8,128)(2,1)S(1)}, bf16[1936,128]{1,0:T(8,128)(2,1)S(1)}, u32[]{:S(2)}, u32[]{:S(2)}) collective-permute-start(bf16[1936,128]{1,0:T(8,128)(2,1)S(1)} %collective-permute-done.7.rb2), channel_id=1, source_target_pairs={{1,4},{2,15},{5,8},{6,3},{9,12},{10,7},{13,0},{14,11},{17,20},{18,... | collective-permute-start | bytes 1486856 | tf_op jit(solution)/shard_map/ppermute | solution.py:394
  50.3 5.1 %shard_map.30 = (bf16[10,256,2048]{2,1,0:T(8,128)(2,1)S(1)}, bf16[2560,1536]{1,0:T(8,128)(2,1)S(1)}, f32[20,8,128]{2,1,0:T(8,128)S(1)}) custom-call(bf16[1936,128]{1,0:T(8,128)(2,1)S(1)} %get-tuple-element.19.one.own1, bf16[1936,128]{1,0:T(8,128)(2,1)S(1)} %get-tuple-element.20.two.own2, bf16[1936,128]{1,0:T(8,128)(2,1)S(1)} %collective-permute-done.a1, ...), custom_call_target="tpu_custom_call" | custom-call | flops 1000000000 | bytes 1000000 | tf_op jit(solution)/shard_map/pallas_call | solution.py:325
  55.4 1.9 %collective-permute-done.10.line = bf16[1040,128]{1,0:T(8,128)(2,1)S(1)} collective-permute-done((bf16[1040,128]{1,0:T(8,128)(2,1)S(1)}, bf16[1040,128]{1,0:T(8,128)(2,1)S(1)}, u32[]{:S(2)}, u32[]{:S(2)}) %collective-permute-start.10) | collective-permute-done | bytes 266272 | tf_op jit(solution)/shard_map/ppermute | solution.py:394
  57.3 2.4 %collective-permute-done.8.ends = bf16[1936,128]{1,0:T(8,128)(2,1)S(1)} collective-permute-done((bf16[1936,128]{1,0:T(8,128)(2,1)S(1)}, bf16[1936,128]{1,0:T(8,128)(2,1)S(1)}, u32[]{:S(2)}, u32[]{:S(2)}) %collective-permute-start.8) | collective-permute-done | bytes 495648 | tf_op jit(solution)/shard_map/ppermute | solution.py:394
  59.7 0.0 collective-permute-done.9.cross
  59.7 5.3 %shard_map.31 = (bf16[10,256,2048]{2,1,0:T(8,128)(2,1)S(1)}, bf16[2560,1536]{1,0:T(8,128)(2,1)S(1)}, f32[20,8,128]{2,1,0:T(8,128)S(1)}, f32[15,256,256]{2,1,0:T(...) custom-call(bf16[10,256,2048]{2,1,0:T(8,128)(2,1)S(1)} %get-tuple-el, ...), custom_call_target="tpu_custom_call", output_to_operand_aliasing={{0}: (0, {}), {1}: (1, {}), {2}: (2, {})} | custom-call | flops 6000000000 | bytes 1000000 | tf_op jit(solution)/shard_map/pallas_call | solution.py:325
  65.0 4.2 %collective-permute-done.11.ends = bf16[1936,128]{1,0:T(8,128)(2,1)S(1)} collective-permute-done((bf16[1936,128]{1,0:T(8,128)(2,1)S(1)}, bf16[1936,128]{1,0:T(8,128)(2,1)S(1)}, u32[]{:S(2)}, u32[]{:S(2)}) %collective-permute-start.11) | collective-permute-done | bytes 495648 | tf_op jit(solution)/shard_map/ppermute | solution.py:394
  69.2 3.9 %shard_map.32 = (bf16[10,256,2048]{2,1,0:T(8,128)(2,1)S(1)}, bf16[2560,1536]{1,0:T(8,128)(2,1)S(1)}, f32[20,8,128]{2,1,0:T(8,128)S(1)}, bf16[4,8,128,128]{3,2,1,0:T(8,128)(2,1)}) custom-call(bf16[10,256,2048]{2,1,0:T(8,128)(2,1)S(1)} %get-tuple-element.26.x_in, ...), custom_call_target="tpu_custom_call", output_to_operand_aliasing={{0}: (0, {}), {1}: (1, {}), {2}: (2, {})} | custom-call | flops 6000000000 | bytes 1000000 | tf_op jit(solution)/shard_map/pallas_call | solution.py:325
  (1 shorter events, 0.0 us)
Async XLA Ops:
  2.0 12.2 %collective-permute-start = (bf16[1936,128]{1,0:T(8,128)(2,1)S(1)}, bf16[1936,128]{1,0:T(8,128)(2,1)S(1)}, u32[]{:S(2)}, u32[]{:S(2)}) collective-permute-start(bf16[1936,128]{1,0:T(8,128)(2,1)S(1)} %get-tuple-element.19.one.own1), channel_id=1, source_target_pairs={{0,1},{2,3},{1,0},{3,2},{4,5},{6,7},{5,4},{7,6},{8,9},{10,11},{9,8... | collective-permute-start | bytes 1486856 | tf_op jit(solution)/shard_map/ppermute | solution.py:386
  2.3 12.7 %collective-permute-start.2 = (bf16[1936,128]{1,0:T(8,128)(2,1)S(1)}, bf16[1936,128]{1,0:T(8,128)(2,1)}, u32[]{:S(2)}, u32[]{:S(2)}) collective-permute-start(bf16[1936,128]{1,0:T(8,128)(2,1)S(1)} %get-tuple-element.20.two.own2), channel_id=1, source_target_pairs={{1,2},{2,1},{5,6},{6,5},{9,10},{10,9},{13,14},{14,13},{17,18},{18,... | collective-permute-start | bytes 1486856 | tf_op jit(solution)/shard_map/ppermute | solution.py:386
  3.8 21.2 %collective-permute-start.1 = (bf16[1936,128]{1,0:T(8,128)(2,1)S(1)}, bf16[1936,128]{1,0:T(8,128)(2,1)}, u32[]{:S(2)}, u32[]{:S(2)}) collective-permute-start(bf16[1936,128]{1,0:T(8,128)(2,1)S(1)} %get-tuple-element.21), channel_id=1, source_target_pairs={{0,1},{2,3},{1,0},{3,2},{4,5},{6,7},{5,4},{7,6},{8,9},{10,11},{9,8... | collective-permute-start | bytes 1486856 | tf_op jit(solution)/shard_map/ppermute | solution.py:386
  5.6 20.1 %collective-permute-start.3 = (bf16[1936,128]{1,0:T(8,128)(2,1)S(1)}, bf16[1936,128]{1,0:T(8,128)(2,1)}, u32[]{:S(2)}, u32[]{:S(2)}) collective-permute-start(bf16[1936,128]{1,0:T(8,128)(2,1)S(1)} %get-tuple-element.22), channel_id=1, source_target_pairs={{1,2},{2,1},{5,6},{6,5},{9,10},{10,9},{13,14},{14,13},{17,18},{18,... | collective-permute-start | bytes 1486856 | tf_op jit(solution)/shard_map/ppermute | solution.py:386
  14.3 12.7 %collective-permute-start.6 = (bf16[1936,128]{1,0:T(8,128)(2,1)S(1)}, bf16[1936,128]{1,0:T(8,128)(2,1)S(1)}, u32[]{:S(2)}, u32[]{:S(2)}) collective-permute-start(bf16[1936,128]{1,0:T(8,128)(2,1)S(1)} %collective-permute-done.a1), channel_id=1, source_target_pairs={{1,2},{2,1},{5,6},{6,5},{9,10},{10,9},{13,14},{14,13},{17,18},{18,... | collective-permute-start | bytes 1486856 | tf_op jit(solution)/shard_map/ppermute | solution.py:386
  15.0 20.5 %collective-permute-start.4 = (bf16[1936,128]{1,0:T(8,128)(2,1)}, bf16[1936,128]{1,0:T(8,128)(2,1)S(1)}, u32[]{:S(2)}, u32[]{:S(2)}) collective-permute-start(bf16[1936,128]{1,0:T(8,128)(2,1)} %collective-permute-done.2.b1), channel_id=1, source_target_pairs={{2,3},{1,0},{6,7},{5,4},{10,11},{9,8},{14,15},{13,12},{18,19},{17,... | collective-permute-start | bytes 1486856 | tf_op jit(solution)/shard_map/ppermute | solution.py:386
  25.0 14.6 %collective-permute-start.7 = (bf16[1936,128]{1,0:T(8,128)(2,1)}, bf16[1936,128]{1,0:T(8,128)(2,1)S(1)}, u32[]{:S(2)}, u32[]{:S(2)}) collective-permute-start(bf16[1936,128]{1,0:T(8,128)(2,1)} %collective-permute-done.1.a2), channel_id=1, source_target_pairs={{1,2},{2,1},{5,6},{6,5},{9,10},{10,9},{13,14},{14,13},{17,18},{18,... | collective-permute-start | bytes 1486856 | tf_op jit(solution)/shard_map/ppermute | solution.py:386
  25.7 20.4 %collective-permute-start.5 = (bf16[1936,128]{1,0:T(8,128)(2,1)}, bf16[1936,128]{1,0:T(8,128)(2,1)S(1)}, u32[]{:S(2)}, u32[]{:S(2)}) collective-permute-start(bf16[1936,128]{1,0:T(8,128)(2,1)} %collective-permute-done.3.b2), channel_id=1, source_target_pairs={{2,3},{1,0},{6,7},{5,4},{10,11},{9,8},{14,15},{13,12},{18,19},{17,... | collective-permute-start | bytes 1486856 | tf_op jit(solution)/shard_map/ppermute | solution.py:386
  35.6 24.1 %collective-permute-start.9 = (bf16[1936,128]{1,0:T(8,128)(2,1)S(1)}, bf16[1936,128]{1,0:T(8,128)(2,1)S(1)}, u32[]{:S(2)}, u32[]{:S(2)}) collective-permute-start(bf16[1936,128]{1,0:T(8,128)(2,1)S(1)} %broadcast_select_fusion.1), channel_id=1, source_target_pairs={{0,4},{1,5},{2,14},{3,15},{4,8},{5,9},{6,2},{7,3},{8,12},{9,13},{1... | collective-permute-start | bytes 1486856 | tf_op jit(solution)/shard_map/ppermute | solution.py:394
  38.3 21.4 %collective-permute-start.8 = (bf16[1936,128]{1,0:T(8,128)(2,1)S(1)}, bf16[1936,128]{1,0:T(8,128)(2,1)S(1)}, u32[]{:S(2)}, u32[]{:S(2)}) collective-permute-start(bf16[1936,128]{1,0:T(8,128)(2,1)S(1)} %collective-permute-done.6.rb1), channel_id=1, source_target_pairs={{1,4},{2,15},{5,8},{6,3},{9,12},{10,7},{13,0},{14,11},{17,20},{18,... | collective-permute-start | bytes 1486856 | tf_op jit(solution)/shard_map/ppermute | solution.py:394
  46.2 11.1 %collective-permute-start.10 = (bf16[1040,128]{1,0:T(8,128)(2,1)S(1)}, bf16[1040,128]{1,0:T(8,128)(2,1)S(1)}, u32[]{:S(2)}, u32[]{:S(2)}) collective-permute-start(bf16[1040,128]{1,0:T(8,128)(2,1)S(1)} %slice_select_fusion), channel_id=1, source_target_pairs={{0,4},{1,5},{2,14},{3,15},{4,8},{5,9},{6,2},{7,3},{8,12},{9,13},{1... | collective-permute-start | bytes 798728 | tf_op jit(solution)/shard_map/ppermute | solution.py:394
  49.0 20.2 %collective-permute-start.11 = (bf16[1936,128]{1,0:T(8,128)(2,1)S(1)}, bf16[1936,128]{1,0:T(8,128)(2,1)S(1)}, u32[]{:S(2)}, u32[]{:S(2)}) collective-permute-start(bf16[1936,128]{1,0:T(8,128)(2,1)S(1)} %collective-permute-done.7.rb2), channel_id=1, source_target_pairs={{1,4},{2,15},{5,8},{6,3},{9,12},{10,7},{13,0},{14,11},{17,20},{18,... | collective-permute-start | bytes 1486856 | tf_op jit(solution)/shard_map/ppermute | solution.py:394

commit v10 on v9

--- a/solution.py
+++ b/solution.py
@@ -61,7 +61,7 @@
     return p, q
 
 
-def pack(present, upper_hbm, one, two, upper, sems):
+def pack(present_hbm, upper_hbm, one, two, present, upper, sems):
     p, q = triangles()
     right = lax.broadcasted_iota(jnp.int32, (1, B), 1) >= B // 2
 
@@ -71,11 +71,14 @@
 
     odd = lax.rem(lax.axis_index("col"), 2)
     halves = (2 * odd, 2 - 2 * odd)
+    pattern = pltpu.make_async_copy(present_hbm, present, sems.at[2])
+    pattern.start()
     copies = []
     for n, first in enumerate(halves):
         part = pl.ds(first, 2)
         copies.append(pltpu.make_async_copy(upper_hbm.at[part], upper.at[part], sems.at[n]))
         copies[-1].start()
+    pattern.wait()
     for first, out, copy in zip(halves, (one, two), copies):
         copy.wait()
         one, two = block(first, 0), block(first + 1, 0)
@@ -357,9 +360,13 @@
     return pl.pallas_call(
         pack,
         out_shape=PAIRS,
-        in_specs=[SMEM, pl.BlockSpec(memory_space=pltpu.HBM)],
+        in_specs=[pl.BlockSpec(memory_space=pltpu.HBM)] * 2,
         out_specs=[VMEM, VMEM],
-        scratch_shapes=[pltpu.VMEM(upper.shape, upper.dtype), pltpu.SemaphoreType.DMA((2,))],
+        scratch_shapes=[
+            pltpu.SMEM(present.shape, present.dtype),
+            pltpu.VMEM(upper.shape, upper.dtype),
+            pltpu.SemaphoreType.DMA((3,)),
+        ],
         compiler_params=pltpu.CompilerParams(vmem_limit_bytes=56 * 1024 * 1024),
     )(present, upper)
 

time: 73.6 us -> 72.9 us (level)
  no operation moved by 1% of the time
where the time goes in v10:
time: 72.9 us; the launch traced here: 72.6 us
  waiting for transfers between devices  39.4 us (54%)
  starting transfers between devices  17 us (23%)
  Pallas kernels  15.8 us (22%)
    ppermute x8, waiting for transfers between devices, swap(): return lax.ppermute(block, 'col', pairs)  30.9 us
    pallas_call x3, Pallas kernels, call(): pl.pallas_call(functools.partial(kernel, z_count), out_shape=outs, in_spe...  14.4 us
    ppermute x8, starting transfers between devices, swap(): return lax.ppermute(block, 'col', pairs)  8.93 us
    ppermute x4, waiting for transfers between devices, hop(): return lax.ppermute(block, ('row', 'col'), pairs)  8.42 us
    ppermute x4, starting transfers between devices, hop(): return lax.ppermute(block, ('row', 'col'), pairs)  8.05 us
  transfers between devices with their start and end apart: 12, of which 7 were waited for; matrix products, arithmetic and copies ran while one was open for 0% of the time, Pallas kernels for 14%

profile of v10, /device:TPU:25, one launch (start us, length us, event | category | flops | bytes accessed | tf_op | source)
XLA Modules:
  0.0 72.6 jit_solution(1969427015162017206)
XLA Ops:
  0.0 1.3 %shard_map.28 = (bf16[1936,128]{1,0:T(8,128)(2,1)S(1)}, bf16[1936,128]{1,0:T(8,128)(2,1)S(1)}) custom-call(s32[4,8]{1,0:T(4,128)} %present_hbm.1, bf16[4,8,128,128]{3,2,1,0:T(8,128)(2,1)} %upper_hbm.1), custom_call_target="tpu_custom_call" | custom-call | tf_op jit(solution)/shard_map/pallas_call | solution.py:360
  1.3 0.2 collective-permute-start
  1.6 1.5 %collective-permute-start.2 = (bf16[1936,128]{1,0:T(8,128)(2,1)S(1)}, bf16[1936,128]{1,0:T(8,128)(2,1)}, u32[]{:S(2)}, u32[]{:S(2)}) collective-permute-start(bf16[1936,128]{1,0:T(8,128)(2,1)S(1)} %get-tuple-element.20.two.own2), channel_id=1, source_target_pairs={{1,2},{2,1},{5,6},{6,5},{9,10},{10,9},{13,14},{14,13},{17,18},{18,... | collective-permute-start | bytes 1486856 | tf_op jit(solution)/shard_map/ppermute | solution.py:393
  3.0 0.1 shard_map.29
  3.1 1.8 %collective-permute-start.1 = (bf16[1936,128]{1,0:T(8,128)(2,1)S(1)}, bf16[1936,128]{1,0:T(8,128)(2,1)}, u32[]{:S(2)}, u32[]{:S(2)}) collective-permute-start(bf16[1936,128]{1,0:T(8,128)(2,1)S(1)} %get-tuple-element.21), channel_id=1, source_target_pairs={{0,1},{2,3},{1,0},{3,2},{4,5},{6,7},{5,4},{7,6},{8,9},{10,11},{9,8... | collective-permute-start | bytes 1486856 | tf_op jit(solution)/shard_map/ppermute | solution.py:393
  4.9 1.5 %collective-permute-start.3 = (bf16[1936,128]{1,0:T(8,128)(2,1)S(1)}, bf16[1936,128]{1,0:T(8,128)(2,1)}, u32[]{:S(2)}, u32[]{:S(2)}) collective-permute-start(bf16[1936,128]{1,0:T(8,128)(2,1)S(1)} %get-tuple-element.22), channel_id=1, source_target_pairs={{1,2},{2,1},{5,6},{6,5},{9,10},{10,9},{13,14},{14,13},{17,18},{18,... | collective-permute-start | bytes 1486856 | tf_op jit(solution)/shard_map/ppermute | solution.py:393
  6.4 7.2 %collective-permute-done.a1 = bf16[1936,128]{1,0:T(8,128)(2,1)S(1)} collective-permute-done((bf16[1936,128]{1,0:T(8,128)(2,1)S(1)}, bf16[1936,128]{1,0:T(8,128)(2,1)S(1)}, u32[]{:S(2)}, u32[]{:S(2)}) %collective-permute-start) | collective-permute-done | bytes 495648 | tf_op jit(solution)/shard_map/ppermute | solution.py:393
  13.6 0.7 collective-permute-start.6
  14.3 0.0 collective-permute-done.2.b1
  14.3 1.3 %collective-permute-start.4 = (bf16[1936,128]{1,0:T(8,128)(2,1)}, bf16[1936,128]{1,0:T(8,128)(2,1)S(1)}, u32[]{:S(2)}, u32[]{:S(2)}) collective-permute-start(bf16[1936,128]{1,0:T(8,128)(2,1)} %collective-permute-done.2.b1), channel_id=1, source_target_pairs={{2,3},{1,0},{6,7},{5,4},{10,11},{9,8},{14,15},{13,12},{18,19},{17,... | collective-permute-start | bytes 1486856 | tf_op jit(solution)/shard_map/ppermute | solution.py:393
  15.6 8.7 %collective-permute-done.1.a2 = bf16[1936,128]{1,0:T(8,128)(2,1)} collective-permute-done((bf16[1936,128]{1,0:T(8,128)(2,1)S(1)}, bf16[1936,128]{1,0:T(8,128)(2,1)}, u32[]{:S(2)}, u32[]{:S(2)}) %collective-permute-start.1) | collective-permute-done | bytes 495648 | tf_op jit(solution)/shard_map/ppermute | solution.py:393
  24.3 0.7 collective-permute-start.7
  25.0 0.0 collective-permute-done.3.b2
  25.0 1.3 %collective-permute-start.5 = (bf16[1936,128]{1,0:T(8,128)(2,1)}, bf16[1936,128]{1,0:T(8,128)(2,1)S(1)}, u32[]{:S(2)}, u32[]{:S(2)}) collective-permute-start(bf16[1936,128]{1,0:T(8,128)(2,1)} %collective-permute-done.3.b2), channel_id=1, source_target_pairs={{2,3},{1,0},{6,7},{5,4},{10,11},{9,8},{14,15},{13,12},{18,19},{17,... | collective-permute-start | bytes 1486856 | tf_op jit(solution)/shard_map/ppermute | solution.py:393
  26.3 0.0 collective-permute-done.6.rb1
  26.3 8.5 %collective-permute-done.4.ra1 = bf16[1936,128]{1,0:T(8,128)(2,1)S(1)} collective-permute-done((bf16[1936,128]{1,0:T(8,128)(2,1)}, bf16[1936,128]{1,0:T(8,128)(2,1)S(1)}, u32[]{:S(2)}, u32[]{:S(2)}) %collective-permute-start.4) | collective-permute-done | bytes 495648 | tf_op jit(solution)/shard_map/ppermute | solution.py:393
  34.8 0.1 broadcast_select_fusion.1
  34.9 2.7 %collective-permute-start.9 = (bf16[1936,128]{1,0:T(8,128)(2,1)S(1)}, bf16[1936,128]{1,0:T(8,128)(2,1)S(1)}, u32[]{:S(2)}, u32[]{:S(2)}) collective-permute-start(bf16[1936,128]{1,0:T(8,128)(2,1)S(1)} %broadcast_select_fusion.1), channel_id=1, source_target_pairs={{0,4},{1,5},{2,14},{3,15},{4,8},{5,9},{6,2},{7,3},{8,12},{9,13},{1... | collective-permute-start | bytes 1486856 | tf_op jit(solution)/shard_map/ppermute | solution.py:401
  37.6 1.3 %collective-permute-start.8 = (bf16[1936,128]{1,0:T(8,128)(2,1)S(1)}, bf16[1936,128]{1,0:T(8,128)(2,1)S(1)}, u32[]{:S(2)}, u32[]{:S(2)}) collective-permute-start(bf16[1936,128]{1,0:T(8,128)(2,1)S(1)} %collective-permute-done.6.rb1), channel_id=1, source_target_pairs={{1,4},{2,15},{5,8},{6,3},{9,12},{10,7},{13,0},{14,11},{17,20},{18,... | collective-permute-start | bytes 1486856 | tf_op jit(solution)/shard_map/ppermute | solution.py:401
  38.9 0.0 collective-permute-done.7.rb2
  38.9 6.5 %collective-permute-done.5.ra2 = bf16[1936,128]{1,0:T(8,128)(2,1)S(1)} collective-permute-done((bf16[1936,128]{1,0:T(8,128)(2,1)}, bf16[1936,128]{1,0:T(8,128)(2,1)S(1)}, u32[]{:S(2)}, u32[]{:S(2)}) %collective-permute-start.5) | collective-permute-done | bytes 495648 | tf_op jit(solution)/shard_map/ppermute | solution.py:393
  45.5 0.1 broadcast_select_fusion
  45.6 2.7 %collective-permute-start.10 = (bf16[1040,128]{1,0:T(8,128)(2,1)S(1)}, bf16[1040,128]{1,0:T(8,128)(2,1)S(1)}, u32[]{:S(2)}, u32[]{:S(2)}) collective-permute-start(bf16[1040,128]{1,0:T(8,128)(2,1)S(1)} %slice_select_fusion), channel_id=1, source_target_pairs={{0,4},{1,5},{2,14},{3,15},{4,8},{5,9},{6,2},{7,3},{8,12},{9,13},{1... | collective-permute-start | bytes 798728 | tf_op jit(solution)/shard_map/ppermute | solution.py:401
  48.3 1.3 %collective-permute-start.11 = (bf16[1936,128]{1,0:T(8,128)(2,1)S(1)}, bf16[1936,128]{1,0:T(8,128)(2,1)S(1)}, u32[]{:S(2)}, u32[]{:S(2)}) collective-permute-start(bf16[1936,128]{1,0:T(8,128)(2,1)S(1)} %collective-permute-done.7.rb2), channel_id=1, source_target_pairs={{1,4},{2,15},{5,8},{6,3},{9,12},{10,7},{13,0},{14,11},{17,20},{18,... | collective-permute-start | bytes 1486856 | tf_op jit(solution)/shard_map/ppermute | solution.py:401
  49.6 5.1 %shard_map.30 = (bf16[10,256,2048]{2,1,0:T(8,128)(2,1)S(1)}, bf16[2560,1536]{1,0:T(8,128)(2,1)S(1)}, f32[20,8,128]{2,1,0:T(8,128)S(1)}) custom-call(bf16[1936,128]{1,0:T(8,128)(2,1)S(1)} %get-tuple-element.19.one.own1, bf16[1936,128]{1,0:T(8,128)(2,1)S(1)} %get-tuple-element.20.two.own2, bf16[1936,128]{1,0:T(8,128)(2,1)S(1)} %collective-permute-done.a1, ...), custom_call_target="tpu_custom_call" | custom-call | flops 1000000000 | bytes 1000000 | tf_op jit(solution)/shard_map/pallas_call | solution.py:328
  54.7 1.9 %collective-permute-done.10.line = bf16[1040,128]{1,0:T(8,128)(2,1)S(1)} collective-permute-done((bf16[1040,128]{1,0:T(8,128)(2,1)S(1)}, bf16[1040,128]{1,0:T(8,128)(2,1)S(1)}, u32[]{:S(2)}, u32[]{:S(2)}) %collective-permute-start.10) | collective-permute-done | bytes 266272 | tf_op jit(solution)/shard_map/ppermute | solution.py:401
  56.6 2.4 %collective-permute-done.8.ends = bf16[1936,128]{1,0:T(8,128)(2,1)S(1)} collective-permute-done((bf16[1936,128]{1,0:T(8,128)(2,1)S(1)}, bf16[1936,128]{1,0:T(8,128)(2,1)S(1)}, u32[]{:S(2)}, u32[]{:S(2)}) %collective-permute-start.8) | collective-permute-done | bytes 495648 | tf_op jit(solution)/shard_map/ppermute | solution.py:401
  59.0 0.0 collective-permute-done.9.cross
  59.0 5.3 %shard_map.31 = (bf16[10,256,2048]{2,1,0:T(8,128)(2,1)S(1)}, bf16[2560,1536]{1,0:T(8,128)(2,1)S(1)}, f32[20,8,128]{2,1,0:T(8,128)S(1)}, f32[15,256,256]{2,1,0:T(...) custom-call(bf16[10,256,2048]{2,1,0:T(8,128)(2,1)S(1)} %get-tuple-el, ...), custom_call_target="tpu_custom_call", output_to_operand_aliasing={{0}: (0, {}), {1}: (1, {}), {2}: (2, {})} | custom-call | flops 6000000000 | bytes 1000000 | tf_op jit(solution)/shard_map/pallas_call | solution.py:328
  64.3 4.2 %collective-permute-done.11.ends = bf16[1936,128]{1,0:T(8,128)(2,1)S(1)} collective-permute-done((bf16[1936,128]{1,0:T(8,128)(2,1)S(1)}, bf16[1936,128]{1,0:T(8,128)(2,1)S(1)}, u32[]{:S(2)}, u32[]{:S(2)}) %collective-permute-start.11) | collective-permute-done | bytes 495648 | tf_op jit(solution)/shard_map/ppermute | solution.py:401
  68.5 3.9 %shard_map.32 = (bf16[10,256,2048]{2,1,0:T(8,128)(2,1)S(1)}, bf16[2560,1536]{1,0:T(8,128)(2,1)S(1)}, f32[20,8,128]{2,1,0:T(8,128)S(1)}, bf16[4,8,128,128]{3,2,1,0:T(8,128)(2,1)}) custom-call(bf16[10,256,2048]{2,1,0:T(8,128)(2,1)S(1)} %get-tuple-element.26.x_in, ...), custom_call_target="tpu_custom_call", output_to_operand_aliasing={{0}: (0, {}), {1}: (1, {}), {2}: (2, {})} | custom-call | flops 6000000000 | bytes 1000000 | tf_op jit(solution)/shard_map/pallas_call | solution.py:328
  (1 shorter events, 0.0 us)
Async XLA Ops:
  1.3 12.2 %collective-permute-start = (bf16[1936,128]{1,0:T(8,128)(2,1)S(1)}, bf16[1936,128]{1,0:T(8,128)(2,1)S(1)}, u32[]{:S(2)}, u32[]{:S(2)}) collective-permute-start(bf16[1936,128]{1,0:T(8,128)(2,1)S(1)} %get-tuple-element.19.one.own1), channel_id=1, source_target_pairs={{0,1},{2,3},{1,0},{3,2},{4,5},{6,7},{5,4},{7,6},{8,9},{10,11},{9,8... | collective-permute-start | bytes 1486856 | tf_op jit(solution)/shard_map/ppermute | solution.py:393
  1.6 12.7 %collective-permute-start.2 = (bf16[1936,128]{1,0:T(8,128)(2,1)S(1)}, bf16[1936,128]{1,0:T(8,128)(2,1)}, u32[]{:S(2)}, u32[]{:S(2)}) collective-permute-start(bf16[1936,128]{1,0:T(8,128)(2,1)S(1)} %get-tuple-element.20.two.own2), channel_id=1, source_target_pairs={{1,2},{2,1},{5,6},{6,5},{9,10},{10,9},{13,14},{14,13},{17,18},{18,... | collective-permute-start | bytes 1486856 | tf_op jit(solution)/shard_map/ppermute | solution.py:393
  3.1 21.2 %collective-permute-start.1 = (bf16[1936,128]{1,0:T(8,128)(2,1)S(1)}, bf16[1936,128]{1,0:T(8,128)(2,1)}, u32[]{:S(2)}, u32[]{:S(2)}) collective-permute-start(bf16[1936,128]{1,0:T(8,128)(2,1)S(1)} %get-tuple-element.21), channel_id=1, source_target_pairs={{0,1},{2,3},{1,0},{3,2},{4,5},{6,7},{5,4},{7,6},{8,9},{10,11},{9,8... | collective-permute-start | bytes 1486856 | tf_op jit(solution)/shard_map/ppermute | solution.py:393
  4.9 20.1 %collective-permute-start.3 = (bf16[1936,128]{1,0:T(8,128)(2,1)S(1)}, bf16[1936,128]{1,0:T(8,128)(2,1)}, u32[]{:S(2)}, u32[]{:S(2)}) collective-permute-start(bf16[1936,128]{1,0:T(8,128)(2,1)S(1)} %get-tuple-element.22), channel_id=1, source_target_pairs={{1,2},{2,1},{5,6},{6,5},{9,10},{10,9},{13,14},{14,13},{17,18},{18,... | collective-permute-start | bytes 1486856 | tf_op jit(solution)/shard_map/ppermute | solution.py:393
  13.6 12.7 %collective-permute-start.6 = (bf16[1936,128]{1,0:T(8,128)(2,1)S(1)}, bf16[1936,128]{1,0:T(8,128)(2,1)S(1)}, u32[]{:S(2)}, u32[]{:S(2)}) collective-permute-start(bf16[1936,128]{1,0:T(8,128)(2,1)S(1)} %collective-permute-done.a1), channel_id=1, source_target_pairs={{1,2},{2,1},{5,6},{6,5},{9,10},{10,9},{13,14},{14,13},{17,18},{18,... | collective-permute-start | bytes 1486856 | tf_op jit(solution)/shard_map/ppermute | solution.py:393
  14.3 20.5 %collective-permute-start.4 = (bf16[1936,128]{1,0:T(8,128)(2,1)}, bf16[1936,128]{1,0:T(8,128)(2,1)S(1)}, u32[]{:S(2)}, u32[]{:S(2)}) collective-permute-start(bf16[1936,128]{1,0:T(8,128)(2,1)} %collective-permute-done.2.b1), channel_id=1, source_target_pairs={{2,3},{1,0},{6,7},{5,4},{10,11},{9,8},{14,15},{13,12},{18,19},{17,... | collective-permute-start | bytes 1486856 | tf_op jit(solution)/shard_map/ppermute | solution.py:393
  24.3 14.6 %collective-permute-start.7 = (bf16[1936,128]{1,0:T(8,128)(2,1)}, bf16[1936,128]{1,0:T(8,128)(2,1)S(1)}, u32[]{:S(2)}, u32[]{:S(2)}) collective-permute-start(bf16[1936,128]{1,0:T(8,128)(2,1)} %collective-permute-done.1.a2), channel_id=1, source_target_pairs={{1,2},{2,1},{5,6},{6,5},{9,10},{10,9},{13,14},{14,13},{17,18},{18,... | collective-permute-start | bytes 1486856 | tf_op jit(solution)/shard_map/ppermute | solution.py:393
  25.0 20.4 %collective-permute-start.5 = (bf16[1936,128]{1,0:T(8,128)(2,1)}, bf16[1936,128]{1,0:T(8,128)(2,1)S(1)}, u32[]{:S(2)}, u32[]{:S(2)}) collective-permute-start(bf16[1936,128]{1,0:T(8,128)(2,1)} %collective-permute-done.3.b2), channel_id=1, source_target_pairs={{2,3},{1,0},{6,7},{5,4},{10,11},{9,8},{14,15},{13,12},{18,19},{17,... | collective-permute-start | bytes 1486856 | tf_op jit(solution)/shard_map/ppermute | solution.py:393
  34.9 24.1 %collective-permute-start.9 = (bf16[1936,128]{1,0:T(8,128)(2,1)S(1)}, bf16[1936,128]{1,0:T(8,128)(2,1)S(1)}, u32[]{:S(2)}, u32[]{:S(2)}) collective-permute-start(bf16[1936,128]{1,0:T(8,128)(2,1)S(1)} %broadcast_select_fusion.1), channel_id=1, source_target_pairs={{0,4},{1,5},{2,14},{3,15},{4,8},{5,9},{6,2},{7,3},{8,12},{9,13},{1... | collective-permute-start | bytes 1486856 | tf_op jit(solution)/shard_map/ppermute | solution.py:401
  37.6 21.4 %collective-permute-start.8 = (bf16[1936,128]{1,0:T(8,128)(2,1)S(1)}, bf16[1936,128]{1,0:T(8,128)(2,1)S(1)}, u32[]{:S(2)}, u32[]{:S(2)}) collective-permute-start(bf16[1936,128]{1,0:T(8,128)(2,1)S(1)} %collective-permute-done.6.rb1), channel_id=1, source_target_pairs={{1,4},{2,15},{5,8},{6,3},{9,12},{10,7},{13,0},{14,11},{17,20},{18,... | collective-permute-start | bytes 1486856 | tf_op jit(solution)/shard_map/ppermute | solution.py:401
  45.6 11.1 %collective-permute-start.10 = (bf16[1040,128]{1,0:T(8,128)(2,1)S(1)}, bf16[1040,128]{1,0:T(8,128)(2,1)S(1)}, u32[]{:S(2)}, u32[]{:S(2)}) collective-permute-start(bf16[1040,128]{1,0:T(8,128)(2,1)S(1)} %slice_select_fusion), channel_id=1, source_target_pairs={{0,4},{1,5},{2,14},{3,15},{4,8},{5,9},{6,2},{7,3},{8,12},{9,13},{1... | collective-permute-start | bytes 798728 | tf_op jit(solution)/shard_map/ppermute | solution.py:401
  48.3 20.2 %collective-permute-start.11 = (bf16[1936,128]{1,0:T(8,128)(2,1)S(1)}, bf16[1936,128]{1,0:T(8,128)(2,1)S(1)}, u32[]{:S(2)}, u32[]{:S(2)}) collective-permute-start(bf16[1936,128]{1,0:T(8,128)(2,1)S(1)} %collective-permute-done.7.rb2), channel_id=1, source_target_pairs={{1,4},{2,15},{5,8},{6,3},{9,12},{10,7},{13,0},{14,11},{17,20},{18,... | collective-permute-start | bytes 1486856 | tf_op jit(solution)/shard_map/ppermute | solution.py:401

commit v11 on v10

--- a/solution.py
+++ b/solution.py
@@ -127,6 +127,7 @@
     for L in range(4, 10):
         for J in range(L - 4, L + 1):
             terms = square_terms(late, J, L)
+            lo, size = (1, 1) if L - J == 4 else (0, 2)
             end = max(stage for _, stage in terms)
             if now > end or (now == 0 and end > 0):
                 continue
@@ -134,8 +135,8 @@
             s = None
             for m, n in runs(mine):
                 t = lax.dot_general(
-                    x_ref[J, :, blk(m - 2 * J + 7, n)],
-                    x_ref[L, :, blk(m - 2 * L + 7, n)],
+                    x_ref[J, blk(lo, size), blk(m - 2 * J + 7, n)],
+                    x_ref[L, blk(0, size), blk(m - 2 * L + 7, n)],
                     NT,
                     preferred_element_type=jnp.float32,
                 )
@@ -143,10 +144,10 @@
             place = L % 3 * 5 + J - L + 4
             if now < end:
                 if s is not None:
-                    part_ref[place] = s
+                    part_ref[place, blk(0, size), blk(0, size)] = s
                 continue
             if now == 2 and len(mine) < len(terms):
-                s = s + part_ref[place]
+                s = s + part_ref[place, blk(0, size), blk(0, size)]
             for dj in range(2):
                 for dl in range(2):
                     j, l = 2 * J + dj, 2 * L + dl
@@ -156,7 +157,7 @@
                     else:
                         w = w_ref[min(j, l), pl.ds(off, 1)]
                         y_ref[blk(j), blk(l - 8)] = (
-                            s[dj * B : (dj + 1) * B, dl * B : (dl + 1) * B] * w
+                            s[(dj - lo) * B : (dj - lo + 1) * B, dl * B : (dl + 1) * B] * w
                         ).astype(jnp.bfloat16)
 
 
@@ -165,14 +166,17 @@
         complete = {}
         for L in range(I, I + 5):
             terms = cube_terms(late, I, L)
+            lo, size = (1, 1) if L - I == 4 else (0, 2)
             end = max(stage for _, stage in terms)
             mine = [j for j, stage in terms if (stage == 2) == (now == 2)]
             c = None
             for up in (True, False):
                 for j, n in runs([j for j in mine if (j <= 2 * L) == up]):
-                    left = x_ref[I, :, blk(j - 2 * I + 7, n)]
+                    left = x_ref[I, blk(lo, size), blk(j - 2 * I + 7, n)]
                     right = (
-                        y_ref[blk(j, n), blk(2 * L - 8, 2)] if up else y_ref[blk(2 * L, 2), blk(j - 8, n)]
+                        y_ref[blk(j, n), blk(2 * L - 8, size)]
+                        if up
+                        else y_ref[blk(2 * L, size), blk(j - 8, n)]
                     )
                     t = lax.dot_general(
                         left, right, NN if up else NT, preferred_element_type=jnp.float32
@@ -181,10 +185,10 @@
             place = (I - 4) * 5 + L - I
             if now < end:
                 if c is not None:
-                    part_ref[place] = c
+                    part_ref[place, blk(0, size), blk(0, size)] = c
                 continue
             if now == 2 and end == 2 and len(mine) < len(terms):
-                c = c + part_ref[place]
+                c = c + part_ref[place, blk(0, size), blk(0, size)]
             for di in range(2):
                 i = 2 * I + di
                 offsets = [off for off in (2 * L - i, 2 * L + 1 - i) if 0 <= off <= 7]
@@ -197,7 +201,7 @@
                     dl = l - 2 * L
                     w = w_ref[i, pl.ds(off, 1)]
                     sq = y_ref[blk(i), blk(l - 8)].astype(jnp.float32)
-                    cube = w * c[di * B : (di + 1) * B, dl * B : (dl + 1) * B]
+                    cube = w * c[(di - lo) * B : (di - lo + 1) * B, dl * B : (dl + 1) * B]
                     ready[i - 8, off] = (3.0 * sq - 2.0 * cube).astype(jnp.bfloat16)
                 complete.setdefault((i - 8, end < 2), []).extend(offsets)
         if send is not None:

time: 72.9 us -> 72.7 us (level)
  no operation moved by 1% of the time
where the time goes in v11:
time: 72.7 us; the launch traced here: 72.3 us
  waiting for transfers between devices  39.7 us (55%)
  starting transfers between devices  17 us (23%)
  Pallas kernels  15.2 us (21%)
    ppermute x8, waiting for transfers between devices, swap(): return lax.ppermute(block, 'col', pairs)  30.9 us
    pallas_call x3, Pallas kernels, call(): pl.pallas_call(functools.partial(kernel, z_count), out_shape=outs, in_spe...  13.8 us
    ppermute x8, starting transfers between devices, swap(): return lax.ppermute(block, 'col', pairs)  8.93 us
    ppermute x4, waiting for transfers between devices, hop(): return lax.ppermute(block, ('row', 'col'), pairs)  8.74 us
    ppermute x4, starting transfers between devices, hop(): return lax.ppermute(block, ('row', 'col'), pairs)  8.05 us
  transfers between devices with their start and end apart: 12, of which 7 were waited for; matrix products, arithmetic and copies ran while one was open for 0% of the time, Pallas kernels for 14%

profile of v11, /device:TPU:25, one launch (start us, length us, event | category | flops | bytes accessed | tf_op | source)
XLA Modules:
  0.0 72.3 jit_solution(17501781193464188545)
XLA Ops:
  0.0 1.3 %shard_map.28 = (bf16[1936,128]{1,0:T(8,128)(2,1)S(1)}, bf16[1936,128]{1,0:T(8,128)(2,1)S(1)}) custom-call(s32[4,8]{1,0:T(4,128)} %present_hbm.1, bf16[4,8,128,128]{3,2,1,0:T(8,128)(2,1)} %upper_hbm.1), custom_call_target="tpu_custom_call" | custom-call | tf_op jit(solution)/shard_map/pallas_call | solution.py:364
  1.3 0.2 collective-permute-start
  1.6 1.5 %collective-permute-start.2 = (bf16[1936,128]{1,0:T(8,128)(2,1)S(1)}, bf16[1936,128]{1,0:T(8,128)(2,1)}, u32[]{:S(2)}, u32[]{:S(2)}) collective-permute-start(bf16[1936,128]{1,0:T(8,128)(2,1)S(1)} %get-tuple-element.20.two.own2), channel_id=1, source_target_pairs={{1,2},{2,1},{5,6},{6,5},{9,10},{10,9},{13,14},{14,13},{17,18},{18,... | collective-permute-start | bytes 1486856 | tf_op jit(solution)/shard_map/ppermute | solution.py:397
  3.0 0.1 shard_map.29
  3.1 1.8 %collective-permute-start.1 = (bf16[1936,128]{1,0:T(8,128)(2,1)S(1)}, bf16[1936,128]{1,0:T(8,128)(2,1)}, u32[]{:S(2)}, u32[]{:S(2)}) collective-permute-start(bf16[1936,128]{1,0:T(8,128)(2,1)S(1)} %get-tuple-element.21), channel_id=1, source_target_pairs={{0,1},{2,3},{1,0},{3,2},{4,5},{6,7},{5,4},{7,6},{8,9},{10,11},{9,8... | collective-permute-start | bytes 1486856 | tf_op jit(solution)/shard_map/ppermute | solution.py:397
  4.9 1.5 %collective-permute-start.3 = (bf16[1936,128]{1,0:T(8,128)(2,1)S(1)}, bf16[1936,128]{1,0:T(8,128)(2,1)}, u32[]{:S(2)}, u32[]{:S(2)}) collective-permute-start(bf16[1936,128]{1,0:T(8,128)(2,1)S(1)} %get-tuple-element.22), channel_id=1, source_target_pairs={{1,2},{2,1},{5,6},{6,5},{9,10},{10,9},{13,14},{14,13},{17,18},{18,... | collective-permute-start | bytes 1486856 | tf_op jit(solution)/shard_map/ppermute | solution.py:397
  6.4 7.2 %collective-permute-done.a1 = bf16[1936,128]{1,0:T(8,128)(2,1)S(1)} collective-permute-done((bf16[1936,128]{1,0:T(8,128)(2,1)S(1)}, bf16[1936,128]{1,0:T(8,128)(2,1)S(1)}, u32[]{:S(2)}, u32[]{:S(2)}) %collective-permute-start) | collective-permute-done | bytes 495648 | tf_op jit(solution)/shard_map/ppermute | solution.py:397
  13.6 0.7 collective-permute-start.6
  14.3 0.0 collective-permute-done.2.b1
  14.3 1.3 %collective-permute-start.4 = (bf16[1936,128]{1,0:T(8,128)(2,1)}, bf16[1936,128]{1,0:T(8,128)(2,1)S(1)}, u32[]{:S(2)}, u32[]{:S(2)}) collective-permute-start(bf16[1936,128]{1,0:T(8,128)(2,1)} %collective-permute-done.2.b1), channel_id=1, source_target_pairs={{2,3},{1,0},{6,7},{5,4},{10,11},{9,8},{14,15},{13,12},{18,19},{17,... | collective-permute-start | bytes 1486856 | tf_op jit(solution)/shard_map/ppermute | solution.py:397
  15.6 8.7 %collective-permute-done.1.a2 = bf16[1936,128]{1,0:T(8,128)(2,1)} collective-permute-done((bf16[1936,128]{1,0:T(8,128)(2,1)S(1)}, bf16[1936,128]{1,0:T(8,128)(2,1)}, u32[]{:S(2)}, u32[]{:S(2)}) %collective-permute-start.1) | collective-permute-done | bytes 495648 | tf_op jit(solution)/shard_map/ppermute | solution.py:397
  24.3 0.7 collective-permute-start.7
  25.0 0.0 collective-permute-done.3.b2
  25.0 1.3 %collective-permute-start.5 = (bf16[1936,128]{1,0:T(8,128)(2,1)}, bf16[1936,128]{1,0:T(8,128)(2,1)S(1)}, u32[]{:S(2)}, u32[]{:S(2)}) collective-permute-start(bf16[1936,128]{1,0:T(8,128)(2,1)} %collective-permute-done.3.b2), channel_id=1, source_target_pairs={{2,3},{1,0},{6,7},{5,4},{10,11},{9,8},{14,15},{13,12},{18,19},{17,... | collective-permute-start | bytes 1486856 | tf_op jit(solution)/shard_map/ppermute | solution.py:397
  26.3 0.0 collective-permute-done.6.rb1
  26.3 8.5 %collective-permute-done.4.ra1 = bf16[1936,128]{1,0:T(8,128)(2,1)S(1)} collective-permute-done((bf16[1936,128]{1,0:T(8,128)(2,1)}, bf16[1936,128]{1,0:T(8,128)(2,1)S(1)}, u32[]{:S(2)}, u32[]{:S(2)}) %collective-permute-start.4) | collective-permute-done | bytes 495648 | tf_op jit(solution)/shard_map/ppermute | solution.py:397
  34.8 0.1 broadcast_select_fusion.1
  34.9 2.7 %collective-permute-start.9 = (bf16[1936,128]{1,0:T(8,128)(2,1)S(1)}, bf16[1936,128]{1,0:T(8,128)(2,1)S(1)}, u32[]{:S(2)}, u32[]{:S(2)}) collective-permute-start(bf16[1936,128]{1,0:T(8,128)(2,1)S(1)} %broadcast_select_fusion.1), channel_id=1, source_target_pairs={{0,4},{1,5},{2,14},{3,15},{4,8},{5,9},{6,2},{7,3},{8,12},{9,13},{1... | collective-permute-start | bytes 1486856 | tf_op jit(solution)/shard_map/ppermute | solution.py:405
  37.6 1.3 %collective-permute-start.8 = (bf16[1936,128]{1,0:T(8,128)(2,1)S(1)}, bf16[1936,128]{1,0:T(8,128)(2,1)S(1)}, u32[]{:S(2)}, u32[]{:S(2)}) collective-permute-start(bf16[1936,128]{1,0:T(8,128)(2,1)S(1)} %collective-permute-done.6.rb1), channel_id=1, source_target_pairs={{1,4},{2,15},{5,8},{6,3},{9,12},{10,7},{13,0},{14,11},{17,20},{18,... | collective-permute-start | bytes 1486856 | tf_op jit(solution)/shard_map/ppermute | solution.py:405
  38.9 0.0 collective-permute-done.7.rb2
  38.9 6.5 %collective-permute-done.5.ra2 = bf16[1936,128]{1,0:T(8,128)(2,1)S(1)} collective-permute-done((bf16[1936,128]{1,0:T(8,128)(2,1)}, bf16[1936,128]{1,0:T(8,128)(2,1)S(1)}, u32[]{:S(2)}, u32[]{:S(2)}) %collective-permute-start.5) | collective-permute-done | bytes 495648 | tf_op jit(solution)/shard_map/ppermute | solution.py:397
  45.5 0.1 broadcast_select_fusion
  45.6 2.7 %collective-permute-start.10 = (bf16[1040,128]{1,0:T(8,128)(2,1)S(1)}, bf16[1040,128]{1,0:T(8,128)(2,1)S(1)}, u32[]{:S(2)}, u32[]{:S(2)}) collective-permute-start(bf16[1040,128]{1,0:T(8,128)(2,1)S(1)} %slice_select_fusion), channel_id=1, source_target_pairs={{0,4},{1,5},{2,14},{3,15},{4,8},{5,9},{6,2},{7,3},{8,12},{9,13},{1... | collective-permute-start | bytes 798728 | tf_op jit(solution)/shard_map/ppermute | solution.py:405
  48.3 1.3 %collective-permute-start.11 = (bf16[1936,128]{1,0:T(8,128)(2,1)S(1)}, bf16[1936,128]{1,0:T(8,128)(2,1)S(1)}, u32[]{:S(2)}, u32[]{:S(2)}) collective-permute-start(bf16[1936,128]{1,0:T(8,128)(2,1)S(1)} %collective-permute-done.7.rb2), channel_id=1, source_target_pairs={{1,4},{2,15},{5,8},{6,3},{9,12},{10,7},{13,0},{14,11},{17,20},{18,... | collective-permute-start | bytes 1486856 | tf_op jit(solution)/shard_map/ppermute | solution.py:405
  49.6 5.0 %shard_map.30 = (bf16[10,256,2048]{2,1,0:T(8,128)(2,1)S(1)}, bf16[2560,1536]{1,0:T(8,128)(2,1)S(1)}, f32[20,8,128]{2,1,0:T(8,128)S(1)}) custom-call(bf16[1936,128]{1,0:T(8,128)(2,1)S(1)} %get-tuple-element.19.one.own1, bf16[1936,128]{1,0:T(8,128)(2,1)S(1)} %get-tuple-element.20.two.own2, bf16[1936,128]{1,0:T(8,128)(2,1)S(1)} %collective-permute-done.a1, ...), custom_call_target="tpu_custom_call" | custom-call | flops 1000000000 | bytes 1000000 | tf_op jit(solution)/shard_map/pallas_call | solution.py:332
  54.6 2.0 %collective-permute-done.10.line = bf16[1040,128]{1,0:T(8,128)(2,1)S(1)} collective-permute-done((bf16[1040,128]{1,0:T(8,128)(2,1)S(1)}, bf16[1040,128]{1,0:T(8,128)(2,1)S(1)}, u32[]{:S(2)}, u32[]{:S(2)}) %collective-permute-start.10) | collective-permute-done | bytes 266272 | tf_op jit(solution)/shard_map/ppermute | solution.py:405
  56.6 2.4 %collective-permute-done.8.ends = bf16[1936,128]{1,0:T(8,128)(2,1)S(1)} collective-permute-done((bf16[1936,128]{1,0:T(8,128)(2,1)S(1)}, bf16[1936,128]{1,0:T(8,128)(2,1)S(1)}, u32[]{:S(2)}, u32[]{:S(2)}) %collective-permute-start.8) | collective-permute-done | bytes 495648 | tf_op jit(solution)/shard_map/ppermute | solution.py:405
  59.0 0.0 collective-permute-done.9.cross
  59.0 5.1 %shard_map.31 = (bf16[10,256,2048]{2,1,0:T(8,128)(2,1)S(1)}, bf16[2560,1536]{1,0:T(8,128)(2,1)S(1)}, f32[20,8,128]{2,1,0:T(8,128)S(1)}, f32[15,256,256]{2,1,0:T(...) custom-call(bf16[10,256,2048]{2,1,0:T(8,128)(2,1)S(1)} %get-tuple-el, ...), custom_call_target="tpu_custom_call", output_to_operand_aliasing={{0}: (0, {}), {1}: (1, {}), {2}: (2, {})} | custom-call | flops 6000000000 | bytes 1000000 | tf_op jit(solution)/shard_map/pallas_call | solution.py:332
  64.1 4.4 %collective-permute-done.11.ends = bf16[1936,128]{1,0:T(8,128)(2,1)S(1)} collective-permute-done((bf16[1936,128]{1,0:T(8,128)(2,1)S(1)}, bf16[1936,128]{1,0:T(8,128)(2,1)S(1)}, u32[]{:S(2)}, u32[]{:S(2)}) %collective-permute-start.11) | collective-permute-done | bytes 495648 | tf_op jit(solution)/shard_map/ppermute | solution.py:405
  68.5 3.6 %shard_map.32 = (bf16[10,256,2048]{2,1,0:T(8,128)(2,1)S(1)}, bf16[2560,1536]{1,0:T(8,128)(2,1)S(1)}, f32[20,8,128]{2,1,0:T(8,128)S(1)}, bf16[4,8,128,128]{3,2,1,0:T(8,128)(2,1)}) custom-call(bf16[10,256,2048]{2,1,0:T(8,128)(2,1)S(1)} %get-tuple-element.26.x_in, ...), custom_call_target="tpu_custom_call", output_to_operand_aliasing={{0}: (0, {}), {1}: (1, {}), {2}: (2, {})} | custom-call | flops 6000000000 | bytes 1000000 | tf_op jit(solution)/shard_map/pallas_call | solution.py:332
  (1 shorter events, 0.0 us)
Async XLA Ops:
  1.3 12.2 %collective-permute-start = (bf16[1936,128]{1,0:T(8,128)(2,1)S(1)}, bf16[1936,128]{1,0:T(8,128)(2,1)S(1)}, u32[]{:S(2)}, u32[]{:S(2)}) collective-permute-start(bf16[1936,128]{1,0:T(8,128)(2,1)S(1)} %get-tuple-element.19.one.own1), channel_id=1, source_target_pairs={{0,1},{2,3},{1,0},{3,2},{4,5},{6,7},{5,4},{7,6},{8,9},{10,11},{9,8... | collective-permute-start | bytes 1486856 | tf_op jit(solution)/shard_map/ppermute | solution.py:397
  1.6 12.7 %collective-permute-start.2 = (bf16[1936,128]{1,0:T(8,128)(2,1)S(1)}, bf16[1936,128]{1,0:T(8,128)(2,1)}, u32[]{:S(2)}, u32[]{:S(2)}) collective-permute-start(bf16[1936,128]{1,0:T(8,128)(2,1)S(1)} %get-tuple-element.20.two.own2), channel_id=1, source_target_pairs={{1,2},{2,1},{5,6},{6,5},{9,10},{10,9},{13,14},{14,13},{17,18},{18,... | collective-permute-start | bytes 1486856 | tf_op jit(solution)/shard_map/ppermute | solution.py:397
  3.1 21.2 %collective-permute-start.1 = (bf16[1936,128]{1,0:T(8,128)(2,1)S(1)}, bf16[1936,128]{1,0:T(8,128)(2,1)}, u32[]{:S(2)}, u32[]{:S(2)}) collective-permute-start(bf16[1936,128]{1,0:T(8,128)(2,1)S(1)} %get-tuple-element.21), channel_id=1, source_target_pairs={{0,1},{2,3},{1,0},{3,2},{4,5},{6,7},{5,4},{7,6},{8,9},{10,11},{9,8... | collective-permute-start | bytes 1486856 | tf_op jit(solution)/shard_map/ppermute | solution.py:397
  4.9 20.1 %collective-permute-start.3 = (bf16[1936,128]{1,0:T(8,128)(2,1)S(1)}, bf16[1936,128]{1,0:T(8,128)(2,1)}, u32[]{:S(2)}, u32[]{:S(2)}) collective-permute-start(bf16[1936,128]{1,0:T(8,128)(2,1)S(1)} %get-tuple-element.22), channel_id=1, source_target_pairs={{1,2},{2,1},{5,6},{6,5},{9,10},{10,9},{13,14},{14,13},{17,18},{18,... | collective-permute-start | bytes 1486856 | tf_op jit(solution)/shard_map/ppermute | solution.py:397
  13.6 12.7 %collective-permute-start.6 = (bf16[1936,128]{1,0:T(8,128)(2,1)S(1)}, bf16[1936,128]{1,0:T(8,128)(2,1)S(1)}, u32[]{:S(2)}, u32[]{:S(2)}) collective-permute-start(bf16[1936,128]{1,0:T(8,128)(2,1)S(1)} %collective-permute-done.a1), channel_id=1, source_target_pairs={{1,2},{2,1},{5,6},{6,5},{9,10},{10,9},{13,14},{14,13},{17,18},{18,... | collective-permute-start | bytes 1486856 | tf_op jit(solution)/shard_map/ppermute | solution.py:397
  14.3 20.5 %collective-permute-start.4 = (bf16[1936,128]{1,0:T(8,128)(2,1)}, bf16[1936,128]{1,0:T(8,128)(2,1)S(1)}, u32[]{:S(2)}, u32[]{:S(2)}) collective-permute-start(bf16[1936,128]{1,0:T(8,128)(2,1)} %collective-permute-done.2.b1), channel_id=1, source_target_pairs={{2,3},{1,0},{6,7},{5,4},{10,11},{9,8},{14,15},{13,12},{18,19},{17,... | collective-permute-start | bytes 1486856 | tf_op jit(solution)/shard_map/ppermute | solution.py:397
  24.3 14.6 %collective-permute-start.7 = (bf16[1936,128]{1,0:T(8,128)(2,1)}, bf16[1936,128]{1,0:T(8,128)(2,1)S(1)}, u32[]{:S(2)}, u32[]{:S(2)}) collective-permute-start(bf16[1936,128]{1,0:T(8,128)(2,1)} %collective-permute-done.1.a2), channel_id=1, source_target_pairs={{1,2},{2,1},{5,6},{6,5},{9,10},{10,9},{13,14},{14,13},{17,18},{18,... | collective-permute-start | bytes 1486856 | tf_op jit(solution)/shard_map/ppermute | solution.py:397
  25.0 20.4 %collective-permute-start.5 = (bf16[1936,128]{1,0:T(8,128)(2,1)}, bf16[1936,128]{1,0:T(8,128)(2,1)S(1)}, u32[]{:S(2)}, u32[]{:S(2)}) collective-permute-start(bf16[1936,128]{1,0:T(8,128)(2,1)} %collective-permute-done.3.b2), channel_id=1, source_target_pairs={{2,3},{1,0},{6,7},{5,4},{10,11},{9,8},{14,15},{13,12},{18,19},{17,... | collective-permute-start | bytes 1486856 | tf_op jit(solution)/shard_map/ppermute | solution.py:397
  34.9 24.1 %collective-permute-start.9 = (bf16[1936,128]{1,0:T(8,128)(2,1)S(1)}, bf16[1936,128]{1,0:T(8,128)(2,1)S(1)}, u32[]{:S(2)}, u32[]{:S(2)}) collective-permute-start(bf16[1936,128]{1,0:T(8,128)(2,1)S(1)} %broadcast_select_fusion.1), channel_id=1, source_target_pairs={{0,4},{1,5},{2,14},{3,15},{4,8},{5,9},{6,2},{7,3},{8,12},{9,13},{1... | collective-permute-start | bytes 1486856 | tf_op jit(solution)/shard_map/ppermute | solution.py:405
  37.6 21.4 %collective-permute-start.8 = (bf16[1936,128]{1,0:T(8,128)(2,1)S(1)}, bf16[1936,128]{1,0:T(8,128)(2,1)S(1)}, u32[]{:S(2)}, u32[]{:S(2)}) collective-permute-start(bf16[1936,128]{1,0:T(8,128)(2,1)S(1)} %collective-permute-done.6.rb1), channel_id=1, source_target_pairs={{1,4},{2,15},{5,8},{6,3},{9,12},{10,7},{13,0},{14,11},{17,20},{18,... | collective-permute-start | bytes 1486856 | tf_op jit(solution)/shard_map/ppermute | solution.py:405
  45.6 11.1 %collective-permute-start.10 = (bf16[1040,128]{1,0:T(8,128)(2,1)S(1)}, bf16[1040,128]{1,0:T(8,128)(2,1)S(1)}, u32[]{:S(2)}, u32[]{:S(2)}) collective-permute-start(bf16[1040,128]{1,0:T(8,128)(2,1)S(1)} %slice_select_fusion), channel_id=1, source_target_pairs={{0,4},{1,5},{2,14},{3,15},{4,8},{5,9},{6,2},{7,3},{8,12},{9,13},{1... | collective-permute-start | bytes 798728 | tf_op jit(solution)/shard_map/ppermute | solution.py:405
  48.3 20.2 %collective-permute-start.11 = (bf16[1936,128]{1,0:T(8,128)(2,1)S(1)}, bf16[1936,128]{1,0:T(8,128)(2,1)S(1)}, u32[]{:S(2)}, u32[]{:S(2)}) collective-permute-start(bf16[1936,128]{1,0:T(8,128)(2,1)S(1)} %collective-permute-done.7.rb2), channel_id=1, source_target_pairs={{1,4},{2,15},{5,8},{6,3},{9,12},{10,7},{13,0},{14,11},{17,20},{18,... | collective-permute-start | bytes 1486856 | tf_op jit(solution)/shard_map/ppermute | solution.py:405

commit v12 on v11

--- a/solution.py
+++ b/solution.py
@@ -161,6 +161,11 @@
                         ).astype(jnp.bfloat16)
 
 
+def before(late, i):
+    pairs = [(L, max(stage for _, stage in cube_terms(late, i // 2, L))) for L in range(i // 2, i // 2 + 5)]
+    return [l - i for L, end in pairs if end < 2 for l in (2 * L, 2 * L + 1) if 0 <= l - i <= 7]
+
+
 def purify(late, now, x_ref, y_ref, w_ref, part_ref, ready, send=None):
     for I in (4, 5):
         complete = {}
@@ -192,21 +197,20 @@
             for di in range(2):
                 i = 2 * I + di
                 offsets = [off for off in (2 * L - i, 2 * L + 1 - i) if 0 <= off <= 7]
-                if not offsets:
+                if not offsets or (now == 2 and end < 2):
                     continue
                 for off in offsets:
-                    if now == 2 and end < 2:
-                        break
                     l = i + off
                     dl = l - 2 * L
                     w = w_ref[i, pl.ds(off, 1)]
                     sq = y_ref[blk(i), blk(l - 8)].astype(jnp.float32)
                     cube = w * c[(di - lo) * B : (di - lo + 1) * B, dl * B : (dl + 1) * B]
                     ready[i - 8, off] = (3.0 * sq - 2.0 * cube).astype(jnp.bfloat16)
-                complete.setdefault((i - 8, end < 2), []).extend(offsets)
-        if send is not None:
-            for (i, early), offsets in complete.items():
-                send(i, int(early), min(offsets), len(offsets))
+                complete.setdefault(i - 8, []).extend(offsets)
+            if send is not None and L in (I + 2, I + 4):
+                for i, offsets in complete.items():
+                    send(i, int(L > I + 2), min(offsets), len(offsets))
+                complete = {}
 
 
 def take_all(x_ref, w_ref, pieces):
@@ -298,14 +302,18 @@
     def work(late):
         copies = []
 
-        def send(i, early, offset, count):
+        def send(i, turn, offset, count):
             part = pl.ds(offset, count)
             copy = pltpu.make_async_copy(
-                (done if early else ready).at[i, part], out.at[i, part], sems.at[i, early]
+                (done if turn == 2 else ready).at[i, part], out.at[i, part], sems.at[i, turn]
             )
             copy.start()
             copies.append(copy)
 
+        for i in range(4):
+            offsets = before(late, i + 8)
+            if offsets:
+                send(i, 2, min(offsets), len(offsets))
         square(late, 2, x_ref, y_ref, w_ref, sums)
         purify(late, 2, x_ref, y_ref, w_ref, cubes, ready, send)
         for copy in copies:
@@ -348,7 +356,7 @@
     got = call(stage_1, z_count, outs, [VMEM] * 6, aliases, [], 6 * 10**9, *kept, *rows_1)
     outs = KEPT + [jax.ShapeDtypeStruct((4, 8, B, B), jnp.bfloat16)]
     specs = [VMEM] * 3 + [pl.BlockSpec(memory_space=pl.ANY)]
-    scratch = [pltpu.VMEM((4, 8, B, B), jnp.bfloat16), pltpu.SemaphoreType.DMA((4, 2))]
+    scratch = [pltpu.VMEM((4, 8, B, B), jnp.bfloat16), pltpu.SemaphoreType.DMA((4, 3))]
     return call(stage_2, z_count, outs, specs, aliases, scratch, 6 * 10**9, *got, *rows_2)[3]
 
 

time: 72.7 us -> 72.6 us (level)
  no operation moved by 1% of the time
where the time goes in v12:
time: 72.6 us; the launch traced here: 72.2 us
  waiting for transfers between devices  39.7 us (55%)
  starting transfers between devices  17 us (23%)
  Pallas kernels  15.1 us (21%)
    ppermute x8, waiting for transfers between devices, swap(): return lax.ppermute(block, 'col', pairs)  30.9 us
    pallas_call x3, Pallas kernels, call(): pl.pallas_call(functools.partial(kernel, z_count), out_shape=outs, in_spe...  13.7 us
    ppermute x8, starting transfers between devices, swap(): return lax.ppermute(block, 'col', pairs)  8.93 us
    ppermute x4, waiting for transfers between devices, hop(): return lax.ppermute(block, ('row', 'col'), pairs)  8.74 us
    ppermute x4, starting transfers between devices, hop(): return lax.ppermute(block, ('row', 'col'), pairs)  8.05 us
  transfers between devices with their start and end apart: 12, of which 7 were waited for; matrix products, arithmetic and copies ran while one was open for 0% of the time, Pallas kernels for 14%

profile of v12, /device:TPU:25, one launch (start us, length us, event | category | flops | bytes accessed | tf_op | source)
XLA Modules:
  0.0 72.2 jit_solution(5070373704302819049)
XLA Ops:
  0.0 1.3 %shard_map.28 = (bf16[1936,128]{1,0:T(8,128)(2,1)S(1)}, bf16[1936,128]{1,0:T(8,128)(2,1)S(1)}) custom-call(s32[4,8]{1,0:T(4,128)} %present_hbm.1, bf16[4,8,128,128]{3,2,1,0:T(8,128)(2,1)} %upper_hbm.1), custom_call_target="tpu_custom_call" | custom-call | tf_op jit(solution)/shard_map/pallas_call | solution.py:372
  1.3 0.2 collective-permute-start
  1.6 1.5 %collective-permute-start.2 = (bf16[1936,128]{1,0:T(8,128)(2,1)S(1)}, bf16[1936,128]{1,0:T(8,128)(2,1)}, u32[]{:S(2)}, u32[]{:S(2)}) collective-permute-start(bf16[1936,128]{1,0:T(8,128)(2,1)S(1)} %get-tuple-element.20.two.own2), channel_id=1, source_target_pairs={{1,2},{2,1},{5,6},{6,5},{9,10},{10,9},{13,14},{14,13},{17,18},{18,... | collective-permute-start | bytes 1486856 | tf_op jit(solution)/shard_map/ppermute | solution.py:405
  3.0 0.1 shard_map.29
  3.1 1.8 %collective-permute-start.1 = (bf16[1936,128]{1,0:T(8,128)(2,1)S(1)}, bf16[1936,128]{1,0:T(8,128)(2,1)}, u32[]{:S(2)}, u32[]{:S(2)}) collective-permute-start(bf16[1936,128]{1,0:T(8,128)(2,1)S(1)} %get-tuple-element.21), channel_id=1, source_target_pairs={{0,1},{2,3},{1,0},{3,2},{4,5},{6,7},{5,4},{7,6},{8,9},{10,11},{9,8... | collective-permute-start | bytes 1486856 | tf_op jit(solution)/shard_map/ppermute | solution.py:405
  4.9 1.5 %collective-permute-start.3 = (bf16[1936,128]{1,0:T(8,128)(2,1)S(1)}, bf16[1936,128]{1,0:T(8,128)(2,1)}, u32[]{:S(2)}, u32[]{:S(2)}) collective-permute-start(bf16[1936,128]{1,0:T(8,128)(2,1)S(1)} %get-tuple-element.22), channel_id=1, source_target_pairs={{1,2},{2,1},{5,6},{6,5},{9,10},{10,9},{13,14},{14,13},{17,18},{18,... | collective-permute-start | bytes 1486856 | tf_op jit(solution)/shard_map/ppermute | solution.py:405
  6.4 7.2 %collective-permute-done.a1 = bf16[1936,128]{1,0:T(8,128)(2,1)S(1)} collective-permute-done((bf16[1936,128]{1,0:T(8,128)(2,1)S(1)}, bf16[1936,128]{1,0:T(8,128)(2,1)S(1)}, u32[]{:S(2)}, u32[]{:S(2)}) %collective-permute-start) | collective-permute-done | bytes 495648 | tf_op jit(solution)/shard_map/ppermute | solution.py:405
  13.6 0.7 collective-permute-start.6
  14.3 0.0 collective-permute-done.2.b1
  14.3 1.3 %collective-permute-start.4 = (bf16[1936,128]{1,0:T(8,128)(2,1)}, bf16[1936,128]{1,0:T(8,128)(2,1)S(1)}, u32[]{:S(2)}, u32[]{:S(2)}) collective-permute-start(bf16[1936,128]{1,0:T(8,128)(2,1)} %collective-permute-done.2.b1), channel_id=1, source_target_pairs={{2,3},{1,0},{6,7},{5,4},{10,11},{9,8},{14,15},{13,12},{18,19},{17,... | collective-permute-start | bytes 1486856 | tf_op jit(solution)/shard_map/ppermute | solution.py:405
  15.6 8.7 %collective-permute-done.1.a2 = bf16[1936,128]{1,0:T(8,128)(2,1)} collective-permute-done((bf16[1936,128]{1,0:T(8,128)(2,1)S(1)}, bf16[1936,128]{1,0:T(8,128)(2,1)}, u32[]{:S(2)}, u32[]{:S(2)}) %collective-permute-start.1) | collective-permute-done | bytes 495648 | tf_op jit(solution)/shard_map/ppermute | solution.py:405
  24.3 0.7 collective-permute-start.7
  25.0 0.0 collective-permute-done.3.b2
  25.0 1.3 %collective-permute-start.5 = (bf16[1936,128]{1,0:T(8,128)(2,1)}, bf16[1936,128]{1,0:T(8,128)(2,1)S(1)}, u32[]{:S(2)}, u32[]{:S(2)}) collective-permute-start(bf16[1936,128]{1,0:T(8,128)(2,1)} %collective-permute-done.3.b2), channel_id=1, source_target_pairs={{2,3},{1,0},{6,7},{5,4},{10,11},{9,8},{14,15},{13,12},{18,19},{17,... | collective-permute-start | bytes 1486856 | tf_op jit(solution)/shard_map/ppermute | solution.py:405
  26.3 0.0 collective-permute-done.6.rb1
  26.3 8.5 %collective-permute-done.4.ra1 = bf16[1936,128]{1,0:T(8,128)(2,1)S(1)} collective-permute-done((bf16[1936,128]{1,0:T(8,128)(2,1)}, bf16[1936,128]{1,0:T(8,128)(2,1)S(1)}, u32[]{:S(2)}, u32[]{:S(2)}) %collective-permute-start.4) | collective-permute-done | bytes 495648 | tf_op jit(solution)/shard_map/ppermute | solution.py:405
  34.8 0.1 broadcast_select_fusion.1
  34.9 2.7 %collective-permute-start.9 = (bf16[1936,128]{1,0:T(8,128)(2,1)S(1)}, bf16[1936,128]{1,0:T(8,128)(2,1)S(1)}, u32[]{:S(2)}, u32[]{:S(2)}) collective-permute-start(bf16[1936,128]{1,0:T(8,128)(2,1)S(1)} %broadcast_select_fusion.1), channel_id=1, source_target_pairs={{0,4},{1,5},{2,14},{3,15},{4,8},{5,9},{6,2},{7,3},{8,12},{9,13},{1... | collective-permute-start | bytes 1486856 | tf_op jit(solution)/shard_map/ppermute | solution.py:413
  37.6 1.3 %collective-permute-start.8 = (bf16[1936,128]{1,0:T(8,128)(2,1)S(1)}, bf16[1936,128]{1,0:T(8,128)(2,1)S(1)}, u32[]{:S(2)}, u32[]{:S(2)}) collective-permute-start(bf16[1936,128]{1,0:T(8,128)(2,1)S(1)} %collective-permute-done.6.rb1), channel_id=1, source_target_pairs={{1,4},{2,15},{5,8},{6,3},{9,12},{10,7},{13,0},{14,11},{17,20},{18,... | collective-permute-start | bytes 1486856 | tf_op jit(solution)/shard_map/ppermute | solution.py:413
  38.9 0.0 collective-permute-done.7.rb2
  38.9 6.5 %collective-permute-done.5.ra2 = bf16[1936,128]{1,0:T(8,128)(2,1)S(1)} collective-permute-done((bf16[1936,128]{1,0:T(8,128)(2,1)}, bf16[1936,128]{1,0:T(8,128)(2,1)S(1)}, u32[]{:S(2)}, u32[]{:S(2)}) %collective-permute-start.5) | collective-permute-done | bytes 495648 | tf_op jit(solution)/shard_map/ppermute | solution.py:405
  45.5 0.1 broadcast_select_fusion
  45.6 2.7 %collective-permute-start.10 = (bf16[1040,128]{1,0:T(8,128)(2,1)S(1)}, bf16[1040,128]{1,0:T(8,128)(2,1)S(1)}, u32[]{:S(2)}, u32[]{:S(2)}) collective-permute-start(bf16[1040,128]{1,0:T(8,128)(2,1)S(1)} %slice_select_fusion), channel_id=1, source_target_pairs={{0,4},{1,5},{2,14},{3,15},{4,8},{5,9},{6,2},{7,3},{8,12},{9,13},{1... | collective-permute-start | bytes 798728 | tf_op jit(solution)/shard_map/ppermute | solution.py:413
  48.3 1.3 %collective-permute-start.11 = (bf16[1936,128]{1,0:T(8,128)(2,1)S(1)}, bf16[1936,128]{1,0:T(8,128)(2,1)S(1)}, u32[]{:S(2)}, u32[]{:S(2)}) collective-permute-start(bf16[1936,128]{1,0:T(8,128)(2,1)S(1)} %collective-permute-done.7.rb2), channel_id=1, source_target_pairs={{1,4},{2,15},{5,8},{6,3},{9,12},{10,7},{13,0},{14,11},{17,20},{18,... | collective-permute-start | bytes 1486856 | tf_op jit(solution)/shard_map/ppermute | solution.py:413
  49.6 5.0 %shard_map.30 = (bf16[10,256,2048]{2,1,0:T(8,128)(2,1)S(1)}, bf16[2560,1536]{1,0:T(8,128)(2,1)S(1)}, f32[20,8,128]{2,1,0:T(8,128)S(1)}) custom-call(bf16[1936,128]{1,0:T(8,128)(2,1)S(1)} %get-tuple-element.19.one.own1, bf16[1936,128]{1,0:T(8,128)(2,1)S(1)} %get-tuple-element.20.two.own2, bf16[1936,128]{1,0:T(8,128)(2,1)S(1)} %collective-permute-done.a1, ...), custom_call_target="tpu_custom_call" | custom-call | flops 1000000000 | bytes 1000000 | tf_op jit(solution)/shard_map/pallas_call | solution.py:340
  54.6 2.0 %collective-permute-done.10.line = bf16[1040,128]{1,0:T(8,128)(2,1)S(1)} collective-permute-done((bf16[1040,128]{1,0:T(8,128)(2,1)S(1)}, bf16[1040,128]{1,0:T(8,128)(2,1)S(1)}, u32[]{:S(2)}, u32[]{:S(2)}) %collective-permute-start.10) | collective-permute-done | bytes 266272 | tf_op jit(solution)/shard_map/ppermute | solution.py:413
  56.6 2.4 %collective-permute-done.8.ends = bf16[1936,128]{1,0:T(8,128)(2,1)S(1)} collective-permute-done((bf16[1936,128]{1,0:T(8,128)(2,1)S(1)}, bf16[1936,128]{1,0:T(8,128)(2,1)S(1)}, u32[]{:S(2)}, u32[]{:S(2)}) %collective-permute-start.8) | collective-permute-done | bytes 495648 | tf_op jit(solution)/shard_map/ppermute | solution.py:413
  59.0 0.0 collective-permute-done.9.cross
  59.0 5.1 %shard_map.31 = (bf16[10,256,2048]{2,1,0:T(8,128)(2,1)S(1)}, bf16[2560,1536]{1,0:T(8,128)(2,1)S(1)}, f32[20,8,128]{2,1,0:T(8,128)S(1)}, f32[15,256,256]{2,1,0:T(...) custom-call(bf16[10,256,2048]{2,1,0:T(8,128)(2,1)S(1)} %get-tuple-el, ...), custom_call_target="tpu_custom_call", output_to_operand_aliasing={{0}: (0, {}), {1}: (1, {}), {2}: (2, {})} | custom-call | flops 6000000000 | bytes 1000000 | tf_op jit(solution)/shard_map/pallas_call | solution.py:340
  64.1 4.4 %collective-permute-done.11.ends = bf16[1936,128]{1,0:T(8,128)(2,1)S(1)} collective-permute-done((bf16[1936,128]{1,0:T(8,128)(2,1)S(1)}, bf16[1936,128]{1,0:T(8,128)(2,1)S(1)}, u32[]{:S(2)}, u32[]{:S(2)}) %collective-permute-start.11) | collective-permute-done | bytes 495648 | tf_op jit(solution)/shard_map/ppermute | solution.py:413
  68.5 3.6 %shard_map.32 = (bf16[10,256,2048]{2,1,0:T(8,128)(2,1)S(1)}, bf16[2560,1536]{1,0:T(8,128)(2,1)S(1)}, f32[20,8,128]{2,1,0:T(8,128)S(1)}, bf16[4,8,128,128]{3,2,1,0:T(8,128)(2,1)}) custom-call(bf16[10,256,2048]{2,1,0:T(8,128)(2,1)S(1)} %get-tuple-element.26.x_in, ...), custom_call_target="tpu_custom_call", output_to_operand_aliasing={{0}: (0, {}), {1}: (1, {}), {2}: (2, {})} | custom-call | flops 6000000000 | bytes 1000000 | tf_op jit(solution)/shard_map/pallas_call | solution.py:340
  (1 shorter events, 0.0 us)
Async XLA Ops:
  1.3 12.2 %collective-permute-start = (bf16[1936,128]{1,0:T(8,128)(2,1)S(1)}, bf16[1936,128]{1,0:T(8,128)(2,1)S(1)}, u32[]{:S(2)}, u32[]{:S(2)}) collective-permute-start(bf16[1936,128]{1,0:T(8,128)(2,1)S(1)} %get-tuple-element.19.one.own1), channel_id=1, source_target_pairs={{0,1},{2,3},{1,0},{3,2},{4,5},{6,7},{5,4},{7,6},{8,9},{10,11},{9,8... | collective-permute-start | bytes 1486856 | tf_op jit(solution)/shard_map/ppermute | solution.py:405
  1.6 12.7 %collective-permute-start.2 = (bf16[1936,128]{1,0:T(8,128)(2,1)S(1)}, bf16[1936,128]{1,0:T(8,128)(2,1)}, u32[]{:S(2)}, u32[]{:S(2)}) collective-permute-start(bf16[1936,128]{1,0:T(8,128)(2,1)S(1)} %get-tuple-element.20.two.own2), channel_id=1, source_target_pairs={{1,2},{2,1},{5,6},{6,5},{9,10},{10,9},{13,14},{14,13},{17,18},{18,... | collective-permute-start | bytes 1486856 | tf_op jit(solution)/shard_map/ppermute | solution.py:405
  3.1 21.2 %collective-permute-start.1 = (bf16[1936,128]{1,0:T(8,128)(2,1)S(1)}, bf16[1936,128]{1,0:T(8,128)(2,1)}, u32[]{:S(2)}, u32[]{:S(2)}) collective-permute-start(bf16[1936,128]{1,0:T(8,128)(2,1)S(1)} %get-tuple-element.21), channel_id=1, source_target_pairs={{0,1},{2,3},{1,0},{3,2},{4,5},{6,7},{5,4},{7,6},{8,9},{10,11},{9,8... | collective-permute-start | bytes 1486856 | tf_op jit(solution)/shard_map/ppermute | solution.py:405
  4.9 20.1 %collective-permute-start.3 = (bf16[1936,128]{1,0:T(8,128)(2,1)S(1)}, bf16[1936,128]{1,0:T(8,128)(2,1)}, u32[]{:S(2)}, u32[]{:S(2)}) collective-permute-start(bf16[1936,128]{1,0:T(8,128)(2,1)S(1)} %get-tuple-element.22), channel_id=1, source_target_pairs={{1,2},{2,1},{5,6},{6,5},{9,10},{10,9},{13,14},{14,13},{17,18},{18,... | collective-permute-start | bytes 1486856 | tf_op jit(solution)/shard_map/ppermute | solution.py:405
  13.6 12.7 %collective-permute-start.6 = (bf16[1936,128]{1,0:T(8,128)(2,1)S(1)}, bf16[1936,128]{1,0:T(8,128)(2,1)S(1)}, u32[]{:S(2)}, u32[]{:S(2)}) collective-permute-start(bf16[1936,128]{1,0:T(8,128)(2,1)S(1)} %collective-permute-done.a1), channel_id=1, source_target_pairs={{1,2},{2,1},{5,6},{6,5},{9,10},{10,9},{13,14},{14,13},{17,18},{18,... | collective-permute-start | bytes 1486856 | tf_op jit(solution)/shard_map/ppermute | solution.py:405
  14.3 20.5 %collective-permute-start.4 = (bf16[1936,128]{1,0:T(8,128)(2,1)}, bf16[1936,128]{1,0:T(8,128)(2,1)S(1)}, u32[]{:S(2)}, u32[]{:S(2)}) collective-permute-start(bf16[1936,128]{1,0:T(8,128)(2,1)} %collective-permute-done.2.b1), channel_id=1, source_target_pairs={{2,3},{1,0},{6,7},{5,4},{10,11},{9,8},{14,15},{13,12},{18,19},{17,... | collective-permute-start | bytes 1486856 | tf_op jit(solution)/shard_map/ppermute | solution.py:405
  24.3 14.6 %collective-permute-start.7 = (bf16[1936,128]{1,0:T(8,128)(2,1)}, bf16[1936,128]{1,0:T(8,128)(2,1)S(1)}, u32[]{:S(2)}, u32[]{:S(2)}) collective-permute-start(bf16[1936,128]{1,0:T(8,128)(2,1)} %collective-permute-done.1.a2), channel_id=1, source_target_pairs={{1,2},{2,1},{5,6},{6,5},{9,10},{10,9},{13,14},{14,13},{17,18},{18,... | collective-permute-start | bytes 1486856 | tf_op jit(solution)/shard_map/ppermute | solution.py:405
  25.0 20.4 %collective-permute-start.5 = (bf16[1936,128]{1,0:T(8,128)(2,1)}, bf16[1936,128]{1,0:T(8,128)(2,1)S(1)}, u32[]{:S(2)}, u32[]{:S(2)}) collective-permute-start(bf16[1936,128]{1,0:T(8,128)(2,1)} %collective-permute-done.3.b2), channel_id=1, source_target_pairs={{2,3},{1,0},{6,7},{5,4},{10,11},{9,8},{14,15},{13,12},{18,19},{17,... | collective-permute-start | bytes 1486856 | tf_op jit(solution)/shard_map/ppermute | solution.py:405
  34.9 24.1 %collective-permute-start.9 = (bf16[1936,128]{1,0:T(8,128)(2,1)S(1)}, bf16[1936,128]{1,0:T(8,128)(2,1)S(1)}, u32[]{:S(2)}, u32[]{:S(2)}) collective-permute-start(bf16[1936,128]{1,0:T(8,128)(2,1)S(1)} %broadcast_select_fusion.1), channel_id=1, source_target_pairs={{0,4},{1,5},{2,14},{3,15},{4,8},{5,9},{6,2},{7,3},{8,12},{9,13},{1... | collective-permute-start | bytes 1486856 | tf_op jit(solution)/shard_map/ppermute | solution.py:413
  37.6 21.4 %collective-permute-start.8 = (bf16[1936,128]{1,0:T(8,128)(2,1)S(1)}, bf16[1936,128]{1,0:T(8,128)(2,1)S(1)}, u32[]{:S(2)}, u32[]{:S(2)}) collective-permute-start(bf16[1936,128]{1,0:T(8,128)(2,1)S(1)} %collective-permute-done.6.rb1), channel_id=1, source_target_pairs={{1,4},{2,15},{5,8},{6,3},{9,12},{10,7},{13,0},{14,11},{17,20},{18,... | collective-permute-start | bytes 1486856 | tf_op jit(solution)/shard_map/ppermute | solution.py:413
  45.6 11.1 %collective-permute-start.10 = (bf16[1040,128]{1,0:T(8,128)(2,1)S(1)}, bf16[1040,128]{1,0:T(8,128)(2,1)S(1)}, u32[]{:S(2)}, u32[]{:S(2)}) collective-permute-start(bf16[1040,128]{1,0:T(8,128)(2,1)S(1)} %slice_select_fusion), channel_id=1, source_target_pairs={{0,4},{1,5},{2,14},{3,15},{4,8},{5,9},{6,2},{7,3},{8,12},{9,13},{1... | collective-permute-start | bytes 798728 | tf_op jit(solution)/shard_map/ppermute | solution.py:413
  48.3 20.2 %collective-permute-start.11 = (bf16[1936,128]{1,0:T(8,128)(2,1)S(1)}, bf16[1936,128]{1,0:T(8,128)(2,1)S(1)}, u32[]{:S(2)}, u32[]{:S(2)}) collective-permute-start(bf16[1936,128]{1,0:T(8,128)(2,1)S(1)} %collective-permute-done.7.rb2), channel_id=1, source_target_pairs={{1,4},{2,15},{5,8},{6,3},{9,12},{10,7},{13,0},{14,11},{17,20},{18,... | collective-permute-start | bytes 1486856 | tf_op jit(solution)/shard_map/ppermute | solution.py:413
